TPU v7x, 256 devices: a whole 4x4x8 slice. The times are simulated.
256 devices in a mesh: queue: 16 (over x_lo, z), seq: 16 (over y, x_hi, core).
Axes of the slice: x: 4 (x_hi: 2, x_lo: 2; x = x_hi * 2 + x_lo), y: 4, z: 8, core: 2. Of those that a mesh axis runs over, the one named last changes fastest.
Arguments:
- latents: float32 [32, 1024, 16], P('queue', 'seq'), may hold values from -6 to 6
- levels: int32 [32], P('queue'), may hold values from 0 to 31, as said below
- advance: int32 [16], P('queue'), may hold values from 1 to 2, as said below
- fresh_noise: float32 [1024, 16], P('seq'), may hold values from -6 to 6
- level_mod: float32 [32, 8, 1152], P(None, None, 'seq'), may hold values from -4 to 4
- embed_w: float32 [16, 1152], replicated, may hold values from -1.5 to 1.5
- spatial_qkv: bfloat16 [1152, 3, 1152], replicated
- spatial_out: bfloat16 [1152, 1152], P(None, 'seq'), may hold values from -0.1875 to 0.1875
- temporal_qkv: bfloat16 [1152, 3, 1152], P(None, None, 'seq')
- temporal_out: bfloat16 [1152, 1152], P(None, 'seq'), may hold values from -0.1875 to 0.1875
- final_w: bfloat16 [1152, 16], replicated, may hold values from -0.1875 to 0.1875
Outputs:
- velocity: float32 [32, 1024, 16], P('queue', 'seq')
- queue_next: float32 [32, 1024, 16], P('queue', 'seq')
Inputs may be any that keep to these rules, and one draw needn't show every extreme that they name: `levels`: the level of slot f lies within 2 of f; the first slot has level 0 and the last level 31. `advance`: some window other than the last takes all 2 frames; the last window's entry is not used.
All inputs are finite; a program needn't handle non-finite values.
Results may differ from a plain program's by a relative error of at most 0.02.
Values may be sent and summed in bfloat16 or wider, within the bound.
No kernel may reach another device: no remote copies, remote signals or barrier semaphores. Data moves between devices by JAX's collectives and lax.ppermute only.
A program may use at most 128 MiB of HBM per device.

v0:
```python
import math

import jax
import jax.numpy as jnp
from jax import lax
from jax.sharding import PartitionSpec as P

HEADS = 16


def from_behind(array, axis, by):
    size = lax.axis_size(axis)
    pairs = [(i, i + by) for i in range(size) if 0 <= i + by < size]
    return lax.ppermute(array, axis, pairs)


def layer_norm(hidden):
    mean_value = jnp.mean(hidden, axis=-1, keepdims=True)
    centered = hidden - mean_value
    variance = jnp.mean(centered * centered, axis=-1, keepdims=True)
    return centered * lax.rsqrt(variance + 1e-06)


def modulate(hidden, modulation, index):
    return layer_norm(hidden) * (1.0 + modulation[:, :, index + 1]) + modulation[:, :, index]


def spatial_frames(head_block):
    scale_value = 1.0 / math.sqrt(head_block.shape[-1])

    def one_frame(frame_block):
        query_part = frame_block[:, 0]
        key_part = frame_block[:, 1]
        value_part = frame_block[:, 2]
        scores = (
            jnp.einsum("qhe,khe->hqk", query_part, key_part, preferred_element_type=jnp.float32)
            * scale_value
        )
        attn_probs = jax.nn.softmax(scores, axis=-1).astype(jnp.bfloat16)
        return jnp.einsum(
            "hqk,khe->qhe", attn_probs, value_part, preferred_element_type=jnp.float32
        ).astype(jnp.bfloat16)

    return lax.map(one_frame, head_block)


def temporal_attend(proj_block, advance, is_last):
    frames_dev = proj_block.shape[0]
    head_dim = proj_block.shape[-1]
    ahead = from_behind(proj_block[:, :, 1:], "queue", -1)
    limit = jnp.where(is_last, 0, advance[0])
    query_part = proj_block[:, :, 0]
    key_part = jnp.concatenate([proj_block[:, :, 1], ahead[:, :, 0]], axis=0)
    value_part = jnp.concatenate([proj_block[:, :, 2], ahead[:, :, 1]], axis=0)
    scores = jnp.einsum(
        "ishe,jshe->shij", query_part, key_part, preferred_element_type=jnp.float32
    ) * (1.0 / math.sqrt(head_dim))
    column = jnp.arange(2 * frames_dev, dtype=jnp.int32)
    keep = (column < frames_dev) | (column - frames_dev < limit)
    scores = jnp.where(keep, scores, -jnp.inf)
    attn_probs = jax.nn.softmax(scores, axis=-1).astype(jnp.bfloat16)
    mixed = jnp.einsum(
        "shij,jshe->ishe", attn_probs, value_part, preferred_element_type=jnp.float32
    )
    return mixed.astype(jnp.bfloat16)


def shards(
    latents,
    levels,
    advance,
    fresh_noise,
    level_mod,
    embed_w,
    spatial_qkv,
    spatial_out,
    temporal_qkv,
    temporal_out,
    final_w,
):
    frames_dev, tokens_dev, channels = latents.shape
    frames = level_mod.shape[0]
    model_width = embed_w.shape[1]
    head_dim = model_width // HEADS
    local_width = level_mod.shape[2]
    mod_table = level_mod.reshape(frames, 8 * local_width)
    choose = (levels[:, None] == jnp.arange(frames, dtype=jnp.int32)[None, :]).astype(jnp.float32)
    own_rows = jnp.dot(choose, mod_table, precision=lax.Precision.HIGHEST).reshape(
        frames_dev, 8, local_width
    )
    modulation = lax.all_gather(own_rows, "seq", axis=2, tiled=True).reshape(
        frames_dev, 1, 8, model_width
    )
    embedded = jnp.einsum("fsc,cd->fsd", latents, embed_w, precision=lax.Precision.HIGHEST)
    is_last = lax.axis_index("queue") == lax.axis_size("queue") - 1
    spatial_in = modulate(embedded, modulation, 0).astype(jnp.bfloat16)
    projected = jnp.einsum(
        "fsd,dtk->fstk", spatial_in, spatial_qkv, preferred_element_type=jnp.float32
    )
    token_layout = projected.astype(jnp.bfloat16).reshape(
        frames_dev, tokens_dev, 3, HEADS, head_dim
    )
    attended = spatial_frames(
        lax.all_to_all(token_layout, "seq", split_axis=3, concat_axis=1, tiled=True)
    )
    spatial_mix = lax.all_to_all(attended, "seq", split_axis=1, concat_axis=2, tiled=True).reshape(
        frames_dev, tokens_dev, model_width
    )
    spatial_update = jnp.einsum(
        "fsd,de->fse",
        spatial_mix,
        lax.all_gather(spatial_out, "seq", axis=1, tiled=True),
        preferred_element_type=jnp.float32,
    )
    hidden_one = embedded + modulation[:, :, 2] * spatial_update
    temporal_in = modulate(hidden_one, modulation, 3).astype(jnp.bfloat16)
    temporal_proj = jnp.einsum(
        "fsd,dtk->fstk",
        temporal_in,
        lax.all_gather(temporal_qkv, "seq", axis=2, tiled=True),
        preferred_element_type=jnp.float32,
    ).astype(jnp.bfloat16)
    temporal_proj = temporal_proj.reshape(frames_dev, tokens_dev, 3, HEADS, head_dim)
    temporal_heads = temporal_attend(temporal_proj, advance, is_last)
    temporal_mix = temporal_heads.reshape(frames_dev, tokens_dev, model_width)
    temporal_update = jnp.einsum(
        "fsd,de->fse",
        temporal_mix,
        lax.all_gather(temporal_out, "seq", axis=1, tiled=True),
        preferred_element_type=jnp.float32,
    )
    hidden_two = hidden_one + modulation[:, :, 5] * temporal_update
    final_in = modulate(hidden_two, modulation, 6).astype(jnp.bfloat16)
    velocity = jnp.einsum("fsd,dc->fsc", final_in, final_w, preferred_element_type=jnp.float32)
    updated = latents - velocity / frames
    incoming = from_behind(updated[0], "queue", -1)
    tail_frame = jnp.where(is_last, fresh_noise, incoming)
    queue_next = jnp.concatenate([updated[1:], tail_frame[None]], axis=0)
    return (velocity, queue_next)


def solution(mesh):
    placed = (
        P("queue", "seq", None),
        P("queue"),
        P("queue"),
        P("seq", None),
        P(None, None, "seq"),
        P(),
        P(),
        P(None, "seq"),
        P(None, None, "seq"),
        P(None, "seq"),
        P(),
    )
    return jax.shard_map(
        shards,
        mesh=mesh,
        in_specs=placed,
        out_specs=(P("queue", "seq", None), P("queue", "seq", None)),
        check_vma=False,
    )
```

profile of v0, /device:TPU:2, one launch (start us, length us, event | category | flops | bytes accessed | tf_op | source)
XLA Modules:
  0.0 252.9 jit_solution(1472026502849320805)
XLA Ops:
  8.7 1.0 reshape.128
  10.8 30.1 %all_gather.12 = f32[2,8,1152]{1,0,2:T(2,128)S(1)} all-gather(f32[2,8,72]{1,0,2:T(2,128)S(1)} %copy.92), channel_id=1, replica_groups=mesh['queue'=16,'seq'=16] {'seq'}, dimensions={2}, use_global_device_ids=true | all-gather | bytes 78336 | tf_op jit(solution)/shard_map/all_gather | solution.py:91
  41.9 1.5 fusion.70
  43.6 4.7 %fusion.12 = bf16[2,64,3,1152]{3,1,2,0:T(8,128)(2,1)S(1)} fusion(bf16[1152,3,1152]{2,0,1:T(8,128)(2,1)} %param.19, f32[2,64,1152]{2,1,0:T(8,128)S(1)} %get-tuple-element.59, f32[2,1152]{1,0:T(2,128)S(1)} %get-tuple-element.53, f32[2,1152]{1,0:T(2,128)S(1)} %get-tuple-element.54, f32[2,64]{1,0:T(2,128)S(1)} %add_rsqrt_fusion.2, ...), kind=kOutput, calls=%fused_computation.19 | convolution fusion | flops 1020395520 | bytes 9456640 | tf_op jit(solution)/shard_map/fsd,dtk->fstk/dot_general | solution.py:97
  48.3 2.8 %reshape.130 = bf16[2,64,3,16,72]{4,3,1,2,0:T(8,128)(2,1)S(1)} reshape(bf16[2,64,3,1152]{3,1,2,0:T(8,128)(2,1)S(1)} %fusion.12) | data formatting | bytes 1769472 | tf_op jit(solution)/shard_map/reshape | solution.py:100
  51.1 1.6 copy.94
  52.6 3.7 %all-to-all-start = ((bf16[2,64,3,16,72]{4,1,2,0,3:T(8,128)(2,1)}), bf16[2,64,3,16,72]{4,1,2,0,3:T(8,128)(2,1)S(1)}, u32[]{:S(2)}, u32[]{:S(2)}) async-start(bf16[2,64,3,16,72]{4,1,2,0,3:T(8,128)(2,1)} %copy.94), calls=%async_computation | async-start | bytes 3145728 | tf_op jit(solution)/shard_map/all_to_all | solution.py:104
  57.1 23.1 %all-to-all-done = bf16[2,64,3,16,72]{4,1,2,0,3:T(8,128)(2,1)S(1)} async-done(((bf16[2,64,3,16,72]{4,1,2,0,3:T(8,128)(2,1)}), bf16[2,64,3,16,72]{4,1,2,0,3:T(8,128)(2,1)S(1)}, u32[]{:S(2)}, u32[]{:S(2)}) %all-to-all-start) | async-done | bytes 884768 | tf_op jit(solution)/shard_map/all_to_all | solution.py:104
  80.2 1.2 copy-done.1
  81.4 3.1 %copy.95 = bf16[2,16,64,3,1,72]{2,1,5,3,0,4:T(8,128)(2,1)S(1)} copy(bf16[2,16,64,3,1,72]{5,2,3,0,1,4:T(8,128)(2,1)} %bitcast.156) | data formatting | bytes 1769472 | tf_op jit(solution)/shard_map/all_to_all | solution.py:104
  84.5 1.3 all_to_all.27
  85.7 6.5 %while.10 = (s32[]{:T(128)}, bf16[2,1024,1,72]{1,3,2,0:T(8,128)(2,1)}, bf16[2,1024,3,1,72]{1,4,3,2,0:T(8,128)(2,1)S(1)}, s32[]{:T(128)}) while((s32[]{:T(128)}, bf16[2,1024,1,72]{1,3,2,0:T(8,128)(2,1)}, bf16[2,1024,3,1,72]{1,4,3,2,0:T(8,128)(2,1)S(1)}, s32[]{:T(128)}) %tuple.56), condition=%wide.region_5.6_spmd, body=%wide.region_2.5_spmd.sunk | while | flops 311498752 | bytes 16437365 | solution.py:44
  87.3 1.0 fusion.80
  90.6 1.0 fusion.80
  92.3 2.0 copy.97
  94.2 4.3 %all-to-all-start.1 = ((bf16[2,1024,1,72]{3,0,2,1:T(2,128)(2,1)}), bf16[2,1024,1,72]{3,0,2,1:T(2,128)(2,1)S(1)}, u32[]{:S(2)}, u32[]{:S(2)}) async-start(bf16[2,1024,1,72]{3,0,2,1:T(2,128)(2,1)} %copy.97), calls=%async_computation.1 | async-start | bytes 1048576 | tf_op jit(solution)/shard_map/all_to_all | solution.py:106
  99.2 12.4 %all-to-all-done.1 = bf16[2,1024,1,72]{3,0,2,1:T(2,128)(2,1)S(1)} async-done(((bf16[2,1024,1,72]{3,0,2,1:T(2,128)(2,1)}), bf16[2,1024,1,72]{3,0,2,1:T(2,128)(2,1)S(1)}, u32[]{:S(2)}, u32[]{:S(2)}) %all-to-all-start.1) | async-done | bytes 294944 | tf_op jit(solution)/shard_map/all_to_all | solution.py:106
  112.4 2.8 %fusion.71 = (f32[2,64]{1,0:T(2,128)S(1)}, f32[2,64,1152]{2,1,0:T(8,128)S(1)}) fusion(f32[2,64,1152]{2,1,0:T(8,128)S(1)} %get-tuple-element.59, bf16[2,64,1152]{2,1,0:T(8,128)(2,1)S(1)} %reshape.131, bf16[1152,1152]{0,1:T(8,128)(2,1)} %all-gather.4.cloned.1.call-done, f32[2,1152]{1,0:T(2,128)S(1)} %get-tuple-element.55), kind=kOutput, calls=%fused_computation.100 | convolution fusion | flops 340180864 | bytes 4138496 | tf_op jit(solution)/shard_map/fsd,de->fse/dot_general | solution.py:109
  115.4 45.0 %all-gather.6.cloned.1.call-done = bf16[1152,3,1152]{0,2,1:T(8,128)(2,1)} async-done(((bf16[1152,3,72]{0,2,1:T(8,128)(2,1)}), bf16[1152,3,1152]{0,2,1:T(8,128)(2,1)}) %all-gather.6.cloned.1.call-update) | async-done | bytes 7962640 | tf_op jit(solution)/shard_map/all_gather | solution.py:120
  160.4 6.6 %fusion.15 = bf16[2,64,3,1152]{3,1,2,0:T(8,128)(2,1)} fusion(bf16[1152,3,1152]{0,2,1:T(8,128)(2,1)} %all-gather.6.cloned.1.call-done, f32[2,64,1152]{2,1,0:T(8,128)S(1)} %get-tuple-element.61, f32[2,1152]{1,0:T(2,128)S(1)} %get-tuple-element.50, f32[2,1152]{1,0:T(2,128)S(1)} %get-tuple-element.51, f32[2,64]{1,0:T(2,128)S(1)} %add_rsqrt_fusion.1, ...), kind=kOutput, calls=%fused_computation.20 | convolution fusion | flops 1020395520 | bytes 9456640 | tf_op jit(solution)/shard_map/fsd,dtk->fstk/dot_general | solution.py:117
  167.1 4.0 %reshape.132 = bf16[2,64,3,16,72]{4,3,1,2,0:T(8,128)(2,1)S(1)} reshape(bf16[2,64,3,1152]{3,1,2,0:T(8,128)(2,1)} %fusion.15) | data formatting | bytes 1769472 | tf_op jit(solution)/shard_map/reshape | solution.py:123
  171.2 1.6 copy.110
  172.8 6.3 %collective-permute-start = (bf16[2,64,2,16,72]{4,0,3,1,2:T(2,128)(2,1)S(1)}, bf16[2,64,2,16,72]{4,0,3,1,2:T(2,128)(2,1)S(1)}, u32[]{:S(2)}, u32[]{:S(2)}) collective-permute-start(bf16[2,64,2,16,72]{4,0,3,1,2:T(2,128)(2,1)S(1)} %copy.110), channel_id=1, source_target_pairs={{16,0},{32,16},{48,32},{64,48},{80,64},{96,80},{112,96},{128,112},... | collective-permute-start | bytes 1769480 | tf_op jit(solution)/shard_map/ppermute | solution.py:14
  179.5 1.6 copy_bitcast_fusion
  181.1 20.7 %collective-permute-done = bf16[2,64,2,16,72]{4,0,3,1,2:T(2,128)(2,1)S(1)} collective-permute-done((bf16[2,64,2,16,72]{4,0,3,1,2:T(2,128)(2,1)S(1)}, bf16[2,64,2,16,72]{4,0,3,1,2:T(2,128)(2,1)S(1)}, u32[]{:S(2)}, u32[]{:S(2)}) %collective-permute-start) | collective-permute-done | bytes 589856 | tf_op jit(solution)/shard_map/ppermute | solution.py:14
  202.5 4.7 %fusion.72 = (f32[64,16,2]{2,1,0:T(8,128)}, f32[64,16,2,4]{3,2,1,0:T(2,128)}) fusion(bf16[2,64,16,72]{3,0,2,1:T(2,128)(2,1)S(1)} %get-tuple-element.46, bf16[2,64,16,72]{3,0,2,1:T(2,128)(2,1)S(1)} %get-tuple-element.68, pred[4]{0:T(512)(128)(4,1)S(1)} %compare_or_fusion, bf16[2,64,1,16,72]{4,3,1,2,0:T(8,128)(2,1)S(1)} %get-tuple-element.43), kind=kOutput, calls=%fused_computation.101 | convolution fusion | flops 2392067 | bytes 925700 | tf_op jit(solution)/shard_map/sub | solution.py:61
  207.1 3.3 %fusion.37 = bf16[2,64,16,72]{3,0,2,1:T(2,128)(2,1)S(1)} fusion(bf16[2,64,16,72]{3,0,2,1:T(2,128)(2,1)S(1)} %get-tuple-element.47, bf16[2,64,16,72]{3,0,2,1:T(2,128)(2,1)S(1)} %get-tuple-element.69, f32[64,16,2,4]{3,2,1,0:T(2,128)} %get-tuple-element.63, f32[64,16,2]{2,1,0:T(8,128)} %get-tuple-element.62), kind=kOutput, calls=%fused_computation.34 | convolution fusion | flops 2523136 | bytes 925696 | tf_op jit(solution)/shard_map/shij,jshe->ishe/dot_general | solution.py:62
  211.0 23.3 %all-gather.8.cloned.1.call-done = bf16[1152,1152]{0,1:T(8,128)(2,1)} async-done(((bf16[1152,72]{0,1:T(8,128)(2,1)}), bf16[1152,1152]{0,1:T(8,128)(2,1)}) %all-gather.8.cloned.1.call-update) | async-done | bytes 2654224 | tf_op jit(solution)/shard_map/all_gather | solution.py:129
  234.3 2.8 %fusion.73 = (f32[2,64]{1,0:T(2,128)S(1)}, f32[2,64,1152]{2,1,0:T(8,128)S(1)}) fusion(f32[2,64,1152]{2,1,0:T(8,128)S(1)} %get-tuple-element.61, bf16[2,64,1152]{2,1,0:T(8,128)(2,1)S(1)} %reshape.133, bf16[1152,1152]{0,1:T(8,128)(2,1)} %all-gather.8.cloned.1.call-done, f32[2,1152]{1,0:T(2,128)S(1)} %get-tuple-element.52), kind=kOutput, calls=%fused_computation.102 | convolution fusion | flops 340180864 | bytes 4138496 | tf_op jit(solution)/shard_map/fsd,de->fse/dot_general | solution.py:126
  237.3 1.0 multiply_subtract_fusion
  238.3 6.1 %collective-permute-start.1 = (f32[64,16]{0,1:T(8,128)S(1)}, f32[64,16]{0,1:T(8,128)S(1)}, u32[]{:S(2)}, u32[]{:S(2)}) collective-permute-start(f32[64,16]{0,1:T(8,128)S(1)} %get-tuple-element.57), channel_id=1, source_target_pairs={{16,0},{32,16},{48,32},{64,48},{80,64},{96,80},{112,96},{128,112},... | collective-permute-start | bytes 12296 | tf_op jit(solution)/shard_map/ppermute | solution.py:14
  244.4 1.3 collective-permute-done.1
  (56 shorter events, 12.7 us)
Async XLA Ops:
  7.2 34.7 %copy-start = (f32[16,1152]{1,0:T(8,128)S(1)}, f32[16,1152]{1,0:T(8,128)}, u32[]{:S(2)}) copy-start(f32[16,1152]{1,0:T(8,128)} %param.18) | copy-start | bytes 221188
  7.2 105.2 %all-gather.4.cloned.1.call-start = ((), (), s32[]{:S(2)}) async-start(), calls=%async_computation.2 | async-start | bytes 2820096 | tf_op jit(solution)/shard_map/all_gather | solution.py:112
  7.9 152.5 %all-gather.6.cloned.1.call-start = ((), (), s32[]{:S(2)}) async-start(), calls=%async_computation.3 | async-start | bytes 8460288 | tf_op jit(solution)/shard_map/all_gather | solution.py:120
  52.6 27.6 %all-to-all-start = ((bf16[2,64,3,16,72]{4,1,2,0,3:T(8,128)(2,1)}), bf16[2,64,3,16,72]{4,1,2,0,3:T(8,128)(2,1)S(1)}, u32[]{:S(2)}, u32[]{:S(2)}) async-start(bf16[2,64,3,16,72]{4,1,2,0,3:T(8,128)(2,1)} %copy.94), calls=%async_computation | async-start | bytes 3145728 | tf_op jit(solution)/shard_map/all_to_all | solution.py:104
  56.4 177.9 %all-gather.8.cloned.1.call-start = ((), (), s32[]{:S(2)}) async-start(), calls=%async_computation.4 | async-start | bytes 2820096 | tf_op jit(solution)/shard_map/all_gather | solution.py:129
  80.2 1.2 copy-start.1
  85.8 1.5 copy-start.2
  88.3 0.7 copy-start.3
  89.0 1.5 copy-start.2
  91.5 0.7 copy-start.3
  94.2 17.3 %all-to-all-start.1 = ((bf16[2,1024,1,72]{3,0,2,1:T(2,128)(2,1)}), bf16[2,1024,1,72]{3,0,2,1:T(2,128)(2,1)S(1)}, u32[]{:S(2)}, u32[]{:S(2)}) async-start(bf16[2,1024,1,72]{3,0,2,1:T(2,128)(2,1)} %copy.97), calls=%async_computation.1 | async-start | bytes 1048576 | tf_op jit(solution)/shard_map/all_to_all | solution.py:106
  172.8 28.9 %collective-permute-start = (bf16[2,64,2,16,72]{4,0,3,1,2:T(2,128)(2,1)S(1)}, bf16[2,64,2,16,72]{4,0,3,1,2:T(2,128)(2,1)S(1)}, u32[]{:S(2)}, u32[]{:S(2)}) collective-permute-start(bf16[2,64,2,16,72]{4,0,3,1,2:T(2,128)(2,1)S(1)} %copy.110), channel_id=1, source_target_pairs={{16,0},{32,16},{48,32},{64,48},{80,64},{96,80},{112,96},{128,112},... | collective-permute-start | bytes 1769480 | tf_op jit(solution)/shard_map/ppermute | solution.py:14
  210.4 26.9 %copy-start.4 = (f32[2,64,16]{1,2,0:T(8,128)S(1)}, f32[2,64,16]{1,2,0:T(8,128)}, u32[]{:S(2)}) copy-start(f32[2,64,16]{1,2,0:T(8,128)} %param.13) | copy-start | bytes 24580
  210.4 26.9 %copy-start.6 = (bf16[1152,16]{0,1:T(8,128)(2,1)S(1)}, bf16[1152,16]{0,1:T(8,128)(2,1)}, u32[]{:S(2)}) copy-start(bf16[1152,16]{0,1:T(8,128)(2,1)} %param.23) | copy-start | bytes 110596
  210.4 35.3 %copy-start.5 = (f32[64,16]{0,1:T(8,128)S(1)}, f32[64,16]{0,1:T(8,128)}, u32[]{:S(2)}) copy-start(f32[64,16]{0,1:T(8,128)} %param.16) | copy-start | bytes 12292
  238.3 7.5 %collective-permute-start.1 = (f32[64,16]{0,1:T(8,128)S(1)}, f32[64,16]{0,1:T(8,128)S(1)}, u32[]{:S(2)}, u32[]{:S(2)}) collective-permute-start(f32[64,16]{0,1:T(8,128)S(1)} %get-tuple-element.57), channel_id=1, source_target_pairs={{16,0},{32,16},{48,32},{64,48},{80,64},{96,80},{112,96},{128,112},... | collective-permute-start | bytes 12296 | tf_op jit(solution)/shard_map/ppermute | solution.py:14
Sparse Core Ops, SparseCore 0:
  10.7 66.4 all-gather.3
  79.9 80.4 all-gather.5
  163.1 71.1 all-gather.7
where the time goes:
time: 254 us; the launch traced here: 253 us
  waiting for transfers between devices  128 us (50%)
  matrix products  31.5 us (12%)
  blocking collectives  30.1 us (12%)
  local copies, waits for them, and re-layouts  25.4 us (10%)
  starting transfers between devices  20.6 us (8%)
  between operations  14.7 us (6%)
  other arithmetic  2.77 us (1%)
    all_gather x1, waiting for transfers between devices, shards(): lax.all_gather(temporal_qkv, 'seq', axis=2, tiled=True)  45 us
    all_gather x1, blocking collectives, shards(): lax.all_gather(own_rows, 'seq', axis=2, tiled=True)  30.1 us
    all_gather x1, waiting for transfers between devices, shards(): lax.all_gather(temporal_out, 'seq', axis=1, tiled=True)  23.3 us
    all_to_all x1, waiting for transfers between devices, shards(): lax.all_to_all(token_layout, 'seq', split_axis=3, concat_axis=1, tiled=True)  23.1 us
    ppermute x2, waiting for transfers between devices, from_behind(): return lax.ppermute(array, axis, pairs)  22 us
    ppermute x2, starting transfers between devices, from_behind(): return lax.ppermute(array, axis, pairs)  12.4 us
    all_to_all x1, waiting for transfers between devices, shards(): lax.all_to_all(attended, 'seq', split_axis=1, concat_axis=2, tiled=True)  12.4 us
    dot_general x1, matrix products, shards(): jnp.einsum('fsd,dtk->fstk', temporal_in, lax.all_gather(temporal_qkv, 'se...  6.64 us
  transfers between devices with their start and end apart: 7, of which 6 were waited for; matrix products, arithmetic and copies ran while one was open for 20% of the time, Pallas kernels for 0%

commit v1 on v0

v1 whole, which is shorter than its diff:
```python
import math

import jax
import jax.numpy as jnp
from jax import lax
from jax.experimental import pallas as pl
from jax.experimental.pallas import tpu as pltpu
from jax.sharding import PartitionSpec as P

HEADS = 16
HD = 72
D = HEADS * HD
C = 16
CP = 32
BF = jnp.bfloat16
F32 = jnp.float32
VMEM = pl.BlockSpec(memory_space=pltpu.VMEM)
SMEM = pl.BlockSpec(memory_space=pltpu.SMEM)


def split(value):
    high = value.astype(BF)
    return high, (value - high.astype(F32)).astype(BF)


def dot_tn(a, b):
    return lax.dot_general(a, b, (((0,), (0,)), ((), ())), preferred_element_type=F32)


def dot_nt(a, b):
    return lax.dot_general(a, b, (((1,), (1,)), ((), ())), preferred_element_type=F32)


def dot_nn(a, b):
    return jnp.dot(a, b, preferred_element_type=F32)


def product_tn(a, b):
    a_high, a_low = split(a)
    b_high, b_low = split(b)
    return dot_tn(
        jnp.concatenate([a_high, a_low, a_high], axis=0),
        jnp.concatenate([b_high, b_high, b_low], axis=0),
    )


def both_frames(latents_ref):
    return jnp.concatenate([latents_ref[0], latents_ref[1]], axis=1)


def normalize(hidden):
    width = hidden.shape[0]
    mean_value = jnp.sum(hidden, axis=0, keepdims=True) * (1.0 / width)
    centered = hidden - mean_value
    variance = jnp.sum(centered * centered, axis=0, keepdims=True) * (1.0 / width)
    return centered * lax.rsqrt(variance + 1e-06)


def modulation_columns(mod, rows):
    tokens = 128
    high, low = split(mod)
    row_at = lax.broadcasted_iota(jnp.int32, (16, tokens * len(rows)), 0)
    lane_at = lax.broadcasted_iota(jnp.int32, (16, tokens * len(rows)), 1)
    wanted = jnp.zeros_like(row_at)
    for place, row in enumerate(rows):
        wanted = jnp.where(lane_at // tokens == place, row, wanted)
    wanted = wanted + 8 * ((lane_at % tokens) // 64)
    chosen = (row_at == wanted).astype(F32).astype(BF)
    columns = dot_tn(
        jnp.concatenate([high, low], axis=0), jnp.concatenate([chosen, chosen], axis=0)
    )
    return [columns[:, tokens * i : tokens * (i + 1)] for i in range(len(rows))]


def pack_kernel(levels_ref, latents_ref, embed_ref, table_ref, out_ref):
    channels = both_frames(latents_ref)
    embed = embed_ref[...]
    centered = embed - jnp.sum(embed, axis=1, keepdims=True) * (1.0 / D)
    spread = product_tn(centered, channels)
    variance = jnp.sum(spread * spread, axis=0, keepdims=True) * (1.0 / D)
    scaled = channels * lax.rsqrt(variance + 1e-06)
    peers = out_ref.shape[0]
    for peer in range(peers):
        out_ref[peer, 0:16, :] = scaled
        for frame in range(2):
            rows = table_ref[levels_ref[frame]]
            out_ref[peer, 16 + 8 * frame : 24 + 8 * frame, 0:HD] = rows


def spatial_kernel(own_ref, all_ref, embed_ref, weight_ref, mix_ref, mod_ref, tokens_ref, query_ref, part_ref):
    peers = all_ref.shape[0]
    for peer in range(peers):
        mod_ref[:, HD * peer : HD * (peer + 1)] = all_ref[peer, 16:32, 0:HD]
        for frame in range(2):
            tokens_ref[frame, :, 64 * peer : 64 * (peer + 1)] = all_ref[
                peer, 0:16, 64 * frame : 64 * (frame + 1)
            ]
    mod = mod_ref[...]
    embed = embed_ref[...]
    centered = embed - jnp.sum(embed, axis=1, keepdims=True) * (1.0 / D)
    row16 = lax.broadcasted_iota(jnp.int32, (16, D), 0)
    rows = []
    for frame in range(2):
        rows.append(centered * (1.0 + mod[8 * frame + 1 : 8 * frame + 2]))
        rows.append(jnp.where(row16 == 0, mod[8 * frame : 8 * frame + 1], 0.0))
    high, low = split(jnp.concatenate(rows, axis=0))
    stacked = jnp.concatenate([high, low], axis=0)

    def coefficients(index):
        both = dot_nn(stacked, weight_ref[index])
        return both[0:64] + both[64:128]

    query_all = coefficients(0)
    key_all = coefficients(1)
    value_all = coefficients(2)
    own_head = (
        lax.broadcasted_iota(jnp.int32, (HEADS * CP, D), 0) // CP
        == lax.broadcasted_iota(jnp.int32, (HEADS * CP, D), 1) // HD
    )
    scale = math.log2(math.e) / math.sqrt(HD)
    one_row = (lax.broadcasted_iota(jnp.int32, (16, 64), 0) == 0).astype(F32)
    one_row_all = (lax.broadcasted_iota(jnp.int32, (16, 1024), 0) == 0).astype(F32)
    for frame in range(2):
        query_part = query_all[32 * frame : 32 * (frame + 1)]
        key_part = key_all[32 * frame : 32 * (frame + 1)]
        value_part = value_all[32 * frame : 32 * (frame + 1)]
        key_heads = jnp.where(own_head, jnp.concatenate([key_part] * HEADS, axis=0), 0.0).astype(BF)
        pair = dot_nt(key_heads, query_part.astype(BF)) * scale
        own = jnp.concatenate([own_ref[0, 0:16, 64 * frame : 64 * (frame + 1)], one_row], axis=0)
        own_high, own_low = split(own)
        pair_high, pair_low = split(pair)
        reduced = dot_nn(
            jnp.concatenate([pair_high, pair_low, pair_high], axis=1),
            jnp.concatenate([own_high, own_high, own_low], axis=0),
        )
        for head in range(HEADS):
            query_ref[:, 64 * head : 64 * (head + 1)] = reduced[CP * head : CP * (head + 1)]
        query_high, query_low = split(query_ref[...])
        queries = jnp.concatenate([query_high, query_low, query_high], axis=0)
        tokens = tokens_ref[frame]
        token_high, token_low = split(jnp.concatenate([tokens, one_row_all], axis=0))
        keys = jnp.concatenate([token_high, token_high, token_low], axis=0)
        values = jnp.concatenate(
            [token_high, token_low[0:16]], axis=0
        )
        for chunk in range(4):
            scores = dot_tn(keys, queries[:, 256 * chunk : 256 * (chunk + 1)])
            top = jnp.max(scores, axis=0, keepdims=True)
            weights = jnp.exp2(scores - top).astype(BF)
            summed = dot_nn(values, weights)
            mixed = (summed[0:16] + summed[32:48]) / summed[16:17]
            for sub in range(4):
                head = 4 * chunk + sub
                part_ref[frame, CP * head : CP * head + 16, :] = mixed[:, 64 * sub : 64 * (sub + 1)]
                part_ref[frame, CP * head + 16 : CP * head + 32, :] = one_row
        value_heads = jnp.where(own_head, jnp.concatenate([value_part] * HEADS, axis=0), 0.0).astype(BF)
        mix_ref[64 * frame : 64 * (frame + 1), :] = dot_tn(
            part_ref[frame].astype(BF), value_heads
        ).astype(BF)


def chip_order(me):
    across = me ^ 2
    return [
        me,
        across,
        lax.rem(me + 12, 16),
        lax.rem(me + 4, 16),
        lax.rem(across + 12, 16),
        lax.rem(across + 4, 16),
        lax.rem(me + 8, 16),
        lax.rem(across + 8, 16),
    ]


def at_rows(index):
    return pl.ds(pl.multiple_of(index * HD, 8), HD)


def hidden_kernel(mix_ref, latents_ref, embed_ref, mod_ref, *rest):
    *blocks, hidden_ref, inner_ref, update_ref = rest
    order = chip_order(lax.axis_index("seq"))
    mix = mix_ref[...]
    for place, index in enumerate(order):
        update_ref[at_rows(index), :] = dot_nt(blocks[0][place], mix)
        update_ref[at_rows(index ^ 1), :] = dot_nt(blocks[1][place], mix)
    embedded = product_tn(embed_ref[...], both_frames(latents_ref))
    gate, shift, scale = modulation_columns(mod_ref[...], (2, 3, 4))
    hidden = embedded + gate * update_ref[...]
    hidden_ref[...] = hidden
    inner_ref[...] = (normalize(hidden) * (1.0 + scale) + shift).astype(BF)


def temporal_kernel(advance_ref, own_ref, peer_ref, own_next_ref, peer_next_ref, *rest):
    *blocks, out_own_ref, out_peer_ref = rest
    tokens = jnp.concatenate([own_ref[...], peer_ref[...]], axis=1)
    following = jnp.concatenate([own_next_ref[...], peer_next_ref[...]], axis=1)
    last = lax.axis_index("queue") == lax.axis_size("queue") - 1
    limit = jnp.where(last, 0, advance_ref[0])
    frame = lax.broadcasted_iota(jnp.int32, (1, 128), 1) // 64
    keep_same = frame < limit
    keep_other = (1 - frame) < limit
    scale = math.log2(math.e) / math.sqrt(HD)
    for place, block in enumerate(blocks):
        query = dot_nn(block[0], tokens) * scale
        key = dot_nn(block[1], tokens)
        key_next = dot_nn(block[1], following)
        value = dot_nn(block[2], tokens)
        value_next = dot_nn(block[2], following)
        for side, out_ref in enumerate((out_own_ref, out_peer_ref)):
            lanes = slice(128 * side, 128 * (side + 1))
            asked = query[:, lanes]
            keys = [key[:, lanes], key_next[:, lanes]]
            values = [value[:, lanes], value_next[:, lanes]]
            keys = [keys[0], pltpu.roll(keys[0], 64, 1), keys[1], pltpu.roll(keys[1], 64, 1)]
            values = [values[0], pltpu.roll(values[0], 64, 1), values[1], pltpu.roll(values[1], 64, 1)]
            scores = [jnp.sum(asked * one, axis=0, keepdims=True) for one in keys]
            scores[2] = jnp.where(keep_same, scores[2], -1e30)
            scores[3] = jnp.where(keep_other, scores[3], -1e30)
            top = jnp.maximum(jnp.maximum(scores[0], scores[1]), jnp.maximum(scores[2], scores[3]))
            weights = [jnp.exp2(one - top) for one in scores]
            inverse = 1.0 / (weights[0] + weights[1] + weights[2] + weights[3])
            mixed = sum(w * inverse * v for w, v in zip(weights, values))
            out_ref[HD * place : HD * (place + 1), :] = mixed


def final_kernel(own_ref, peer_ref, hidden_ref, latents_ref, mod_ref, final_ref, *rest):
    *blocks, velocity_ref, updated_ref, mix_ref, update_ref = rest
    order = chip_order(lax.axis_index("seq"))
    for place, index in enumerate(order):
        rows = slice(HD * place, HD * (place + 1))
        mix_ref[at_rows(index), :] = own_ref[rows, :].astype(F32)
        mix_ref[at_rows(index ^ 1), :] = peer_ref[rows, :].astype(F32)
    mix = mix_ref[...].astype(BF)
    for place, index in enumerate(order):
        update_ref[at_rows(index), :] = dot_nn(blocks[0][place], mix)
        update_ref[at_rows(index ^ 1), :] = dot_nn(blocks[1][place], mix)
    gate, shift, scale = modulation_columns(mod_ref[...], (5, 6, 7))
    hidden = hidden_ref[...] + gate * update_ref[...]
    inner = (normalize(hidden) * (1.0 + scale) + shift).astype(BF)
    velocity = dot_nn(final_ref[...], inner)
    for frame in range(2):
        part = velocity[:, 64 * frame : 64 * (frame + 1)]
        velocity_ref[frame] = part
        updated_ref[frame] = latents_ref[frame] - part * (1.0 / 32.0)


def params(mebibytes):
    return pltpu.CompilerParams(vmem_limit_bytes=mebibytes << 20)


def cost(flops, moved):
    return pl.CostEstimate(flops=flops, bytes_accessed=moved, transcendentals=0)


def along_seq(array, to):
    return lax.ppermute(array, "seq", [(i, to(i)) for i in range(16)])


def y_up(array):
    return along_seq(array, lambda i: (i + 4) % 16)


def y_down(array):
    return along_seq(array, lambda i: (i + 12) % 16)


def over_x(array):
    return along_seq(array, lambda i: i ^ 2)


def other_core(array):
    return along_seq(array, lambda i: i ^ 1)


def from_next(array):
    return lax.ppermute(array, "queue", [(i, i - 1) for i in range(1, 16)])


def gather(own):
    across = over_x(own)
    below, above = y_up(own), y_down(own)
    below_across, above_across = y_up(across), y_down(across)
    return [own, across, below, above, below_across, above_across, y_up(below), y_down(above_across)]


def shards(
    latents,
    levels,
    advance,
    fresh_noise,
    level_mod,
    embed_w,
    spatial_qkv,
    spatial_out,
    temporal_qkv,
    temporal_out,
    final_w,
):
    lat = latents.transpose(0, 2, 1)
    spatial_w = spatial_qkv.transpose(1, 0, 2)
    out_w = spatial_out.transpose(1, 0)
    temporal_w = temporal_qkv.transpose(1, 2, 0)
    last_w = temporal_out.transpose(1, 0)
    final_t = final_w.transpose(1, 0)

    packed = pl.pallas_call(
        pack_kernel,
        out_shape=jax.ShapeDtypeStruct((16, 32, 128), F32),
        in_specs=[SMEM, VMEM, VMEM, VMEM],
        out_specs=VMEM,
        name="pack",
    )(levels, lat, embed_w, level_mod)
    everyone = lax.all_to_all(packed, "seq", split_axis=0, concat_axis=0, tiled=True)
    out_own = jnp.stack(gather(out_w))
    out_peer = other_core(out_own)
    temporal_blocks = gather(temporal_w)
    last_own = jnp.stack(gather(last_w))
    last_peer = other_core(last_own)

    mix, mod = pl.pallas_call(
        spatial_kernel,
        out_shape=(
            jax.ShapeDtypeStruct((128, D), BF),
            jax.ShapeDtypeStruct((16, D), F32),
        ),
        in_specs=[VMEM] * 4,
        out_specs=(VMEM, VMEM),
        scratch_shapes=[
            pltpu.VMEM((2, 16, 1024), F32),
            pltpu.VMEM((CP, 1024), F32),
            pltpu.VMEM((2, HEADS * CP, 64), F32),
        ],
        compiler_params=params(40),
        cost_estimate=cost(10**10, 10**7),
        name="spatial",
    )(packed, everyone, embed_w, spatial_w)

    hidden, inner = pl.pallas_call(
        hidden_kernel,
        out_shape=(
            jax.ShapeDtypeStruct((D, 128), F32),
            jax.ShapeDtypeStruct((D, 128), BF),
        ),
        in_specs=[VMEM] * 6,
        out_specs=(VMEM, VMEM),
        scratch_shapes=[pltpu.VMEM((D, 128), F32)],
        compiler_params=params(32),
        name="hidden",
    )(mix, lat, embed_w, mod, out_own, out_peer)
    following = from_next(inner)
    inner_peer = other_core(inner)
    following_peer = other_core(following)
    parts = []
    for first, end in ((0, 4), (4, 6), (6, 8)):
        rows = HD * (end - first)
        parts.append(
            pl.pallas_call(
                temporal_kernel,
                out_shape=(
                    jax.ShapeDtypeStruct((rows, 128), F32),
                    jax.ShapeDtypeStruct((rows, 128), F32),
                ),
                in_specs=[SMEM] + [VMEM] * (4 + end - first),
                out_specs=(VMEM, VMEM),
                compiler_params=params(32),
                name=f"temporal_{first}",
            )(advance, inner, inner_peer, following, following_peer, *temporal_blocks[first:end])
        )
    mix_own = jnp.concatenate([part[0] for part in parts], axis=0)
    mix_peer = jnp.concatenate([other_core(part[1].astype(BF)) for part in parts], axis=0)
    velocity, updated = pl.pallas_call(
        final_kernel,
        out_shape=(
            jax.ShapeDtypeStruct((2, C, 64), F32),
            jax.ShapeDtypeStruct((2, C, 64), F32),
        ),
        in_specs=[VMEM] * 8,
        out_specs=(VMEM, VMEM),
        scratch_shapes=[pltpu.VMEM((D, 128), F32), pltpu.VMEM((D, 128), F32)],
        compiler_params=params(32),
        name="final",
    )(mix_own, mix_peer, hidden, lat, mod, final_t, last_own, last_peer)
    incoming = from_next(updated[0])
    is_last = lax.axis_index("queue") == lax.axis_size("queue") - 1
    tail = jnp.where(is_last, fresh_noise.transpose(1, 0), incoming)
    queue_next = jnp.stack([updated[1], tail])
    return velocity.transpose(0, 2, 1), queue_next.transpose(0, 2, 1)


def solution(mesh):
    placed = (
        P("queue", "seq", None),
        P("queue"),
        P("queue"),
        P("seq", None),
        P(None, None, "seq"),
        P(),
        P(),
        P(None, "seq"),
        P(None, None, "seq"),
        P(None, "seq"),
        P(),
    )
    return jax.shard_map(
        shards,
        mesh=mesh,
        in_specs=placed,
        out_specs=(P("queue", "seq", None), P("queue", "seq", None)),
        check_vma=False,
    )
```

time: 254 us -> 129 us (0.51)
  waiting for transfers between devices: 128 us -> 52.7 us
  matrix products: 31.5 us -> 0 us
  blocking collectives: 30.1 us -> 0 us
  Pallas kernels: 0 us -> 26.5 us
  starting transfers between devices: 20.6 us -> 42.9 us
  local copies, waits for them, and re-layouts: 25.4 us -> 4.51 us
  between operations: 14.7 us -> 1.66 us
    all_gather x3 -> x0, waiting for transfers between devices: 68.3 us -> none  [the longest x1 45 us: shards(): lax.all_gather(temporal_qkv, 'seq', axis=2, tiled=True)]
    all_to_all x2 -> x1, waiting for transfers between devices: 35.5 us -> 0.01 us  [shards(): lax.all_to_all(packed, 'seq', split_axis=0, concat_axis=0, tiled=True)]
    ppermute x2 -> x30, waiting for transfers between devices: 22 us -> 52.7 us  [the longest x28 44.2 us: along_seq(): return lax.ppermute(array, 'seq', [(i, to(i)) for i in range(16)])]
    all_gather x1 -> x0, blocking collectives: 30.1 us -> none  [shards(): lax.all_gather(own_rows, 'seq', axis=2, tiled=True)]
    dot_general x12 -> x0, matrix products: 26.8 us -> none  [the longest x1 6.64 us: shards(): jnp.einsum('fsd,dtk->fstk', temporal_in, lax.all_gather(temporal_qkv, 'se...]
    pallas_call x0 -> x7, Pallas kernels: none -> 26.5 us  [the longest x1 10.4 us: shards(): pl.pallas_call(spatial_kernel, out_shape=(jax.ShapeDtypeStruct((128, D),...]
    ppermute x2 -> x30, starting transfers between devices: 12.4 us -> 37 us  [the longest x28 25.5 us: along_seq(): return lax.ppermute(array, 'seq', [(i, to(i)) for i in range(16)])]
    reshape x6 -> x0, local copies, waits for them, and re-layouts: 10.3 us -> none  [the longest x2 4.34 us: shards(): projected.astype(jnp.bfloat16)]
  transfers between devices with their start and end apart: 7 -> 31, of which waited for: 6 -> 16; matrix products, arithmetic and copies ran while one was open for 20% -> 1% of each run, Pallas kernels for 0% -> 18%
where the time goes in v1:
time: 129 us
  waiting for transfers between devices  52.7 us (41%)
  starting transfers between devices  42.9 us (33%)
  Pallas kernels  26.5 us (21%)
  local copies, waits for them, and re-layouts  4.51 us (3%)
  between operations  1.66 us (1%)
    ppermute x28, waiting for transfers between devices, along_seq(): return lax.ppermute(array, 'seq', [(i, to(i)) for i in range(16)])  44.2 us
    ppermute x28, starting transfers between devices, along_seq(): return lax.ppermute(array, 'seq', [(i, to(i)) for i in range(16)])  25.5 us
    ppermute x2, starting transfers between devices, from_next(): return lax.ppermute(array, 'queue', [(i, i - 1) for i in range(1, 16)])  11.5 us
    pallas_call x1, Pallas kernels, shards(): pl.pallas_call(spatial_kernel, out_shape=(jax.ShapeDtypeStruct((128, D),...  10.4 us
    ppermute x2, waiting for transfers between devices, from_next(): return lax.ppermute(array, 'queue', [(i, i - 1) for i in range(1, 16)])  8.54 us
    pallas_call x3, Pallas kernels, shards(): pl.pallas_call(temporal_kernel, out_shape=(jax.ShapeDtypeStruct((rows, 12...  6.26 us
    all_to_all x1, starting transfers between devices, shards(): lax.all_to_all(packed, 'seq', split_axis=0, concat_axis=0, tiled=True)  5.89 us
    unnamed x28, local copies, waits for them, and re-layouts  4.47 us
  transfers between devices with their start and end apart: 31, of which 16 were waited for; matrix products, arithmetic and copies ran while one was open for 1% of the time, Pallas kernels for 18%

profile of v1, /device:TPU:2, one launch (start us, length us, event | category | flops | bytes accessed | tf_op | source)
XLA Modules:
  0.0 129.0 jit_solution(2158138105210561617)
XLA Ops:
  0.6 2.2 %collective-permute-start = (bf16[72,1152]{1,0:T(8,128)(2,1)}, bf16[72,1152]{1,0:T(8,128)(2,1)S(1)}, u32[]{:S(2)}, u32[]{:S(2)}) collective-permute-start(bf16[72,1152]{1,0:T(8,128)(2,1)} %bitcast.56), channel_id=1, source_target_pairs={{0,2},{1,3},{2,0},{3,1},{4,6},{5,7},{6,4},{7,5},{8,10},{9,11},{10,... | collective-permute-start | bytes 497672 | tf_op jit(solution)/shard_map/ppermute | solution.py:257
  2.9 1.6 %collective-permute-start.1 = (bf16[72,1152]{1,0:T(8,128)(2,1)}, bf16[72,1152]{1,0:T(8,128)(2,1)S(1)}, u32[]{:S(2)}, u32[]{:S(2)}) collective-permute-start(bf16[72,1152]{1,0:T(8,128)(2,1)} %bitcast.57), channel_id=1, source_target_pairs={{0,4},{1,5},{2,6},{3,7},{4,8},{5,9},{6,10},{7,11},{8,12},{9,13},{1... | collective-permute-start | bytes 497672 | tf_op jit(solution)/shard_map/ppermute | solution.py:257
  4.4 1.7 %collective-permute-start.2 = (bf16[72,1152]{1,0:T(8,128)(2,1)}, bf16[72,1152]{1,0:T(8,128)(2,1)S(1)}, u32[]{:S(2)}, u32[]{:S(2)}) collective-permute-start(bf16[72,1152]{1,0:T(8,128)(2,1)} %bitcast.58), channel_id=1, source_target_pairs={{0,12},{1,13},{2,14},{3,15},{4,0},{5,1},{6,2},{7,3},{8,4},{9,5},{1... | collective-permute-start | bytes 497672 | tf_op jit(solution)/shard_map/ppermute | solution.py:257
  6.1 1.4 %collective-permute-start.11 = (bf16[3,72,1152]{2,1,0:T(8,128)(2,1)}, bf16[3,72,1152]{2,1,0:T(8,128)(2,1)}, u32[]{:S(2)}, u32[]{:S(2)}) collective-permute-start(bf16[3,72,1152]{2,1,0:T(8,128)(2,1)} %bitcast.11.rest_0_), channel_id=1, source_target_pairs={{0,2},{1,3},{2,0},{3,1},{4,6},{5,7},{6,4},{7,5},{8,10},{9,11},{10,... | collective-permute-start | bytes 1493000 | tf_op jit(solution)/shard_map/ppermute | solution.py:257
  7.9 2.1 %pack.1.own_ref = f32[16,32,128]{2,1,0:T(8,128)} custom-call(s32[2]{0:T(128)} %levels_ref.1, f32[2,16,64]{2,1,0:T(8,128)} %bitcast.51, f32[16,1152]{1,0:T(8,128)} %embed_ref.5, f32[32,8,72]{2,1,0:T(8,128)} %table_ref.1), custom_call_target="tpu_custom_call" | custom-call | tf_op jit(solution)/shard_map/pack/pallas_call | solution.py:307
  10.0 5.9 %all-to-all-start = ((f32[16,32,128]{2,1,0:T(8,128)}), f32[16,32,128]{2,1,0:T(8,128)}, u32[]{:S(2)}, u32[]{:S(2)}) async-start(f32[16,32,128]{2,1,0:T(8,128)} %pack.1.own_ref), calls=%async_computation | async-start | bytes 524288 | tf_op jit(solution)/shard_map/all_to_all | solution.py:314
  16.8 3.2 %collective-permute-start.13 = (bf16[3,72,1152]{2,1,0:T(8,128)(2,1)}, bf16[3,72,1152]{2,1,0:T(8,128)(2,1)}, u32[]{:S(2)}, u32[]{:S(2)}) collective-permute-start(bf16[3,72,1152]{2,1,0:T(8,128)(2,1)} %bitcast.11.rest_0_), channel_id=1, source_target_pairs={{0,12},{1,13},{2,14},{3,15},{4,0},{5,1},{6,2},{7,3},{8,4},{9,5},{1... | collective-permute-start | bytes 1493000 | tf_op jit(solution)/shard_map/ppermute | solution.py:257
  20.0 3.1 %collective-permute-start.21 = (bf16[72,1152]{1,0:T(8,128)(2,1)S(1)}, bf16[72,1152]{1,0:T(8,128)(2,1)S(1)}, u32[]{:S(2)}, u32[]{:S(2)}) collective-permute-start(bf16[72,1152]{1,0:T(8,128)(2,1)S(1)} %bitcast.59), channel_id=1, source_target_pairs={{0,2},{1,3},{2,0},{3,1},{4,6},{5,7},{6,4},{7,5},{8,10},{9,11},{10,... | collective-permute-start | bytes 497672 | tf_op jit(solution)/shard_map/ppermute | solution.py:257
  23.2 4.4 %collective-permute-done.21 = bf16[72,1152]{1,0:T(8,128)(2,1)S(1)} collective-permute-done((bf16[72,1152]{1,0:T(8,128)(2,1)S(1)}, bf16[72,1152]{1,0:T(8,128)(2,1)S(1)}, u32[]{:S(2)}, u32[]{:S(2)}) %collective-permute-start.21) | collective-permute-done | bytes 165920 | tf_op jit(solution)/shard_map/ppermute | solution.py:257
  27.7 1.8 %collective-permute-start.23 = (bf16[72,1152]{1,0:T(8,128)(2,1)S(1)}, bf16[72,1152]{1,0:T(8,128)(2,1)S(1)}, u32[]{:S(2)}, u32[]{:S(2)}) collective-permute-start(bf16[72,1152]{1,0:T(8,128)(2,1)S(1)} %bitcast.61), channel_id=1, source_target_pairs={{0,12},{1,13},{2,14},{3,15},{4,0},{5,1},{6,2},{7,3},{8,4},{9,5},{1... | collective-permute-start | bytes 497672 | tf_op jit(solution)/shard_map/ppermute | solution.py:257
  30.2 5.8 %collective-permute-done.23 = bf16[72,1152]{1,0:T(8,128)(2,1)S(1)} collective-permute-done((bf16[72,1152]{1,0:T(8,128)(2,1)S(1)}, bf16[72,1152]{1,0:T(8,128)(2,1)S(1)}, u32[]{:S(2)}, u32[]{:S(2)}) %collective-permute-start.23) | collective-permute-done | bytes 165920 | tf_op jit(solution)/shard_map/ppermute | solution.py:257
  36.0 3.5 %collective-permute-start.4 = (bf16[72,1152]{1,0:T(8,128)(2,1)S(1)}, bf16[72,1152]{1,0:T(8,128)(2,1)S(1)}, u32[]{:S(2)}, u32[]{:S(2)}) collective-permute-start(bf16[72,1152]{1,0:T(8,128)(2,1)S(1)} %collective-permute-done), channel_id=1, source_target_pairs={{0,12},{1,13},{2,14},{3,15},{4,0},{5,1},{6,2},{7,3},{8,4},{9,5},{1... | collective-permute-start | bytes 497672 | tf_op jit(solution)/shard_map/ppermute | solution.py:257
  39.7 3.4 %collective-permute-done.4 = bf16[72,1152]{1,0:T(8,128)(2,1)S(1)} collective-permute-done((bf16[72,1152]{1,0:T(8,128)(2,1)S(1)}, bf16[72,1152]{1,0:T(8,128)(2,1)S(1)}, u32[]{:S(2)}, u32[]{:S(2)}) %collective-permute-start.4) | collective-permute-done | bytes 165920 | tf_op jit(solution)/shard_map/ppermute | solution.py:257
  43.4 3.2 %collective-permute-done.5 = bf16[72,1152]{1,0:T(8,128)(2,1)S(1)} collective-permute-done((bf16[72,1152]{1,0:T(8,128)(2,1)S(1)}, bf16[72,1152]{1,0:T(8,128)(2,1)S(1)}, u32[]{:S(2)}, u32[]{:S(2)}) %collective-permute-start.5) | collective-permute-done | bytes 165920 | tf_op jit(solution)/shard_map/ppermute | solution.py:257
  46.8 3.3 %collective-permute-done.24 = bf16[72,1152]{1,0:T(8,128)(2,1)S(1)} collective-permute-done((bf16[72,1152]{1,0:T(8,128)(2,1)S(1)}, bf16[72,1152]{1,0:T(8,128)(2,1)S(1)}, u32[]{:S(2)}, u32[]{:S(2)}) %collective-permute-start.24) | collective-permute-done | bytes 165920 | tf_op jit(solution)/shard_map/ppermute | solution.py:257
  50.1 1.8 %collective-permute-done.25 = bf16[72,1152]{1,0:T(8,128)(2,1)S(1)} collective-permute-done((bf16[72,1152]{1,0:T(8,128)(2,1)S(1)}, bf16[72,1152]{1,0:T(8,128)(2,1)S(1)}, u32[]{:S(2)}, u32[]{:S(2)}) %collective-permute-start.25) | collective-permute-done | bytes 165920 | tf_op jit(solution)/shard_map/ppermute | solution.py:257
  51.9 1.7 %collective-permute-start.6 = (bf16[72,1152]{1,0:T(8,128)(2,1)S(1)}, bf16[72,1152]{1,0:T(8,128)(2,1)S(1)}, u32[]{:S(2)}, u32[]{:S(2)}) collective-permute-start(bf16[72,1152]{1,0:T(8,128)(2,1)S(1)} %collective-permute-done.4), channel_id=1, source_target_pairs={{0,12},{1,13},{2,14},{3,15},{4,0},{5,1},{6,2},{7,3},{8,4},{9,5},{1... | collective-permute-start | bytes 497672 | tf_op jit(solution)/shard_map/ppermute | solution.py:257
  53.7 3.0 %collective-permute-done.26 = bf16[72,1152]{1,0:T(8,128)(2,1)S(1)} collective-permute-done((bf16[72,1152]{1,0:T(8,128)(2,1)S(1)}, bf16[72,1152]{1,0:T(8,128)(2,1)S(1)}, u32[]{:S(2)}, u32[]{:S(2)}) %collective-permute-start.26) | collective-permute-done | bytes 165920 | tf_op jit(solution)/shard_map/ppermute | solution.py:257
  58.1 3.9 %collective-permute-done.27 = bf16[72,1152]{1,0:T(8,128)(2,1)S(1)} collective-permute-done((bf16[72,1152]{1,0:T(8,128)(2,1)S(1)}, bf16[72,1152]{1,0:T(8,128)(2,1)S(1)}, u32[]{:S(2)}, u32[]{:S(2)}) %collective-permute-start.27) | collective-permute-done | bytes 165920 | tf_op jit(solution)/shard_map/ppermute | solution.py:257
  62.1 2.0 %collective-permute-start.15 = (bf16[3,72,1152]{2,1,0:T(8,128)(2,1)}, bf16[3,72,1152]{2,1,0:T(8,128)(2,1)S(1)}, u32[]{:S(2)}, u32[]{:S(2)}) collective-permute-start(bf16[3,72,1152]{2,1,0:T(8,128)(2,1)} %collective-permute-done.11.rest_1_), channel_id=1, source_target_pairs={{0,12},{1,13},{2,14},{3,15},{4,0},{5,1},{6,2},{7,3},{8,4},{9,5},{1... | collective-permute-start | bytes 1493000 | tf_op jit(solution)/shard_map/ppermute | solution.py:257
  64.2 3.3 %copy-done.4 = bf16[1152,3,1152]{2,0,1:T(8,128)(2,1)S(1)} copy-done((bf16[1152,3,1152]{2,0,1:T(8,128)(2,1)S(1)}, bf16[1152,3,1152]{2,0,1:T(8,128)(2,1)}, u32[]{:S(2)}) %copy-start.4) | copy-done | bytes 7962648
  67.4 10.4 %spatial.1 = (bf16[128,1152]{1,0:T(8,128)(2,1)S(1)}, f32[16,1152]{1,0:T(8,128)S(1)}) custom-call(f32[16,32,128]{2,1,0:T(8,128)S(1)} %copy-done, f32[16,32,128]{2,1,0:T(8,128)} %all-to-all-done.all_ref, f32[16,1152]{1,0:T(8,128)S(1)} %copy-done.1, bf16[3,1152,1152]{2,1,0:T(8,128)(2,1)S(1)} %bitcast.55), custom_call_target="tpu_custom_call" | custom-call | flops 10000000000 | bytes 10000000 | tf_op jit(solution)/shard_map/spatial/pallas_call | solution.py:321
  77.8 3.9 %hidden.1 = (f32[1152,128]{1,0:T(8,128)S(1)}, bf16[1152,128]{1,0:T(8,128)(2,1)S(1)}) custom-call(bf16[128,1152]{1,0:T(8,128)(2,1)S(1)} %get-tuple-element.14.mix_ref, f32[2,16,64]{2,1,0:T(8,128)S(1)} %bitcast.52, f32[16,1152]{1,0:T(8,128)S(1)} %copy-done.1, f32[16,1152]{1,0:T(8,128)S(1)} %get-tuple-element.15.mod_ref, ...), custom_call_target="tpu_custom_call" | custom-call | tf_op jit(solution)/shard_map/hidden/pallas_call | solution.py:339
  81.7 8.6 %collective-permute-start.9 = (bf16[1152,128]{1,0:T(8,128)(2,1)S(1)}, bf16[1152,128]{1,0:T(8,128)(2,1)S(1)}, u32[]{:S(2)}, u32[]{:S(2)}) collective-permute-start(bf16[1152,128]{1,0:T(8,128)(2,1)S(1)} %get-tuple-element.16.own_ref), channel_id=1, source_target_pairs={{16,0},{32,16},{48,32},{64,48},{80,64},{96,80},{112,96},{128,112},... | collective-permute-start | bytes 884744 | tf_op jit(solution)/shard_map/ppermute | solution.py:277
  91.0 5.9 %collective-permute-done.9.own_next_ref = bf16[1152,128]{1,0:T(8,128)(2,1)S(1)} collective-permute-done((bf16[1152,128]{1,0:T(8,128)(2,1)S(1)}, bf16[1152,128]{1,0:T(8,128)(2,1)S(1)}, u32[]{:S(2)}, u32[]{:S(2)}) %collective-permute-start.9) | collective-permute-done | bytes 294944 | tf_op jit(solution)/shard_map/ppermute | solution.py:277
  98.8 3.7 %temporal_0.1 = (f32[288,128]{1,0:T(8,128)S(1)}, f32[288,128]{1,0:T(8,128)S(1)}) custom-call(s32[1]{0:T(128)S(6)} %copy.27.advance_ref, bf16[1152,128]{1,0:T(8,128)(2,1)S(1)} %get-tuple-element.16.own_ref, bf16[1152,128]{1,0:T(8,128)(2,1)S(1)} %collective-permute-done.8.peer_ref, bf16[1152,128]{1,0:T(8,128)(2,1)S(1)} %collective-permute-done.9.own_next_ref, ...), custom_call_target="tpu_custom_call" | custom-call | tf_op jit(solution)/shard_map/temporal_0/pallas_call | solution.py:358
  102.8 3.6 %collective-permute-done.14.rest_0_ = bf16[3,72,1152]{2,1,0:T(8,128)(2,1)S(1)} collective-permute-done((bf16[3,72,1152]{2,1,0:T(8,128)(2,1)}, bf16[3,72,1152]{2,1,0:T(8,128)(2,1)S(1)}, u32[]{:S(2)}, u32[]{:S(2)}) %collective-permute-start.14) | collective-permute-done | bytes 497696 | tf_op jit(solution)/shard_map/ppermute | solution.py:257
  107.8 8.5 %collective-permute-done.16.rest_0_ = bf16[3,72,1152]{2,1,0:T(8,128)(2,1)S(1)} collective-permute-done((bf16[3,72,1152]{2,1,0:T(8,128)(2,1)}, bf16[3,72,1152]{2,1,0:T(8,128)(2,1)S(1)}, u32[]{:S(2)}, u32[]{:S(2)}) %collective-permute-start.16) | collective-permute-done | bytes 497696 | tf_op jit(solution)/shard_map/ppermute | solution.py:257
  116.3 1.3 temporal_6.1
  119.0 3.9 %final.1 = (f32[2,16,64]{2,1,0:T(8,128)}, f32[2,16,64]{2,1,0:T(8,128)S(1)}) custom-call(f32[576,128]{1,0:T(8,128)S(1)} %pad_maximum_fusion.own_ref, bf16[576,128]{1,0:T(8,128)(2,1)S(1)} %pad_maximum_fusion.1.peer_ref, f32[1152,128]{1,0:T(8,128)S(1)} %get-tuple-element.23.hidden_ref, f32[2,16,64]{2,1,0:T(8,128)S(1)} %bitcast.53, ...), custom_call_target="tpu_custom_call" | custom-call | tf_op jit(solution)/shard_map/final/pallas_call | solution.py:372
  122.8 2.9 %collective-permute-start.29 = (f32[16,64]{1,0:T(8,128)S(1)}, f32[16,64]{1,0:T(8,128)S(1)}, u32[]{:S(2)}, u32[]{:S(2)}) collective-permute-start(f32[16,64]{1,0:T(8,128)S(1)} %get-tuple-element.27), channel_id=1, source_target_pairs={{16,0},{32,16},{48,32},{64,48},{80,64},{96,80},{112,96},{128,112},... | collective-permute-start | bytes 12296 | tf_op jit(solution)/shard_map/ppermute | solution.py:277
  125.8 2.6 %collective-permute-done.29 = f32[16,64]{1,0:T(8,128)S(1)} collective-permute-done((f32[16,64]{1,0:T(8,128)S(1)}, f32[16,64]{1,0:T(8,128)S(1)}, u32[]{:S(2)}, u32[]{:S(2)}) %collective-permute-start.29) | collective-permute-done | bytes 4128 | tf_op jit(solution)/shard_map/ppermute | solution.py:277
  (75 shorter events, 9.9 us)
Async XLA Ops:
  0.6 16.2 %collective-permute-start = (bf16[72,1152]{1,0:T(8,128)(2,1)}, bf16[72,1152]{1,0:T(8,128)(2,1)S(1)}, u32[]{:S(2)}, u32[]{:S(2)}) collective-permute-start(bf16[72,1152]{1,0:T(8,128)(2,1)} %bitcast.56), channel_id=1, source_target_pairs={{0,2},{1,3},{2,0},{3,1},{4,6},{5,7},{6,4},{7,5},{8,10},{9,11},{10,... | collective-permute-start | bytes 497672 | tf_op jit(solution)/shard_map/ppermute | solution.py:257
  2.9 17.2 %collective-permute-start.1 = (bf16[72,1152]{1,0:T(8,128)(2,1)}, bf16[72,1152]{1,0:T(8,128)(2,1)S(1)}, u32[]{:S(2)}, u32[]{:S(2)}) collective-permute-start(bf16[72,1152]{1,0:T(8,128)(2,1)} %bitcast.57), channel_id=1, source_target_pairs={{0,4},{1,5},{2,6},{3,7},{4,8},{5,9},{6,10},{7,11},{8,12},{9,13},{1... | collective-permute-start | bytes 497672 | tf_op jit(solution)/shard_map/ppermute | solution.py:257
  4.4 18.7 %collective-permute-start.2 = (bf16[72,1152]{1,0:T(8,128)(2,1)}, bf16[72,1152]{1,0:T(8,128)(2,1)S(1)}, u32[]{:S(2)}, u32[]{:S(2)}) collective-permute-start(bf16[72,1152]{1,0:T(8,128)(2,1)} %bitcast.58), channel_id=1, source_target_pairs={{0,12},{1,13},{2,14},{3,15},{4,0},{5,1},{6,2},{7,3},{8,4},{9,5},{1... | collective-permute-start | bytes 497672 | tf_op jit(solution)/shard_map/ppermute | solution.py:257
  6.1 56.0 %collective-permute-start.11 = (bf16[3,72,1152]{2,1,0:T(8,128)(2,1)}, bf16[3,72,1152]{2,1,0:T(8,128)(2,1)}, u32[]{:S(2)}, u32[]{:S(2)}) collective-permute-start(bf16[3,72,1152]{2,1,0:T(8,128)(2,1)} %bitcast.11.rest_0_), channel_id=1, source_target_pairs={{0,2},{1,3},{2,0},{3,1},{4,6},{5,7},{6,4},{7,5},{8,10},{9,11},{10,... | collective-permute-start | bytes 1493000 | tf_op jit(solution)/shard_map/ppermute | solution.py:257
  7.5 82.9 %collective-permute-start.12 = (bf16[3,72,1152]{2,1,0:T(8,128)(2,1)}, bf16[3,72,1152]{2,1,0:T(8,128)(2,1)}, u32[]{:S(2)}, u32[]{:S(2)}) collective-permute-start(bf16[3,72,1152]{2,1,0:T(8,128)(2,1)} %bitcast.11.rest_0_), channel_id=1, source_target_pairs={{0,4},{1,5},{2,6},{3,7},{4,8},{5,9},{6,10},{7,11},{8,12},{9,13},{1... | collective-permute-start | bytes 1493000 | tf_op jit(solution)/shard_map/ppermute | solution.py:257
  10.0 54.2 %all-to-all-start = ((f32[16,32,128]{2,1,0:T(8,128)}), f32[16,32,128]{2,1,0:T(8,128)}, u32[]{:S(2)}, u32[]{:S(2)}) async-start(f32[16,32,128]{2,1,0:T(8,128)} %pack.1.own_ref), calls=%async_computation | async-start | bytes 524288 | tf_op jit(solution)/shard_map/all_to_all | solution.py:314
  16.8 73.6 %collective-permute-start.13 = (bf16[3,72,1152]{2,1,0:T(8,128)(2,1)}, bf16[3,72,1152]{2,1,0:T(8,128)(2,1)}, u32[]{:S(2)}, u32[]{:S(2)}) collective-permute-start(bf16[3,72,1152]{2,1,0:T(8,128)(2,1)} %bitcast.11.rest_0_), channel_id=1, source_target_pairs={{0,12},{1,13},{2,14},{3,15},{4,0},{5,1},{6,2},{7,3},{8,4},{9,5},{1... | collective-permute-start | bytes 1493000 | tf_op jit(solution)/shard_map/ppermute | solution.py:257
  20.0 7.6 %collective-permute-start.21 = (bf16[72,1152]{1,0:T(8,128)(2,1)S(1)}, bf16[72,1152]{1,0:T(8,128)(2,1)S(1)}, u32[]{:S(2)}, u32[]{:S(2)}) collective-permute-start(bf16[72,1152]{1,0:T(8,128)(2,1)S(1)} %bitcast.59), channel_id=1, source_target_pairs={{0,2},{1,3},{2,0},{3,1},{4,6},{5,7},{6,4},{7,5},{8,10},{9,11},{10,... | collective-permute-start | bytes 497672 | tf_op jit(solution)/shard_map/ppermute | solution.py:257
  23.1 7.0 %collective-permute-start.22 = (bf16[72,1152]{1,0:T(8,128)(2,1)S(1)}, bf16[72,1152]{1,0:T(8,128)(2,1)S(1)}, u32[]{:S(2)}, u32[]{:S(2)}) collective-permute-start(bf16[72,1152]{1,0:T(8,128)(2,1)S(1)} %bitcast.60), channel_id=1, source_target_pairs={{0,4},{1,5},{2,6},{3,7},{4,8},{5,9},{6,10},{7,11},{8,12},{9,13},{1... | collective-permute-start | bytes 497672 | tf_op jit(solution)/shard_map/ppermute | solution.py:257
  27.7 8.3 %collective-permute-start.23 = (bf16[72,1152]{1,0:T(8,128)(2,1)S(1)}, bf16[72,1152]{1,0:T(8,128)(2,1)S(1)}, u32[]{:S(2)}, u32[]{:S(2)}) collective-permute-start(bf16[72,1152]{1,0:T(8,128)(2,1)S(1)} %bitcast.61), channel_id=1, source_target_pairs={{0,12},{1,13},{2,14},{3,15},{4,0},{5,1},{6,2},{7,3},{8,4},{9,5},{1... | collective-permute-start | bytes 497672 | tf_op jit(solution)/shard_map/ppermute | solution.py:257
  30.2 9.4 %collective-permute-start.3 = (bf16[72,1152]{1,0:T(8,128)(2,1)S(1)}, bf16[72,1152]{1,0:T(8,128)(2,1)S(1)}, u32[]{:S(2)}, u32[]{:S(2)}) collective-permute-start(bf16[72,1152]{1,0:T(8,128)(2,1)S(1)} %collective-permute-done), channel_id=1, source_target_pairs={{0,4},{1,5},{2,6},{3,7},{4,8},{5,9},{6,10},{7,11},{8,12},{9,13},{1... | collective-permute-start | bytes 497672 | tf_op jit(solution)/shard_map/ppermute | solution.py:257
  36.0 7.0 %collective-permute-start.4 = (bf16[72,1152]{1,0:T(8,128)(2,1)S(1)}, bf16[72,1152]{1,0:T(8,128)(2,1)S(1)}, u32[]{:S(2)}, u32[]{:S(2)}) collective-permute-start(bf16[72,1152]{1,0:T(8,128)(2,1)S(1)} %collective-permute-done), channel_id=1, source_target_pairs={{0,12},{1,13},{2,14},{3,15},{4,0},{5,1},{6,2},{7,3},{8,4},{9,5},{1... | collective-permute-start | bytes 497672 | tf_op jit(solution)/shard_map/ppermute | solution.py:257
  39.5 24.7 %copy-start = (f32[16,32,128]{2,1,0:T(8,128)S(1)}, f32[16,32,128]{2,1,0:T(8,128)}, u32[]{:S(2)}) copy-start(f32[16,32,128]{2,1,0:T(8,128)} %pack.1.own_ref) | copy-start | bytes 786436
  39.5 7.0 %collective-permute-start.5 = (bf16[72,1152]{1,0:T(8,128)(2,1)S(1)}, bf16[72,1152]{1,0:T(8,128)(2,1)S(1)}, u32[]{:S(2)}, u32[]{:S(2)}) collective-permute-start(bf16[72,1152]{1,0:T(8,128)(2,1)S(1)} %collective-permute-done.1), channel_id=1, source_target_pairs={{0,4},{1,5},{2,6},{3,7},{4,8},{5,9},{6,10},{7,11},{8,12},{9,13},{1... | collective-permute-start | bytes 497672 | tf_op jit(solution)/shard_map/ppermute | solution.py:257
  43.0 7.1 %collective-permute-start.24 = (bf16[72,1152]{1,0:T(8,128)(2,1)S(1)}, bf16[72,1152]{1,0:T(8,128)(2,1)S(1)}, u32[]{:S(2)}, u32[]{:S(2)}) collective-permute-start(bf16[72,1152]{1,0:T(8,128)(2,1)S(1)} %collective-permute-done.21), channel_id=1, source_target_pairs={{0,4},{1,5},{2,6},{3,7},{4,8},{5,9},{6,10},{7,11},{8,12},{9,13},{1... | collective-permute-start | bytes 497672 | tf_op jit(solution)/shard_map/ppermute | solution.py:257
  46.6 5.3 %collective-permute-start.25 = (bf16[72,1152]{1,0:T(8,128)(2,1)S(1)}, bf16[72,1152]{1,0:T(8,128)(2,1)S(1)}, u32[]{:S(2)}, u32[]{:S(2)}) collective-permute-start(bf16[72,1152]{1,0:T(8,128)(2,1)S(1)} %collective-permute-done.21), channel_id=1, source_target_pairs={{0,12},{1,13},{2,14},{3,15},{4,0},{5,1},{6,2},{7,3},{8,4},{9,5},{1... | collective-permute-start | bytes 497672 | tf_op jit(solution)/shard_map/ppermute | solution.py:257
  50.1 6.6 %collective-permute-start.26 = (bf16[72,1152]{1,0:T(8,128)(2,1)S(1)}, bf16[72,1152]{1,0:T(8,128)(2,1)S(1)}, u32[]{:S(2)}, u32[]{:S(2)}) collective-permute-start(bf16[72,1152]{1,0:T(8,128)(2,1)S(1)} %collective-permute-done.22), channel_id=1, source_target_pairs={{0,4},{1,5},{2,6},{3,7},{4,8},{5,9},{6,10},{7,11},{8,12},{9,13},{1... | collective-permute-start | bytes 497672 | tf_op jit(solution)/shard_map/ppermute | solution.py:257
  51.9 6.1 %collective-permute-start.6 = (bf16[72,1152]{1,0:T(8,128)(2,1)S(1)}, bf16[72,1152]{1,0:T(8,128)(2,1)S(1)}, u32[]{:S(2)}, u32[]{:S(2)}) collective-permute-start(bf16[72,1152]{1,0:T(8,128)(2,1)S(1)} %collective-permute-done.4), channel_id=1, source_target_pairs={{0,12},{1,13},{2,14},{3,15},{4,0},{5,1},{6,2},{7,3},{8,4},{9,5},{1... | collective-permute-start | bytes 497672 | tf_op jit(solution)/shard_map/ppermute | solution.py:257
  56.7 5.3 %collective-permute-start.27 = (bf16[72,1152]{1,0:T(8,128)(2,1)S(1)}, bf16[72,1152]{1,0:T(8,128)(2,1)S(1)}, u32[]{:S(2)}, u32[]{:S(2)}) collective-permute-start(bf16[72,1152]{1,0:T(8,128)(2,1)S(1)} %collective-permute-done.25), channel_id=1, source_target_pairs={{0,12},{1,13},{2,14},{3,15},{4,0},{5,1},{6,2},{7,3},{8,4},{9,5},{1... | collective-permute-start | bytes 497672 | tf_op jit(solution)/shard_map/ppermute | solution.py:257
  58.0 19.8 %collective-permute-start.7 = (bf16[8,72,1152]{2,1,0:T(8,128)(2,1)S(1)}, bf16[8,72,1152]{2,1,0:T(8,128)(2,1)}, u32[]{:S(2)}, u32[]{:S(2)}) collective-permute-start(bf16[8,72,1152]{2,1,0:T(8,128)(2,1)S(1)} %bitcast_dynamic-update-slice_fusion.9.rest_0_), channel_id=1, source_target_pairs={{0,1},{1,0},{2,3},{3,2},{4,5},{5,4},{6,7},{7,6},{8,9},{9,8},{10,11... | collective-permute-start | bytes 3981320 | tf_op jit(solution)/shard_map/ppermute | solution.py:257
  62.0 56.9 %collective-permute-start.28 = (bf16[8,72,1152]{2,1,0:T(8,128)(2,1)S(1)}, bf16[8,72,1152]{2,1,0:T(8,128)(2,1)}, u32[]{:S(2)}, u32[]{:S(2)}) collective-permute-start(bf16[8,72,1152]{2,1,0:T(8,128)(2,1)S(1)} %bitcast_dynamic-update-slice_fusion.2.rest_0_), channel_id=1, source_target_pairs={{0,1},{1,0},{2,3},{3,2},{4,5},{5,4},{6,7},{7,6},{8,9},{9,8},{10,11... | collective-permute-start | bytes 3981320 | tf_op jit(solution)/shard_map/ppermute | solution.py:257
  62.1 28.7 %collective-permute-start.15 = (bf16[3,72,1152]{2,1,0:T(8,128)(2,1)}, bf16[3,72,1152]{2,1,0:T(8,128)(2,1)S(1)}, u32[]{:S(2)}, u32[]{:S(2)}) collective-permute-start(bf16[3,72,1152]{2,1,0:T(8,128)(2,1)} %collective-permute-done.11.rest_1_), channel_id=1, source_target_pairs={{0,12},{1,13},{2,14},{3,15},{4,0},{5,1},{6,2},{7,3},{8,4},{9,5},{1... | collective-permute-start | bytes 1493000 | tf_op jit(solution)/shard_map/ppermute | solution.py:257
  81.7 15.2 %collective-permute-start.9 = (bf16[1152,128]{1,0:T(8,128)(2,1)S(1)}, bf16[1152,128]{1,0:T(8,128)(2,1)S(1)}, u32[]{:S(2)}, u32[]{:S(2)}) collective-permute-start(bf16[1152,128]{1,0:T(8,128)(2,1)S(1)} %get-tuple-element.16.own_ref), channel_id=1, source_target_pairs={{16,0},{32,16},{48,32},{64,48},{80,64},{96,80},{112,96},{128,112},... | collective-permute-start | bytes 884744 | tf_op jit(solution)/shard_map/ppermute | solution.py:277
  90.4 6.8 %collective-permute-start.8 = (bf16[1152,128]{1,0:T(8,128)(2,1)S(1)}, bf16[1152,128]{1,0:T(8,128)(2,1)S(1)}, u32[]{:S(2)}, u32[]{:S(2)}) collective-permute-start(bf16[1152,128]{1,0:T(8,128)(2,1)S(1)} %get-tuple-element.16.own_ref), channel_id=1, source_target_pairs={{0,1},{1,0},{2,3},{3,2},{4,5},{5,4},{6,7},{7,6},{8,9},{9,8},{10,11... | collective-permute-start | bytes 884744 | tf_op jit(solution)/shard_map/ppermute | solution.py:257
  90.5 15.9 %collective-permute-start.14 = (bf16[3,72,1152]{2,1,0:T(8,128)(2,1)}, bf16[3,72,1152]{2,1,0:T(8,128)(2,1)S(1)}, u32[]{:S(2)}, u32[]{:S(2)}) collective-permute-start(bf16[3,72,1152]{2,1,0:T(8,128)(2,1)} %collective-permute-done.11.rest_1_), channel_id=1, source_target_pairs={{0,4},{1,5},{2,6},{3,7},{4,8},{5,9},{6,10},{7,11},{8,12},{9,13},{1... | collective-permute-start | bytes 1493000 | tf_op jit(solution)/shard_map/ppermute | solution.py:257
  90.9 25.4 %collective-permute-start.16 = (bf16[3,72,1152]{2,1,0:T(8,128)(2,1)}, bf16[3,72,1152]{2,1,0:T(8,128)(2,1)S(1)}, u32[]{:S(2)}, u32[]{:S(2)}) collective-permute-start(bf16[3,72,1152]{2,1,0:T(8,128)(2,1)} %collective-permute-done.12.rest_2_), channel_id=1, source_target_pairs={{0,4},{1,5},{2,6},{3,7},{4,8},{5,9},{6,10},{7,11},{8,12},{9,13},{1... | collective-permute-start | bytes 1493000 | tf_op jit(solution)/shard_map/ppermute | solution.py:257
  96.9 19.4 %collective-permute-start.17 = (bf16[3,72,1152]{2,1,0:T(8,128)(2,1)S(1)}, bf16[3,72,1152]{2,1,0:T(8,128)(2,1)S(1)}, u32[]{:S(2)}, u32[]{:S(2)}) collective-permute-start(bf16[3,72,1152]{2,1,0:T(8,128)(2,1)S(1)} %collective-permute-done.15.rest_1_), channel_id=1, source_target_pairs={{0,12},{1,13},{2,14},{3,15},{4,0},{5,1},{6,2},{7,3},{8,4},{9,5},{1... | collective-permute-start | bytes 1493000 | tf_op jit(solution)/shard_map/ppermute | solution.py:257
  97.2 1.6 %collective-permute-start.10 = (bf16[1152,128]{1,0:T(8,128)(2,1)S(1)}, bf16[1152,128]{1,0:T(8,128)(2,1)S(1)}, u32[]{:S(2)}, u32[]{:S(2)}) collective-permute-start(bf16[1152,128]{1,0:T(8,128)(2,1)S(1)} %collective-permute-done.9.own_next_ref), channel_id=1, source_target_pairs={{0,1},{1,0},{2,3},{3,2},{4,5},{5,4},{6,7},{7,6},{8,9},{9,8},{10,11... | collective-permute-start | bytes 884744 | tf_op jit(solution)/shard_map/ppermute | solution.py:257
  102.6 16.4 %collective-permute-start.18 = (bf16[288,128]{1,0:T(8,128)(2,1)S(1)}, bf16[288,128]{1,0:T(8,128)(2,1)S(1)}, u32[]{:S(2)}, u32[]{:S(2)}) collective-permute-start(bf16[288,128]{1,0:T(8,128)(2,1)S(1)} %convert_element_type.9), channel_id=1, source_target_pairs={{0,1},{1,0},{2,3},{3,2},{4,5},{5,4},{6,7},{7,6},{8,9},{9,8},{10,11... | collective-permute-start | bytes 221192 | tf_op jit(solution)/shard_map/ppermute | solution.py:257
  107.7 10.1 %collective-permute-start.19 = (bf16[144,128]{1,0:T(8,128)(2,1)S(1)}, bf16[144,128]{1,0:T(8,128)(2,1)S(1)}, u32[]{:S(2)}, u32[]{:S(2)}) collective-permute-start(bf16[144,128]{1,0:T(8,128)(2,1)S(1)} %convert_element_type.10), channel_id=1, source_target_pairs={{0,1},{1,0},{2,3},{3,2},{4,5},{5,4},{6,7},{7,6},{8,9},{9,8},{10,11... | collective-permute-start | bytes 110600 | tf_op jit(solution)/shard_map/ppermute | solution.py:257
  117.6 1.3 %collective-permute-start.20 = (bf16[144,128]{1,0:T(8,128)(2,1)S(1)}, bf16[144,128]{1,0:T(8,128)(2,1)S(1)}, u32[]{:S(2)}, u32[]{:S(2)}) collective-permute-start(bf16[144,128]{1,0:T(8,128)(2,1)S(1)} %convert_element_type.11), channel_id=1, source_target_pairs={{0,1},{1,0},{2,3},{3,2},{4,5},{5,4},{6,7},{7,6},{8,9},{9,8},{10,11... | collective-permute-start | bytes 110600 | tf_op jit(solution)/shard_map/ppermute | solution.py:257
  122.8 5.5 %collective-permute-start.29 = (f32[16,64]{1,0:T(8,128)S(1)}, f32[16,64]{1,0:T(8,128)S(1)}, u32[]{:S(2)}, u32[]{:S(2)}) collective-permute-start(f32[16,64]{1,0:T(8,128)S(1)} %get-tuple-element.27), channel_id=1, source_target_pairs={{16,0},{32,16},{48,32},{64,48},{80,64},{96,80},{112,96},{128,112},... | collective-permute-start | bytes 12296 | tf_op jit(solution)/shard_map/ppermute | solution.py:277
  (6 other events, 75.2 us)

commit v2 on v1

v2 whole, which is shorter than its diff:
```python
import functools
import math

import jax
import jax.numpy as jnp
from jax import lax
from jax.experimental import pallas as pl
from jax.experimental.pallas import tpu as pltpu
from jax.sharding import PartitionSpec as P

HEADS = 16
HD = 72
D = HEADS * HD
C = 16
CP = 32
BF = jnp.bfloat16
F32 = jnp.float32
VMEM = pl.BlockSpec(memory_space=pltpu.VMEM)
SMEM = pl.BlockSpec(memory_space=pltpu.SMEM)
ANY = pl.BlockSpec(memory_space=pl.ANY)


def split(value):
    high = value.astype(BF)
    return high, (value - high.astype(F32)).astype(BF)


def dot_tn(a, b):
    return lax.dot_general(a, b, (((0,), (0,)), ((), ())), preferred_element_type=F32)


def dot_nt(a, b):
    return lax.dot_general(a, b, (((1,), (1,)), ((), ())), preferred_element_type=F32)


def dot_nn(a, b):
    return jnp.dot(a, b, preferred_element_type=F32)


def product_tn(a, b):
    a_high, a_low = split(a)
    b_high, b_low = split(b)
    return dot_tn(
        jnp.concatenate([a_high, a_low, a_high], axis=0),
        jnp.concatenate([b_high, b_high, b_low], axis=0),
    )


def both_frames(latents_ref):
    return jnp.concatenate([latents_ref[0], latents_ref[1]], axis=1)


def normalize(hidden):
    width = hidden.shape[0]
    mean_value = jnp.sum(hidden, axis=0, keepdims=True) * (1.0 / width)
    centered = hidden - mean_value
    variance = jnp.sum(centered * centered, axis=0, keepdims=True) * (1.0 / width)
    return centered * lax.rsqrt(variance + 1e-06)


def modulation_columns(mod, rows):
    tokens = 128
    high, low = split(mod)
    row_at = lax.broadcasted_iota(jnp.int32, (16, tokens * len(rows)), 0)
    lane_at = lax.broadcasted_iota(jnp.int32, (16, tokens * len(rows)), 1)
    wanted = jnp.zeros_like(row_at)
    for place, row in enumerate(rows):
        wanted = jnp.where(lane_at // tokens == place, row, wanted)
    wanted = wanted + 8 * ((lane_at % tokens) // 64)
    chosen = (row_at == wanted).astype(F32).astype(BF)
    columns = dot_tn(
        jnp.concatenate([high, low], axis=0), jnp.concatenate([chosen, chosen], axis=0)
    )
    return [columns[:, tokens * i : tokens * (i + 1)] for i in range(len(rows))]


def pack_kernel(levels_ref, latents_ref, embed_ref, table_ref, out_ref):
    channels = both_frames(latents_ref)
    embed = embed_ref[...]
    centered = embed - jnp.sum(embed, axis=1, keepdims=True) * (1.0 / D)
    spread = product_tn(centered, channels)
    variance = jnp.sum(spread * spread, axis=0, keepdims=True) * (1.0 / D)
    inverse = lax.rsqrt(variance + 1e-06)
    peers = out_ref.shape[0]
    for peer in range(peers):
        out_ref[peer, 0:16, :] = channels
        out_ref[peer, 32:40, :] = jnp.broadcast_to(inverse, (8, 128))
        for frame in range(2):
            rows = table_ref[levels_ref[frame]]
            out_ref[peer, 16 + 8 * frame : 24 + 8 * frame, 0:HD] = rows


def coefficient_kernel(all_ref, embed_ref, weight_ref, coef_ref, mod_ref, tokens_ref, held_ref, sems):
    parts, rows = sems.shape[1], D // sems.shape[1]
    copies = [
        [
            pltpu.make_async_copy(
                weight_ref.at[index, pl.ds(rows * part, rows)],
                held_ref.at[index, pl.ds(rows * part, rows)],
                sems.at[index, part],
            )
            for part in range(parts)
        ]
        for index in range(3)
    ]
    for index in range(3):
        for copy in copies[index]:
            copy.start()
    peers = all_ref.shape[0]
    for peer in range(peers):
        mod_ref[:, HD * peer : HD * (peer + 1)] = all_ref[peer, 16:32, 0:HD]
        scaled = all_ref[peer, 0:16] * all_ref[peer, 32:33]
        for frame in range(2):
            tokens_ref[frame, :, 64 * peer : 64 * (peer + 1)] = scaled[:, 64 * frame : 64 * (frame + 1)]
    mod = mod_ref[...]
    embed = embed_ref[...]
    centered = embed - jnp.sum(embed, axis=1, keepdims=True) * (1.0 / D)
    row16 = lax.broadcasted_iota(jnp.int32, (16, D), 0)
    rows = []
    for frame in range(2):
        rows.append(centered * (1.0 + mod[8 * frame + 1 : 8 * frame + 2]))
        rows.append(jnp.where(row16 == 0, mod[8 * frame : 8 * frame + 1], 0.0))
    high, low = split(jnp.concatenate(rows, axis=0))
    stacked = jnp.concatenate([high, low], axis=0)
    for index in range(3):
        for copy in copies[index]:
            copy.wait()
        both = dot_nn(stacked, held_ref[index])
        for frame in range(2):
            rows = slice(CP * frame, CP * (frame + 1))
            coef_ref[frame, index] = both[rows] + both[64:128][rows]


def attend_kernel(frame, own_ref, tokens_ref, coef_ref, *refs):
    mix_ref, query_ref, part_ref = refs[-3:]
    own_head = (
        lax.broadcasted_iota(jnp.int32, (HEADS * CP, D), 0) // CP
        == lax.broadcasted_iota(jnp.int32, (HEADS * CP, D), 1) // HD
    )
    scale = math.log2(math.e) / math.sqrt(HD)
    one_row = (lax.broadcasted_iota(jnp.int32, (16, 64), 0) == 0).astype(F32)
    one_row_all = (lax.broadcasted_iota(jnp.int32, (16, 1024), 0) == 0).astype(F32)
    key_heads = jnp.where(own_head, jnp.concatenate([coef_ref[frame, 1]] * HEADS, axis=0), 0.0).astype(BF)
    pair = dot_nt(key_heads, coef_ref[frame, 0].astype(BF)) * scale
    mine = own_ref[0:16] * own_ref[32:33]
    own = jnp.concatenate([mine[:, 64 * frame : 64 * (frame + 1)], one_row], axis=0)
    own_high, own_low = split(own)
    pair_high, pair_low = split(pair)
    reduced = dot_nn(
        jnp.concatenate([pair_high, pair_low, pair_high], axis=1),
        jnp.concatenate([own_high, own_high, own_low], axis=0),
    )
    for head in range(HEADS):
        query_ref[:, 64 * head : 64 * (head + 1)] = reduced[CP * head : CP * (head + 1)]
    query_high, query_low = split(query_ref[...])
    queries = jnp.concatenate([query_high, query_low, query_high], axis=0)
    token_high, token_low = split(jnp.concatenate([tokens_ref[frame], one_row_all], axis=0))
    keys = jnp.concatenate([token_high, token_high, token_low], axis=0)
    values = jnp.concatenate([token_high, token_low[0:16]], axis=0)
    for chunk in range(4):
        scores = dot_tn(keys, queries[:, 256 * chunk : 256 * (chunk + 1)])
        top = jnp.max(scores, axis=0, keepdims=True)
        weights = jnp.exp2(scores - top).astype(BF)
        summed = dot_nn(values, weights)
        mixed = (summed[0:16] + summed[32:48]) / summed[16:17]
        for sub in range(4):
            head = 4 * chunk + sub
            part_ref[CP * head : CP * head + 16, :] = mixed[:, 64 * sub : 64 * (sub + 1)]
            part_ref[CP * head + 16 : CP * head + 32, :] = one_row
    value_heads = jnp.where(own_head, jnp.concatenate([coef_ref[frame, 2]] * HEADS, axis=0), 0.0).astype(BF)
    mix_ref[...] = dot_tn(part_ref[...].astype(BF), value_heads).astype(BF)


def lay_kernel(after_ref, source_ref, out_ref):
    out_ref[...] = source_ref[...]


def gate_kernel(after_ref, held_ref, passed_ref):
    pass


def y_order(me):
    return [me, lax.rem(me + 12, 16), lax.rem(me + 4, 16), lax.rem(me + 8, 16)]


def at_rows(index):
    return pl.ds(pl.multiple_of(index * HD, 8), HD)


def place_rows(out_ref, product, order):
    for place, index in enumerate(order):
        out_ref[at_rows(index), :] = product[HD * place : HD * (place + 1)]


def hidden_kernel(first_ref, second_ref, latents_ref, embed_ref, mod_ref, *rest):
    *blocks, hidden_ref, inner_ref, update_ref = rest
    mix = jnp.concatenate([first_ref[...], second_ref[...]], axis=0).T
    me = lax.axis_index("seq")
    for flip, block in enumerate(blocks):
        place_rows(update_ref, dot_nn(block[...], mix), y_order(me ^ flip))
    embedded = product_tn(embed_ref[...], both_frames(latents_ref))
    gate, shift, scale = modulation_columns(mod_ref[...], (2, 3, 4))
    hidden = embedded + gate * update_ref[...]
    hidden_ref[...] = hidden
    inner_ref[...] = (normalize(hidden) * (1.0 + scale) + shift).astype(BF)


def temporal_kernel(advance_ref, *refs):
    sources, outs, (held_ref, sems) = refs[:4], refs[12:16], refs[16:]
    copies = [
        pltpu.make_async_copy(source, held_ref.at[place], sems.at[place]) for place, source in enumerate(sources)
    ]
    for copy in copies:
        copy.start()
    tokens = jnp.concatenate([one[...] for one in refs[4:8]], axis=1)
    following = jnp.concatenate([one[...] for one in refs[8:12]], axis=1)
    last = lax.axis_index("queue") == lax.axis_size("queue") - 1
    limit = jnp.where(last, 0, advance_ref[0])
    frame = lax.broadcasted_iota(jnp.int32, (1, 128), 1) // 64
    keep_same = frame < limit
    keep_other = (1 - frame) < limit
    scale = math.log2(math.e) / math.sqrt(HD)
    for place, copy in enumerate(copies):
        copy.wait()
        block = held_ref[place]
        both = dot_nn(block, tokens)
        ahead = dot_nn(block[HD : 3 * HD], following)
        query, key, value = (both[HD * index : HD * (index + 1)] for index in range(3))
        key_next, value_next = ahead[0:HD], ahead[HD : 2 * HD]
        for side, out_ref in enumerate(outs):
            lanes = slice(128 * side, 128 * (side + 1))
            asked = query[:, lanes] * scale
            keys = [key[:, lanes], key_next[:, lanes]]
            values = [value[:, lanes], value_next[:, lanes]]
            keys = [keys[0], pltpu.roll(keys[0], 64, 1), keys[1], pltpu.roll(keys[1], 64, 1)]
            values = [values[0], pltpu.roll(values[0], 64, 1), values[1], pltpu.roll(values[1], 64, 1)]
            scores = [jnp.sum(asked * one, axis=0, keepdims=True) for one in keys]
            scores[2] = jnp.where(keep_same, scores[2], -1e30)
            scores[3] = jnp.where(keep_other, scores[3], -1e30)
            top = jnp.maximum(jnp.maximum(scores[0], scores[1]), jnp.maximum(scores[2], scores[3]))
            weights = [jnp.exp2(one - top) for one in scores]
            inverse = 1.0 / (weights[0] + weights[1] + weights[2] + weights[3])
            mixed = sum(w * inverse * v for w, v in zip(weights, values))
            out_ref[HD * place : HD * (place + 1), :] = mixed.astype(BF)


def final_kernel(hidden_ref, latents_ref, mod_ref, final_ref, *rest):
    mixes, blocks, (velocity_ref, updated_ref, mix_ref, update_ref) = rest[0:4], rest[4:6], rest[6:]
    me = lax.axis_index("seq")
    for flip, part in enumerate(mixes):
        place_rows(mix_ref, part[...].astype(F32), y_order(me ^ flip))
    mix = mix_ref[...].astype(BF)
    for flip, block in enumerate(blocks):
        at = lax.rem(me ^ flip, 4)
        order = [4 * place + (at ^ side) for place in range(4) for side in (0, 2)]
        place_rows(update_ref, dot_nn(block[...], mix), order)
    gate, shift, scale = modulation_columns(mod_ref[...], (5, 6, 7))
    hidden = hidden_ref[...] + gate * update_ref[...]
    inner = (normalize(hidden) * (1.0 + scale) + shift).astype(BF)
    velocity = dot_nn(final_ref[...], inner)
    for frame in range(2):
        part = velocity[:, 64 * frame : 64 * (frame + 1)]
        velocity_ref[frame] = part
        updated_ref[frame] = latents_ref[frame] - part * (1.0 / 32.0)


def params(mebibytes):
    return pltpu.CompilerParams(vmem_limit_bytes=mebibytes << 20)


def takes(microseconds):
    return pl.CostEstimate(
        flops=int(microseconds * 1.15e9), bytes_accessed=1000, transcendentals=0
    )


def along_seq(array, to):
    return lax.ppermute(array, "seq", [(i, to(i)) for i in range(16)])


def y_up(array):
    return along_seq(array, lambda i: (i + 4) % 16)


def y_down(array):
    return along_seq(array, lambda i: (i + 12) % 16)


def over_x(array):
    return along_seq(array, lambda i: i ^ 2)


def other_core(array):
    return along_seq(array, lambda i: i ^ 1)


def from_next(array):
    return lax.ppermute(array, "queue", [(i, i - 1) for i in range(1, 16)])


def over_both(array):
    return along_seq(array, lambda i: i ^ 3)


def y_far(array):
    return along_seq(array, lambda i: (i + 8) % 16)


def stack_after(after, blocks, name):
    return pl.pallas_call(
        stack_kernel,
        out_shape=jax.ShapeDtypeStruct((len(blocks), *blocks[0].shape), BF),
        in_specs=[VMEM] * (1 + len(blocks)),
        out_specs=VMEM,
        cost_estimate=takes(2),
        name=name,
    )(after, *blocks)


def gate(held, after, name):
    return pl.pallas_call(
        gate_kernel,
        out_shape=jax.ShapeDtypeStruct(held.shape, held.dtype),
        in_specs=[ANY, ANY],
        out_specs=ANY,
        input_output_aliases={1: 0},
        cost_estimate=takes(0.2),
        name=name,
    )(after, held)


def shards(
    latents,
    levels,
    advance,
    fresh_noise,
    level_mod,
    embed_w,
    spatial_qkv,
    spatial_out,
    temporal_qkv,
    temporal_out,
    final_w,
):
    lat = latents.transpose(0, 2, 1)
    spatial_w = spatial_qkv.transpose(1, 0, 2)
    out_w = spatial_out.transpose(1, 0)
    temporal_w = temporal_qkv.transpose(1, 2, 0).reshape(3 * HD, D)
    last_w = temporal_out.transpose(1, 0)
    final_t = final_w.transpose(1, 0)

    packed = pl.pallas_call(
        pack_kernel,
        out_shape=jax.ShapeDtypeStruct((16, 40, 128), F32),
        in_specs=[SMEM, VMEM, VMEM, VMEM],
        out_specs=VMEM,
        cost_estimate=takes(2),
        name="pack",
    )(levels, lat, embed_w, level_mod)
    everyone = lax.all_to_all(packed, "seq", split_axis=0, concat_axis=0, tiled=True)
    with jax.named_scope("out_y"):
        out_own = jnp.stack([out_w, y_up(out_w), y_down(out_w), y_far(out_w)])
    with jax.named_scope("out_x"):
        out_across = over_x(out_own)
    with jax.named_scope("out_core"):
        out_peer = other_core(out_own)
    qkv_copy = pl.pallas_call(
        lay_kernel,
        out_shape=jax.ShapeDtypeStruct((3 * HD, D), BF),
        in_specs=[ANY, VMEM],
        out_specs=VMEM,
        cost_estimate=takes(1.5),
        name="lay",
    )(out_own, temporal_w)
    with jax.named_scope("qkv_y"):
        below, above, far = y_up(qkv_copy), y_down(qkv_copy), y_far(qkv_copy)
    with jax.named_scope("last_x"):
        last_pair = jnp.stack([last_w, over_x(last_w)])
    last_held = gate(last_pair, far, "gate_pair")
    with jax.named_scope("last_y"):
        rings = [[4 * y + i for y in range(4)] for i in range(4)]
        last_own = lax.all_to_all(
            jnp.broadcast_to(last_held[None], (4, 2, HD, D)),
            "seq",
            split_axis=0,
            concat_axis=0,
            tiled=True,
            axis_index_groups=rings,
        )

    coef, mod, tokens = pl.pallas_call(
        coefficient_kernel,
        out_shape=(
            jax.ShapeDtypeStruct((2, 3, CP, D), F32),
            jax.ShapeDtypeStruct((16, D), F32),
            jax.ShapeDtypeStruct((2, 16, 1024), F32),
        ),
        in_specs=[VMEM] * 2 + [ANY],
        out_specs=(VMEM, VMEM, VMEM),
        scratch_shapes=[pltpu.VMEM((3, D, D), BF), pltpu.SemaphoreType.DMA((3, 4))],
        compiler_params=params(48),
        cost_estimate=takes(20),
        name="coefficients",
    )(everyone, embed_w, spatial_w)

    def attend(frame, *after):
        return pl.pallas_call(
            functools.partial(attend_kernel, frame),
            out_shape=jax.ShapeDtypeStruct((64, D), BF),
            in_specs=[VMEM] * 3 + [ANY] * len(after),
            out_specs=VMEM,
            scratch_shapes=[
                pltpu.VMEM((CP, 1024), F32),
                pltpu.VMEM((HEADS * CP, 64), F32),
            ],
            compiler_params=params(24),
            cost_estimate=takes(1),
            name="attend",
        )(packed[0], tokens, coef, *after)

    first = attend(0)
    second = attend(1, first, below, above, last_pair)
    out_across = gate(out_across, second, "gate_out")
    with jax.named_scope("out_core"):
        out_both = other_core(out_across)

    hidden, inner = pl.pallas_call(
        hidden_kernel,
        out_shape=(
            jax.ShapeDtypeStruct((D, 128), F32),
            jax.ShapeDtypeStruct((D, 128), BF),
        ),
        in_specs=[VMEM] * 9,
        out_specs=(VMEM, VMEM),
        scratch_shapes=[pltpu.VMEM((D, 128), F32)],
        compiler_params=params(24),
        cost_estimate=takes(2),
        name="hidden",
    )(first, second, lat, embed_w, mod, *(one.reshape(4 * HD, D) for one in (out_own, out_peer, out_across, out_both)))
    with jax.named_scope("inner"):
        pairs = [(16 * q + j, 16 * (q - 1) + (j ^ 2)) for q in range(1, 16) for j in range(16)]
        following_across = lax.ppermute(inner, ("queue", "seq"), pairs)
        across = over_x(inner)
        following = from_next(inner)
    with jax.named_scope("inner_core"):
        tokens_four = [inner, other_core(inner), across, other_core(across)]
        following_four = [following, other_core(following), following_across, other_core(following_across)]
    parts = pl.pallas_call(
        temporal_kernel,
        out_shape=(jax.ShapeDtypeStruct((4 * HD, 128), BF),) * 4,
        in_specs=[SMEM] + [ANY] * 4 + [VMEM] * 8,
        out_specs=(VMEM,) * 4,
        scratch_shapes=[pltpu.VMEM((4, 3 * HD, D), BF), pltpu.SemaphoreType.DMA((4,))],
        compiler_params=params(48),
        cost_estimate=takes(4),
        name="temporal",
    )(advance, qkv_copy, below, above, far, *tokens_four, *following_four)
    last_own = gate(last_own, parts[0], "gate_last")
    with jax.named_scope("last_core"):
        last_all = [one.reshape(8 * HD, D) for one in (last_own, other_core(last_own))]
    with jax.named_scope("back"):
        mix_all = [parts[0], other_core(parts[1]), over_x(parts[2]), over_both(parts[3])]
    velocity, updated = pl.pallas_call(
        final_kernel,
        out_shape=(
            jax.ShapeDtypeStruct((2, C, 64), F32),
            jax.ShapeDtypeStruct((2, C, 64), F32),
        ),
        in_specs=[VMEM] * 10,
        out_specs=(VMEM, VMEM),
        scratch_shapes=[pltpu.VMEM((D, 128), F32), pltpu.VMEM((D, 128), F32)],
        compiler_params=params(24),
        cost_estimate=takes(2.4),
        name="final",
    )(hidden, lat, mod, final_t, *mix_all, *last_all)
    incoming = from_next(updated[0])
    is_last = lax.axis_index("queue") == lax.axis_size("queue") - 1
    tail = jnp.where(is_last, fresh_noise.transpose(1, 0), incoming)
    queue_next = jnp.stack([updated[1], tail])
    return velocity.transpose(0, 2, 1), queue_next.transpose(0, 2, 1)


def solution(mesh):
    placed = (
        P("queue", "seq", None),
        P("queue"),
        P("queue"),
        P("seq", None),
        P(None, None, "seq"),
        P(),
        P(),
        P(None, "seq"),
        P(None, None, "seq"),
        P(None, "seq"),
        P(),
    )
    return jax.shard_map(
        shards,
        mesh=mesh,
        in_specs=placed,
        out_specs=(P("queue", "seq", None), P("queue", "seq", None)),
        check_vma=False,
    )
```

time: 129 us -> 108 us (0.84)
  waiting for transfers between devices: 52.7 us -> 17.2 us
  local copies, waits for them, and re-layouts: 4.51 us -> 16.2 us
  other arithmetic: 0.67 us -> 2.52 us
    ppermute x28 -> x19, waiting for transfers between devices: 44.2 us -> 8.7 us  [along_seq(): return lax.ppermute(array, 'seq', [(i, to(i)) for i in range(16)])]
    unnamed x28 -> x68, local copies, waits for them, and re-layouts: 4.47 us -> 13.3 us
    ppermute x2, waiting for transfers between devices: 8.54 us -> 1.34 us  [from_next(): return lax.ppermute(array, 'queue', [(i, i - 1) for i in range(1, 16)])]
    ppermute x28 -> x19, starting transfers between devices: 25.5 us -> 19 us  [along_seq(): return lax.ppermute(array, 'seq', [(i, to(i)) for i in range(16)])]
    all_to_all x0 -> x1, waiting for transfers between devices: none -> 5.36 us  [shards(): lax.all_to_all(jnp.broadcast_to(last_held[None], (4, 2, HD, D)), 'seq', s...]
    ppermute x0 -> x1, starting transfers between devices: none -> 3.7 us  [shards(): following_across = lax.ppermute(inner, ('queue', 'seq'), pairs)]
    all_to_all x0 -> x1, starting transfers between devices: none -> 3.67 us  [shards(): lax.all_to_all(jnp.broadcast_to(last_held[None], (4, 2, HD, D)), 'seq', s...]
    pallas_call x5 -> x9, Pallas kernels: 18.8 us -> 21.6 us  [the longest x2 8.13 us: attend(): pl.pallas_call(functools.partial(attend_kernel, frame), out_shape=jax.Sha...]
  transfers between devices with their start and end apart: 31 -> 24, of which waited for: 16 -> 11; matrix products, arithmetic and copies ran while one was open for 1% -> 4% of each run, Pallas kernels for 18% -> 22%
where the time goes in v2:
time: 108 us; the launch traced here: 107 us
  starting transfers between devices  43.7 us (40%)
  Pallas kernels  25.5 us (24%)
  waiting for transfers between devices  17.2 us (16%)
  local copies, waits for them, and re-layouts  16.2 us (15%)
  other arithmetic  2.52 us (2%)
  between operations  1.64 us (2%)
    ppermute x19, starting transfers between devices, along_seq(): return lax.ppermute(array, 'seq', [(i, to(i)) for i in range(16)])  19 us
    unnamed x68, local copies, waits for them, and re-layouts  13.3 us
    ppermute x2, starting transfers between devices, from_next(): return lax.ppermute(array, 'queue', [(i, i - 1) for i in range(1, 16)])  12.8 us
    ppermute x19, waiting for transfers between devices, along_seq(): return lax.ppermute(array, 'seq', [(i, to(i)) for i in range(16)])  8.7 us
    pallas_call x2, Pallas kernels, attend(): pl.pallas_call(functools.partial(attend_kernel, frame), out_shape=jax.Sha...  8.13 us
    all_to_all x1, waiting for transfers between devices, shards(): lax.all_to_all(jnp.broadcast_to(last_held[None], (4, 2, HD, D)), 'seq', s...  5.36 us
    pallas_call x1, Pallas kernels, shards(): pl.pallas_call(temporal_kernel, out_shape=(jax.ShapeDtypeStruct((4 * HD,...  5.35 us
    all_to_all x1, starting transfers between devices, shards(): lax.all_to_all(packed, 'seq', split_axis=0, concat_axis=0, tiled=True)  4.49 us
  transfers between devices with their start and end apart: 24, of which 11 were waited for; matrix products, arithmetic and copies ran while one was open for 4% of the time, Pallas kernels for 22%

profile of v2, /device:TPU:2, one launch (start us, length us, event | category | flops | bytes accessed | tf_op | source)
XLA Modules:
  0.0 106.8 jit_solution(17237252549751561816)
XLA Ops:
  0.6 1.7 %collective-permute-start = (bf16[72,1152]{1,0:T(8,128)(2,1)}, bf16[72,1152]{1,0:T(8,128)(2,1)S(1)}, u32[]{:S(2)}, u32[]{:S(2)}) collective-permute-start(bf16[72,1152]{1,0:T(8,128)(2,1)} %bitcast.48), channel_id=1, source_target_pairs={{0,4},{1,5},{2,6},{3,7},{4,8},{5,9},{6,10},{7,11},{8,12},{9,13},{1... | collective-permute-start | bytes 497672 | tf_op jit(solution)/shard_map/out_y/ppermute | solution.py:278
  2.3 1.7 %collective-permute-start.1 = (bf16[72,1152]{1,0:T(8,128)(2,1)}, bf16[72,1152]{1,0:T(8,128)(2,1)S(1)}, u32[]{:S(2)}, u32[]{:S(2)}) collective-permute-start(bf16[72,1152]{1,0:T(8,128)(2,1)} %bitcast.49), channel_id=1, source_target_pairs={{0,12},{1,13},{2,14},{3,15},{4,0},{5,1},{6,2},{7,3},{8,4},{9,5},{1... | collective-permute-start | bytes 497672 | tf_op jit(solution)/shard_map/out_y/ppermute | solution.py:278
  3.9 2.0 %collective-permute-start.2 = (bf16[72,1152]{1,0:T(8,128)(2,1)}, bf16[72,1152]{1,0:T(8,128)(2,1)S(1)}, u32[]{:S(2)}, u32[]{:S(2)}) collective-permute-start(bf16[72,1152]{1,0:T(8,128)(2,1)} %bitcast.50), channel_id=1, source_target_pairs={{0,8},{1,9},{2,10},{3,11},{4,12},{5,13},{6,14},{7,15},{8,0},{9,1},... | collective-permute-start | bytes 497672 | tf_op jit(solution)/shard_map/out_y/ppermute | solution.py:278
  5.9 2.2 %pack.1 = f32[16,40,128]{2,1,0:T(8,128)} custom-call(s32[2]{0:T(128)} %levels_ref.1, f32[2,16,64]{2,1,0:T(8,128)} %bitcast.42, f32[16,1152]{1,0:T(8,128)} %embed_ref.5, f32[32,8,72]{2,1,0:T(8,128)} %table_ref.1), custom_call_target="tpu_custom_call" | custom-call | flops 2300000000 | bytes 1000 | tf_op jit(solution)/shard_map/pack/pallas_call | solution.py:352
  8.1 4.5 %all-to-all-start = ((f32[16,40,128]{2,1,0:T(8,128)}), f32[16,40,128]{2,1,0:T(8,128)S(1)}, u32[]{:S(2)}, u32[]{:S(2)}) async-start(f32[16,40,128]{2,1,0:T(8,128)} %pack.1), calls=%async_computation | async-start | bytes 655360 | tf_op jit(solution)/shard_map/all_to_all | solution.py:360
  12.6 3.5 %collective-permute-start.5 = (bf16[72,1152]{1,0:T(8,128)(2,1)S(1)}, bf16[72,1152]{1,0:T(8,128)(2,1)S(1)}, u32[]{:S(2)}, u32[]{:S(2)}) collective-permute-start(bf16[72,1152]{1,0:T(8,128)(2,1)S(1)} %bitcast.45), channel_id=1, source_target_pairs={{0,2},{1,3},{2,0},{3,1},{4,6},{5,7},{6,4},{7,5},{8,10},{9,11},{10,... | collective-permute-start | bytes 497672 | tf_op jit(solution)/shard_map/last_x/ppermute | solution.py:278
  17.8 1.9 %lay.1.refs_0_ = bf16[216,1152]{1,0:T(8,128)(2,1)} custom-call(bf16[4,72,1152]{2,1,0:T(8,128)(2,1)} %pad_maximum_fusion.after_ref, bf16[216,1152]{1,0:T(8,128)(2,1)} %bitcast.56), custom_call_target="tpu_custom_call" | custom-call | flops 1724999936 | bytes 1000 | tf_op jit(solution)/shard_map/lay/pallas_call | solution.py:367
  19.8 1.5 %collective-permute-start.3 = (bf16[216,1152]{1,0:T(8,128)(2,1)}, bf16[216,1152]{1,0:T(8,128)(2,1)S(1)}, u32[]{:S(2)}, u32[]{:S(2)}) collective-permute-start(bf16[216,1152]{1,0:T(8,128)(2,1)} %lay.1.refs_0_), channel_id=1, source_target_pairs={{0,4},{1,5},{2,6},{3,7},{4,8},{5,9},{6,10},{7,11},{8,12},{9,13},{1... | collective-permute-start | bytes 1493000 | tf_op jit(solution)/shard_map/qkv_y/ppermute | solution.py:278
  21.2 1.8 %collective-permute-start.4 = (bf16[216,1152]{1,0:T(8,128)(2,1)}, bf16[216,1152]{1,0:T(8,128)(2,1)}, u32[]{:S(2)}, u32[]{:S(2)}) collective-permute-start(bf16[216,1152]{1,0:T(8,128)(2,1)} %lay.1.refs_0_), channel_id=1, source_target_pairs={{0,12},{1,13},{2,14},{3,15},{4,0},{5,1},{6,2},{7,3},{8,4},{9,5},{1... | collective-permute-start | bytes 1493000 | tf_op jit(solution)/shard_map/qkv_y/ppermute | solution.py:278
  23.1 1.2 %collective-permute-done.5 = bf16[72,1152]{1,0:T(8,128)(2,1)S(1)} collective-permute-done((bf16[72,1152]{1,0:T(8,128)(2,1)S(1)}, bf16[72,1152]{1,0:T(8,128)(2,1)S(1)}, u32[]{:S(2)}, u32[]{:S(2)}) %collective-permute-start.5) | collective-permute-done | bytes 165920 | tf_op jit(solution)/shard_map/last_x/ppermute | solution.py:278
  26.0 4.1 %coefficients.1 = (f32[2,3,32,1152]{3,2,1,0:T(8,128)S(1)}, f32[16,1152]{1,0:T(8,128)S(1)}, f32[2,16,1024]{2,1,0:T(8,128)S(1)}) custom-call(f32[16,40,128]{2,1,0:T(8,128)S(1)} %all-to-all-done.all_ref, f32[16,1152]{1,0:T(8,128)S(1)} %copy-done.13, bf16[3,1152,1152]{2,1,0:T(8,128)(2,1)} %bitcast.55), custom_call_target="tpu_custom_call" | custom-call | flops 23000000512 | bytes 1000 | tf_op jit(solution)/shard_map/coefficients/pallas_call | solution.py:391
  30.0 4.1 %attend.2.refs_0_.first_ref = bf16[64,1152]{1,0:T(8,128)(2,1)S(1)} custom-call(f32[40,128]{1,0:T(8,128)S(1)} %slice_bitcast_fusion.own_ref, f32[2,16,1024]{2,1,0:T(8,128)S(1)} %get-tuple-element.13.tokens_ref, f32[2,3,32,1152]{3,2,1,0:T(8,128)S(1)} %get-tuple-element.14.coef_ref), custom_call_target="tpu_custom_call" | custom-call | flops 1150000000 | bytes 1000 | tf_op jit(solution)/shard_map/attend/pallas_call | solution.py:407
  34.4 4.1 %attend.3.after_ref.second_ref = bf16[64,1152]{1,0:T(8,128)(2,1)S(1)} custom-call(f32[40,128]{1,0:T(8,128)S(1)} %slice_bitcast_fusion.own_ref, f32[2,16,1024]{2,1,0:T(8,128)S(1)} %get-tuple-element.13.tokens_ref, f32[2,3,32,1152]{3,2,1,0:T(8,128)S(1)} %get-tuple-element.14.coef_ref, bf16[64,1152]{1,0:T(8,128)(2,1)S(1)} %attend.2.refs_0_.first_ref, ...), custom_call_target="tpu_custom_call" | custom-call | flops 1150000000 | bytes 1000 | tf_op jit(solution)/shard_map/attend/pallas_call | solution.py:407
  39.2 1.5 %collective-permute-done.7.held_ref = bf16[4,72,1152]{2,1,0:T(8,128)(2,1)S(1)} collective-permute-done((bf16[4,72,1152]{2,1,0:T(8,128)(2,1)S(1)}, bf16[4,72,1152]{2,1,0:T(8,128)(2,1)S(1)}, u32[]{:S(2)}, u32[]{:S(2)}) %collective-permute-start.7) | collective-permute-done | bytes 663584 | tf_op jit(solution)/shard_map/out_x/ppermute | solution.py:278
  41.5 1.8 %collective-permute-start.9 = (bf16[216,1152]{1,0:T(8,128)(2,1)S(1)}, bf16[216,1152]{1,0:T(8,128)(2,1)S(1)}, u32[]{:S(2)}, u32[]{:S(2)}) collective-permute-start(bf16[216,1152]{1,0:T(8,128)(2,1)S(1)} %copy-done.12), channel_id=1, source_target_pairs={{0,8},{1,9},{2,10},{3,11},{4,12},{5,13},{6,14},{7,15},{8,0},{9,1},... | collective-permute-start | bytes 1493000 | tf_op jit(solution)/shard_map/qkv_y/ppermute | solution.py:278
  47.6 1.5 %hidden.1 = (f32[1152,128]{1,0:T(8,128)S(1)}, bf16[1152,128]{1,0:T(8,128)(2,1)S(1)}) custom-call(bf16[64,1152]{1,0:T(8,128)(2,1)S(1)} %copy-done.24, bf16[64,1152]{1,0:T(8,128)(2,1)S(1)} %copy-done.9, f32[2,16,64]{2,1,0:T(8,128)S(1)} %bitcast.43, f32[16,1152]{1,0:T(8,128)S(1)} %copy-done.14, f32[16,1152]{1,0:T(8,128)S(1)} %copy-done.28, ...), custom_call_target="tpu_custom_call" | custom-call | flops 2300000000 | bytes 1000 | tf_op jit(solution)/shard_map/hidden/pallas_call | solution.py:427
  50.6 8.6 %collective-permute-start.13 = (bf16[1152,128]{1,0:T(8,128)(2,1)S(1)}, bf16[1152,128]{1,0:T(8,128)(2,1)}, u32[]{:S(2)}, u32[]{:S(2)}) collective-permute-start(bf16[1152,128]{1,0:T(8,128)(2,1)S(1)} %get-tuple-element.17.refs_4_), channel_id=1, source_target_pairs={{16,0},{32,16},{48,32},{64,48},{80,64},{96,80},{112,96},{128,112},... | collective-permute-start | bytes 884744 | tf_op jit(solution)/shard_map/inner/ppermute | solution.py:298
  59.2 3.7 %collective-permute-start.15 = (bf16[1152,128]{1,0:T(8,128)(2,1)S(1)}, bf16[1152,128]{1,0:T(8,128)(2,1)}, u32[]{:S(2)}, u32[]{:S(2)}) collective-permute-start(bf16[1152,128]{1,0:T(8,128)(2,1)S(1)} %get-tuple-element.17.refs_4_), channel_id=1, source_target_pairs={{16,2},{17,3},{18,0},{19,1},{20,6},{21,7},{22,4},{23,5},{24,10},{2... | collective-permute-start | bytes 884744 | tf_op jit(solution)/shard_map/inner/ppermute | solution.py:442
  63.8 2.2 %broadcast_in_dim.2 = bf16[4,2,72,1152]{3,2,1,0:T(8,128)(2,1)} broadcast(bf16[2,72,1152]{2,1,0:T(8,128)(2,1)} %gate_pair.1), dimensions={1,2,3} | broadcast | bytes 1658880 | tf_op jit(solution)/shard_map/last_y/broadcast_in_dim | solution.py:383
  65.9 3.7 %all-to-all-start.1 = ((bf16[4,2,72,1152]{3,2,1,0:T(8,128)(2,1)}), bf16[4,2,72,1152]{3,2,1,0:T(8,128)(2,1)S(1)}, u32[]{:S(2)}, u32[]{:S(2)}) async-start(bf16[4,2,72,1152]{3,2,1,0:T(8,128)(2,1)} %broadcast_in_dim.2), calls=%async_computation.1 | async-start | bytes 2654208 | tf_op jit(solution)/shard_map/last_y/all_to_all | solution.py:382
  70.5 1.8 %collective-permute-done.15.refs_10_ = bf16[1152,128]{1,0:T(8,128)(2,1)} collective-permute-done((bf16[1152,128]{1,0:T(8,128)(2,1)S(1)}, bf16[1152,128]{1,0:T(8,128)(2,1)}, u32[]{:S(2)}, u32[]{:S(2)}) %collective-permute-start.15) | collective-permute-done | bytes 294944 | tf_op jit(solution)/shard_map/inner/ppermute | solution.py:442
  73.0 1.1 %collective-permute-done.16.refs_11_ = bf16[1152,128]{1,0:T(8,128)(2,1)S(1)} collective-permute-done((bf16[1152,128]{1,0:T(8,128)(2,1)}, bf16[1152,128]{1,0:T(8,128)(2,1)S(1)}, u32[]{:S(2)}, u32[]{:S(2)}) %collective-permute-start.16) | collective-permute-done | bytes 294944 | tf_op jit(solution)/shard_map/inner_core/ppermute | solution.py:278
  74.1 5.3 %temporal.1 = (bf16[288,128]{1,0:T(8,128)(2,1)S(1)}, bf16[288,128]{1,0:T(8,128)(2,1)S(1)}, bf16[288,128]{1,0:T(8,128)(2,1)S(1)}, bf16[288,128]{1,0:T(8,128)(2,1)S(1)}) custom-call(s32[1]{0:T(128)S(6)} %copy.19.advance_ref, bf16[216,1152]{1,0:T(8,128)(2,1)S(1)} %copy-done.12, bf16[216,1152]{1,0:T(8,128)(2,1)S(1)} %collective-permute-done.3.refs_1_, ...), custom_call_target="tpu_custom_call" | custom-call | flops 4600000000 | bytes 1000 | tf_op jit(solution)/shard_map/temporal/pallas_call | solution.py:448
  82.0 5.4 %all-to-all-done.1.held_ref = bf16[4,2,72,1152]{3,2,1,0:T(8,128)(2,1)S(1)} async-done(((bf16[4,2,72,1152]{3,2,1,0:T(8,128)(2,1)}), bf16[4,2,72,1152]{3,2,1,0:T(8,128)(2,1)S(1)}, u32[]{:S(2)}, u32[]{:S(2)}) %all-to-all-start.1) | async-done | bytes 1327136 | tf_op jit(solution)/shard_map/last_y/all_to_all | solution.py:382
  89.4 1.5 %collective-permute-start.18 = (bf16[288,128]{1,0:T(8,128)(2,1)S(1)}, bf16[288,128]{1,0:T(8,128)(2,1)S(1)}, u32[]{:S(2)}, u32[]{:S(2)}) collective-permute-start(bf16[288,128]{1,0:T(8,128)(2,1)S(1)} %copy-done.18), channel_id=1, source_target_pairs={{0,2},{1,3},{2,0},{3,1},{4,6},{5,7},{6,4},{7,5},{8,10},{9,11},{10,... | collective-permute-start | bytes 221192 | tf_op jit(solution)/shard_map/back/ppermute | solution.py:278
  90.9 1.8 %collective-permute-start.19 = (bf16[288,128]{1,0:T(8,128)(2,1)S(1)}, bf16[288,128]{1,0:T(8,128)(2,1)S(1)}, u32[]{:S(2)}, u32[]{:S(2)}) collective-permute-start(bf16[288,128]{1,0:T(8,128)(2,1)S(1)} %copy-done.16), channel_id=1, source_target_pairs={{0,3},{1,2},{2,1},{3,0},{4,7},{5,6},{6,5},{7,4},{8,11},{9,10},{10,... | collective-permute-start | bytes 221192 | tf_op jit(solution)/shard_map/back/ppermute | solution.py:278
  92.7 3.0 %collective-permute-done.18.rest_2_ = bf16[288,128]{1,0:T(8,128)(2,1)S(1)} collective-permute-done((bf16[288,128]{1,0:T(8,128)(2,1)S(1)}, bf16[288,128]{1,0:T(8,128)(2,1)S(1)}, u32[]{:S(2)}, u32[]{:S(2)}) %collective-permute-start.18) | collective-permute-done | bytes 73760 | tf_op jit(solution)/shard_map/back/ppermute | solution.py:278
  95.7 1.2 %collective-permute-done.19.rest_3_ = bf16[288,128]{1,0:T(8,128)(2,1)S(1)} collective-permute-done((bf16[288,128]{1,0:T(8,128)(2,1)S(1)}, bf16[288,128]{1,0:T(8,128)(2,1)S(1)}, u32[]{:S(2)}, u32[]{:S(2)}) %collective-permute-start.19) | collective-permute-done | bytes 73760 | tf_op jit(solution)/shard_map/back/ppermute | solution.py:278
  96.9 1.3 %copy-done.1 = bf16[4,2,72,1152]{3,2,1,0:T(8,128)(2,1)S(1)} copy-done((bf16[4,2,72,1152]{3,2,1,0:T(8,128)(2,1)S(1)}, bf16[4,2,72,1152]{3,2,1,0:T(8,128)(2,1)}, u32[]{:S(2)}) %copy-start.1) | copy-done | bytes 1327128
  98.2 2.4 %final.1 = (f32[2,16,64]{2,1,0:T(8,128)}, f32[2,16,64]{2,1,0:T(8,128)S(1)}) custom-call(f32[1152,128]{1,0:T(8,128)S(1)} %copy-done.26, f32[2,16,64]{2,1,0:T(8,128)S(1)} %bitcast.44, f32[16,1152]{1,0:T(8,128)S(1)} %copy-done.29, bf16[16,1152]{1,0:T(8,128)(2,1)S(1)} %bitcast.41, bf16[288,128]{1,0:T(8,128)(2,1)S(1)} %copy-done.11, ...), custom_call_target="tpu_custom_call" | custom-call | flops 2760000000 | bytes 1000 | tf_op jit(solution)/shard_map/final/pallas_call | solution.py:463
  100.6 4.2 %collective-permute-start.21 = (f32[16,64]{1,0:T(8,128)S(1)}, f32[16,64]{1,0:T(8,128)S(1)}, u32[]{:S(2)}, u32[]{:S(2)}) collective-permute-start(f32[16,64]{1,0:T(8,128)S(1)} %get-tuple-element.25), channel_id=1, source_target_pairs={{16,0},{32,16},{48,32},{64,48},{80,64},{96,80},{112,96},{128,112},... | collective-permute-start | bytes 12296 | tf_op jit(solution)/shard_map/ppermute | solution.py:298
  104.8 1.3 %collective-permute-done.21 = f32[16,64]{1,0:T(8,128)S(1)} collective-permute-done((f32[16,64]{1,0:T(8,128)S(1)}, f32[16,64]{1,0:T(8,128)S(1)}, u32[]{:S(2)}, u32[]{:S(2)}) %collective-permute-start.21) | collective-permute-done | bytes 4128 | tf_op jit(solution)/shard_map/ppermute | solution.py:298
  (102 shorter events, 17.7 us)
Async XLA Ops:
  0.6 16.2 %collective-permute-start = (bf16[72,1152]{1,0:T(8,128)(2,1)}, bf16[72,1152]{1,0:T(8,128)(2,1)S(1)}, u32[]{:S(2)}, u32[]{:S(2)}) collective-permute-start(bf16[72,1152]{1,0:T(8,128)(2,1)} %bitcast.48), channel_id=1, source_target_pairs={{0,4},{1,5},{2,6},{3,7},{4,8},{5,9},{6,10},{7,11},{8,12},{9,13},{1... | collective-permute-start | bytes 497672 | tf_op jit(solution)/shard_map/out_y/ppermute | solution.py:278
  2.3 14.6 %collective-permute-start.1 = (bf16[72,1152]{1,0:T(8,128)(2,1)}, bf16[72,1152]{1,0:T(8,128)(2,1)S(1)}, u32[]{:S(2)}, u32[]{:S(2)}) collective-permute-start(bf16[72,1152]{1,0:T(8,128)(2,1)} %bitcast.49), channel_id=1, source_target_pairs={{0,12},{1,13},{2,14},{3,15},{4,0},{5,1},{6,2},{7,3},{8,4},{9,5},{1... | collective-permute-start | bytes 497672 | tf_op jit(solution)/shard_map/out_y/ppermute | solution.py:278
  3.9 12.9 %collective-permute-start.2 = (bf16[72,1152]{1,0:T(8,128)(2,1)}, bf16[72,1152]{1,0:T(8,128)(2,1)S(1)}, u32[]{:S(2)}, u32[]{:S(2)}) collective-permute-start(bf16[72,1152]{1,0:T(8,128)(2,1)} %bitcast.50), channel_id=1, source_target_pairs={{0,8},{1,9},{2,10},{3,11},{4,12},{5,13},{6,14},{7,15},{8,0},{9,1},... | collective-permute-start | bytes 497672 | tf_op jit(solution)/shard_map/out_y/ppermute | solution.py:278
  5.9 10.9 %copy-start.32 = (bf16[1152,72]{0,1:T(8,128)(2,1)S(1)}, bf16[1152,72]{0,1:T(8,128)(2,1)}, u32[]{:S(2)}) copy-start(bf16[1152,72]{0,1:T(8,128)(2,1)} %param.18) | copy-start | bytes 497668
  8.1 17.8 %all-to-all-start = ((f32[16,40,128]{2,1,0:T(8,128)}), f32[16,40,128]{2,1,0:T(8,128)S(1)}, u32[]{:S(2)}, u32[]{:S(2)}) async-start(f32[16,40,128]{2,1,0:T(8,128)} %pack.1), calls=%async_computation | async-start | bytes 655360 | tf_op jit(solution)/shard_map/all_to_all | solution.py:360
  12.6 11.7 %collective-permute-start.5 = (bf16[72,1152]{1,0:T(8,128)(2,1)S(1)}, bf16[72,1152]{1,0:T(8,128)(2,1)S(1)}, u32[]{:S(2)}, u32[]{:S(2)}) collective-permute-start(bf16[72,1152]{1,0:T(8,128)(2,1)S(1)} %bitcast.45), channel_id=1, source_target_pairs={{0,2},{1,3},{2,0},{3,1},{4,6},{5,7},{6,4},{7,5},{8,10},{9,11},{10,... | collective-permute-start | bytes 497672 | tf_op jit(solution)/shard_map/last_x/ppermute | solution.py:278
  17.8 8.1 %copy-start.13 = (f32[16,1152]{1,0:T(8,128)S(1)}, f32[16,1152]{1,0:T(8,128)}, u32[]{:S(2)}) copy-start(f32[16,1152]{1,0:T(8,128)} %embed_ref.5) | copy-start | bytes 221188
  19.8 14.5 %collective-permute-start.3 = (bf16[216,1152]{1,0:T(8,128)(2,1)}, bf16[216,1152]{1,0:T(8,128)(2,1)S(1)}, u32[]{:S(2)}, u32[]{:S(2)}) collective-permute-start(bf16[216,1152]{1,0:T(8,128)(2,1)} %lay.1.refs_0_), channel_id=1, source_target_pairs={{0,4},{1,5},{2,6},{3,7},{4,8},{5,9},{6,10},{7,11},{8,12},{9,13},{1... | collective-permute-start | bytes 1493000 | tf_op jit(solution)/shard_map/qkv_y/ppermute | solution.py:278
  21.2 13.2 %collective-permute-start.4 = (bf16[216,1152]{1,0:T(8,128)(2,1)}, bf16[216,1152]{1,0:T(8,128)(2,1)}, u32[]{:S(2)}, u32[]{:S(2)}) collective-permute-start(bf16[216,1152]{1,0:T(8,128)(2,1)} %lay.1.refs_0_), channel_id=1, source_target_pairs={{0,12},{1,13},{2,14},{3,15},{4,0},{5,1},{6,2},{7,3},{8,4},{9,5},{1... | collective-permute-start | bytes 1493000 | tf_op jit(solution)/shard_map/qkv_y/ppermute | solution.py:278
  23.0 17.6 %collective-permute-start.7 = (bf16[4,72,1152]{2,1,0:T(8,128)(2,1)S(1)}, bf16[4,72,1152]{2,1,0:T(8,128)(2,1)S(1)}, u32[]{:S(2)}, u32[]{:S(2)}) collective-permute-start(bf16[4,72,1152]{2,1,0:T(8,128)(2,1)S(1)} %copy-done.3), channel_id=1, source_target_pairs={{0,2},{1,3},{2,0},{3,1},{4,6},{5,7},{6,4},{7,5},{8,10},{9,11},{10,... | collective-permute-start | bytes 1990664 | tf_op jit(solution)/shard_map/out_x/ppermute | solution.py:278
  23.1 20.2 %collective-permute-start.6 = (bf16[4,72,1152]{2,1,0:T(8,128)(2,1)S(1)}, bf16[4,72,1152]{2,1,0:T(8,128)(2,1)S(1)}, u32[]{:S(2)}, u32[]{:S(2)}) collective-permute-start(bf16[4,72,1152]{2,1,0:T(8,128)(2,1)S(1)} %copy-done.3), channel_id=1, source_target_pairs={{0,1},{1,0},{2,3},{3,2},{4,5},{5,4},{6,7},{7,6},{8,9},{9,8},{10,11... | collective-permute-start | bytes 1990664 | tf_op jit(solution)/shard_map/out_core/ppermute | solution.py:278
  25.9 8.5 %copy-start.2 = (bf16[2,72,1152]{2,1,0:T(8,128)(2,1)}, bf16[2,72,1152]{2,1,0:T(8,128)(2,1)S(1)}, u32[]{:S(2)}) copy-start(bf16[2,72,1152]{2,1,0:T(8,128)(2,1)S(1)} %pad_maximum_fusion.1.refs_3_.held_ref) | copy-start | bytes 995332
  41.5 2.3 %collective-permute-start.8 = (bf16[4,72,1152]{2,1,0:T(8,128)(2,1)}, bf16[4,72,1152]{2,1,0:T(8,128)(2,1)S(1)}, u32[]{:S(2)}, u32[]{:S(2)}) collective-permute-start(bf16[4,72,1152]{2,1,0:T(8,128)(2,1)} %gate_out.1), channel_id=1, source_target_pairs={{0,1},{1,0},{2,3},{3,2},{4,5},{5,4},{6,7},{7,6},{8,9},{9,8},{10,11... | collective-permute-start | bytes 1990664 | tf_op jit(solution)/shard_map/out_core/ppermute | solution.py:278
  41.5 21.5 %collective-permute-start.9 = (bf16[216,1152]{1,0:T(8,128)(2,1)S(1)}, bf16[216,1152]{1,0:T(8,128)(2,1)S(1)}, u32[]{:S(2)}, u32[]{:S(2)}) collective-permute-start(bf16[216,1152]{1,0:T(8,128)(2,1)S(1)} %copy-done.12), channel_id=1, source_target_pairs={{0,8},{1,9},{2,10},{3,11},{4,12},{5,13},{6,14},{7,15},{8,0},{9,1},... | collective-permute-start | bytes 1493000 | tf_op jit(solution)/shard_map/qkv_y/ppermute | solution.py:278
  49.9 19.8 %collective-permute-start.11 = (bf16[1152,128]{1,0:T(8,128)(2,1)S(1)}, bf16[1152,128]{1,0:T(8,128)(2,1)S(1)}, u32[]{:S(2)}, u32[]{:S(2)}) collective-permute-start(bf16[1152,128]{1,0:T(8,128)(2,1)S(1)} %get-tuple-element.17.refs_4_), channel_id=1, source_target_pairs={{0,2},{1,3},{2,0},{3,1},{4,6},{5,7},{6,4},{7,5},{8,10},{9,11},{10,... | collective-permute-start | bytes 884744 | tf_op jit(solution)/shard_map/inner/ppermute | solution.py:278
  50.6 19.6 %collective-permute-start.13 = (bf16[1152,128]{1,0:T(8,128)(2,1)S(1)}, bf16[1152,128]{1,0:T(8,128)(2,1)}, u32[]{:S(2)}, u32[]{:S(2)}) collective-permute-start(bf16[1152,128]{1,0:T(8,128)(2,1)S(1)} %get-tuple-element.17.refs_4_), channel_id=1, source_target_pairs={{16,0},{32,16},{48,32},{64,48},{80,64},{96,80},{112,96},{128,112},... | collective-permute-start | bytes 884744 | tf_op jit(solution)/shard_map/inner/ppermute | solution.py:298
  59.2 13.1 %collective-permute-start.15 = (bf16[1152,128]{1,0:T(8,128)(2,1)S(1)}, bf16[1152,128]{1,0:T(8,128)(2,1)}, u32[]{:S(2)}, u32[]{:S(2)}) collective-permute-start(bf16[1152,128]{1,0:T(8,128)(2,1)S(1)} %get-tuple-element.17.refs_4_), channel_id=1, source_target_pairs={{16,2},{17,3},{18,0},{19,1},{20,6},{21,7},{22,4},{23,5},{24,10},{2... | collective-permute-start | bytes 884744 | tf_op jit(solution)/shard_map/inner/ppermute | solution.py:442
  65.9 8.2 %copy-start.7 = (bf16[216,1152]{1,0:T(8,128)(2,1)S(1)}, bf16[216,1152]{1,0:T(8,128)(2,1)}, u32[]{:S(2)}) copy-start(bf16[216,1152]{1,0:T(8,128)(2,1)} %copy-done.6) | copy-start | bytes 1492996
  65.9 21.5 %all-to-all-start.1 = ((bf16[4,2,72,1152]{3,2,1,0:T(8,128)(2,1)}), bf16[4,2,72,1152]{3,2,1,0:T(8,128)(2,1)S(1)}, u32[]{:S(2)}, u32[]{:S(2)}) async-start(bf16[4,2,72,1152]{3,2,1,0:T(8,128)(2,1)} %broadcast_in_dim.2), calls=%async_computation.1 | async-start | bytes 2654208 | tf_op jit(solution)/shard_map/last_y/all_to_all | solution.py:382
  69.6 3.4 %collective-permute-start.10 = (bf16[1152,128]{1,0:T(8,128)(2,1)S(1)}, bf16[1152,128]{1,0:T(8,128)(2,1)S(1)}, u32[]{:S(2)}, u32[]{:S(2)}) collective-permute-start(bf16[1152,128]{1,0:T(8,128)(2,1)S(1)} %get-tuple-element.17.refs_4_), channel_id=1, source_target_pairs={{0,1},{1,0},{2,3},{3,2},{4,5},{5,4},{6,7},{7,6},{8,9},{9,8},{10,11... | collective-permute-start | bytes 884744 | tf_op jit(solution)/shard_map/inner_core/ppermute | solution.py:278
  69.7 3.3 %collective-permute-start.12 = (bf16[1152,128]{1,0:T(8,128)(2,1)S(1)}, bf16[1152,128]{1,0:T(8,128)(2,1)S(1)}, u32[]{:S(2)}, u32[]{:S(2)}) collective-permute-start(bf16[1152,128]{1,0:T(8,128)(2,1)S(1)} %collective-permute-done.11.refs_6_), channel_id=1, source_target_pairs={{0,1},{1,0},{2,3},{3,2},{4,5},{5,4},{6,7},{7,6},{8,9},{9,8},{10,11... | collective-permute-start | bytes 884744 | tf_op jit(solution)/shard_map/inner_core/ppermute | solution.py:278
  70.2 2.8 %collective-permute-start.14 = (bf16[1152,128]{1,0:T(8,128)(2,1)}, bf16[1152,128]{1,0:T(8,128)(2,1)S(1)}, u32[]{:S(2)}, u32[]{:S(2)}) collective-permute-start(bf16[1152,128]{1,0:T(8,128)(2,1)} %collective-permute-done.13.refs_8_), channel_id=1, source_target_pairs={{0,1},{1,0},{2,3},{3,2},{4,5},{5,4},{6,7},{7,6},{8,9},{9,8},{10,11... | collective-permute-start | bytes 884744 | tf_op jit(solution)/shard_map/inner_core/ppermute | solution.py:278
  72.4 1.8 %collective-permute-start.16 = (bf16[1152,128]{1,0:T(8,128)(2,1)}, bf16[1152,128]{1,0:T(8,128)(2,1)S(1)}, u32[]{:S(2)}, u32[]{:S(2)}) collective-permute-start(bf16[1152,128]{1,0:T(8,128)(2,1)} %collective-permute-done.15.refs_10_), channel_id=1, source_target_pairs={{0,1},{1,0},{2,3},{3,2},{4,5},{5,4},{6,7},{7,6},{8,9},{9,8},{10,11... | collective-permute-start | bytes 884744 | tf_op jit(solution)/shard_map/inner_core/ppermute | solution.py:278
  88.5 8.4 %copy-start.11 = (bf16[288,128]{1,0:T(8,128)(2,1)S(1)}, bf16[288,128]{1,0:T(8,128)(2,1)}, u32[]{:S(2)}) copy-start(bf16[288,128]{1,0:T(8,128)(2,1)} %copy-done.10) | copy-start | bytes 221188
  88.5 8.4 %copy-start.21 = (bf16[1152,16]{0,1:T(8,128)(2,1)S(1)}, bf16[1152,16]{0,1:T(8,128)(2,1)}, u32[]{:S(2)}) copy-start(bf16[1152,16]{0,1:T(8,128)(2,1)} %param.21) | copy-start | bytes 110596
  88.5 8.4 %copy-start.26 = (f32[1152,128]{1,0:T(8,128)S(1)}, f32[1152,128]{1,0:T(8,128)}, u32[]{:S(2)}) copy-start(f32[1152,128]{1,0:T(8,128)} %copy-done.25) | copy-start | bytes 1769476
  88.5 8.4 %copy-start.29 = (f32[16,1152]{1,0:T(8,128)S(1)}, f32[16,1152]{1,0:T(8,128)}, u32[]{:S(2)}) copy-start(f32[16,1152]{1,0:T(8,128)} %copy-done.27) | copy-start | bytes 221188
  88.5 8.4 %collective-permute-start.20 = (bf16[4,2,72,1152]{3,2,1,0:T(8,128)(2,1)}, bf16[4,2,72,1152]{3,2,1,0:T(8,128)(2,1)S(1)}, u32[]{:S(2)}, u32[]{:S(2)}) collective-permute-start(bf16[4,2,72,1152]{3,2,1,0:T(8,128)(2,1)} %gate_last.1), channel_id=1, source_target_pairs={{0,1},{1,0},{2,3},{3,2},{4,5},{5,4},{6,7},{7,6},{8,9},{9,8},{10,11... | collective-permute-start | bytes 3981320 | tf_op jit(solution)/shard_map/last_core/ppermute | solution.py:278
  89.3 3.4 %collective-permute-start.17 = (bf16[288,128]{1,0:T(8,128)(2,1)S(1)}, bf16[288,128]{1,0:T(8,128)(2,1)S(1)}, u32[]{:S(2)}, u32[]{:S(2)}) collective-permute-start(bf16[288,128]{1,0:T(8,128)(2,1)S(1)} %copy-done.20), channel_id=1, source_target_pairs={{0,1},{1,0},{2,3},{3,2},{4,5},{5,4},{6,7},{7,6},{8,9},{9,8},{10,11... | collective-permute-start | bytes 221192 | tf_op jit(solution)/shard_map/back/ppermute | solution.py:278
  89.4 6.3 %collective-permute-start.18 = (bf16[288,128]{1,0:T(8,128)(2,1)S(1)}, bf16[288,128]{1,0:T(8,128)(2,1)S(1)}, u32[]{:S(2)}, u32[]{:S(2)}) collective-permute-start(bf16[288,128]{1,0:T(8,128)(2,1)S(1)} %copy-done.18), channel_id=1, source_target_pairs={{0,2},{1,3},{2,0},{3,1},{4,6},{5,7},{6,4},{7,5},{8,10},{9,11},{10,... | collective-permute-start | bytes 221192 | tf_op jit(solution)/shard_map/back/ppermute | solution.py:278
  90.9 6.0 %collective-permute-start.19 = (bf16[288,128]{1,0:T(8,128)(2,1)S(1)}, bf16[288,128]{1,0:T(8,128)(2,1)S(1)}, u32[]{:S(2)}, u32[]{:S(2)}) collective-permute-start(bf16[288,128]{1,0:T(8,128)(2,1)S(1)} %copy-done.16), channel_id=1, source_target_pairs={{0,3},{1,2},{2,1},{3,0},{4,7},{5,6},{6,5},{7,4},{8,11},{9,10},{10,... | collective-permute-start | bytes 221192 | tf_op jit(solution)/shard_map/back/ppermute | solution.py:278
  100.6 5.6 %collective-permute-start.21 = (f32[16,64]{1,0:T(8,128)S(1)}, f32[16,64]{1,0:T(8,128)S(1)}, u32[]{:S(2)}, u32[]{:S(2)}) collective-permute-start(f32[16,64]{1,0:T(8,128)S(1)} %get-tuple-element.25), channel_id=1, source_target_pairs={{16,0},{32,16},{48,32},{64,48},{80,64},{96,80},{112,96},{128,112},... | collective-permute-start | bytes 12296 | tf_op jit(solution)/shard_map/ppermute | solution.py:298
  (26 other events, 54.2 us)

commit v3 on v2

--- a/solution.py
+++ b/solution.py
@@ -74,13 +74,14 @@
     return [columns[:, tokens * i : tokens * (i + 1)] for i in range(len(rows))]
 
 
-def pack_kernel(levels_ref, latents_ref, embed_ref, table_ref, out_ref):
+def pack_kernel(levels_ref, latents_ref, embed_ref, table_ref, after_ref, out_ref, own_ref):
     channels = both_frames(latents_ref)
     embed = embed_ref[...]
     centered = embed - jnp.sum(embed, axis=1, keepdims=True) * (1.0 / D)
     spread = product_tn(centered, channels)
     variance = jnp.sum(spread * spread, axis=0, keepdims=True) * (1.0 / D)
     inverse = lax.rsqrt(variance + 1e-06)
+    own_ref[...] = channels * inverse
     peers = out_ref.shape[0]
     for peer in range(peers):
         out_ref[peer, 0:16, :] = channels
@@ -142,8 +143,7 @@
     one_row_all = (lax.broadcasted_iota(jnp.int32, (16, 1024), 0) == 0).astype(F32)
     key_heads = jnp.where(own_head, jnp.concatenate([coef_ref[frame, 1]] * HEADS, axis=0), 0.0).astype(BF)
     pair = dot_nt(key_heads, coef_ref[frame, 0].astype(BF)) * scale
-    mine = own_ref[0:16] * own_ref[32:33]
-    own = jnp.concatenate([mine[:, 64 * frame : 64 * (frame + 1)], one_row], axis=0)
+    own = jnp.concatenate([own_ref[:, 64 * frame : 64 * (frame + 1)], one_row], axis=0)
     own_high, own_low = split(own)
     pair_high, pair_low = split(pair)
     reduced = dot_nn(
@@ -171,14 +171,6 @@
     mix_ref[...] = dot_tn(part_ref[...].astype(BF), value_heads).astype(BF)
 
 
-def lay_kernel(after_ref, source_ref, out_ref):
-    out_ref[...] = source_ref[...]
-
-
-def gate_kernel(after_ref, held_ref, passed_ref):
-    pass
-
-
 def y_order(me):
     return [me, lax.rem(me + 12, 16), lax.rem(me + 4, 16), lax.rem(me + 8, 16)]
 
@@ -206,14 +198,15 @@
 
 
 def temporal_kernel(advance_ref, *refs):
-    sources, outs, (held_ref, sems) = refs[:4], refs[12:16], refs[16:]
+    sources, outs, (held_ref, sems) = refs[:4], refs[12:14], refs[14:]
     copies = [
         pltpu.make_async_copy(source, held_ref.at[place], sems.at[place]) for place, source in enumerate(sources)
     ]
     for copy in copies:
         copy.start()
-    tokens = jnp.concatenate([one[...] for one in refs[4:8]], axis=1)
-    following = jnp.concatenate([one[...] for one in refs[8:12]], axis=1)
+    arrived = [one[...] for one in refs[4:12]]
+    following = jnp.concatenate(arrived[2:4] + arrived[0:2], axis=1)
+    tokens = jnp.concatenate(arrived[6:8] + arrived[4:6], axis=1)
     last = lax.axis_index("queue") == lax.axis_size("queue") - 1
     limit = jnp.where(last, 0, advance_ref[0])
     frame = lax.broadcasted_iota(jnp.int32, (1, 128), 1) // 64
@@ -222,12 +215,12 @@
     scale = math.log2(math.e) / math.sqrt(HD)
     for place, copy in enumerate(copies):
         copy.wait()
-        block = held_ref[place]
+        block = held_ref[place, 0 : 3 * HD]
         both = dot_nn(block, tokens)
         ahead = dot_nn(block[HD : 3 * HD], following)
         query, key, value = (both[HD * index : HD * (index + 1)] for index in range(3))
         key_next, value_next = ahead[0:HD], ahead[HD : 2 * HD]
-        for side, out_ref in enumerate(outs):
+        for side in range(4):
             lanes = slice(128 * side, 128 * (side + 1))
             asked = query[:, lanes] * scale
             keys = [key[:, lanes], key_next[:, lanes]]
@@ -241,19 +234,33 @@
             weights = [jnp.exp2(one - top) for one in scores]
             inverse = 1.0 / (weights[0] + weights[1] + weights[2] + weights[3])
             mixed = sum(w * inverse * v for w, v in zip(weights, values))
-            out_ref[HD * place : HD * (place + 1), :] = mixed.astype(BF)
-
-
-def final_kernel(hidden_ref, latents_ref, mod_ref, final_ref, *rest):
-    mixes, blocks, (velocity_ref, updated_ref, mix_ref, update_ref) = rest[0:4], rest[4:6], rest[6:]
+            outs[side // 2][HD * place : HD * (place + 1), 128 * (side % 2) : 128 * (side % 2 + 1)] = mixed.astype(BF)
+
+
+def pair_order(me):
+    return [index for pair in zip(y_order(me), y_order(me ^ 2)) for index in pair]
+
+
+def output_kernel(near_ref, across_ref, near_peer_ref, across_peer_ref, *refs):
+    blocks, (own_ref, peer_ref, mix_ref) = refs[:4], refs[4:]
     me = lax.axis_index("seq")
-    for flip, part in enumerate(mixes):
+    for flip, part in ((0, near_ref), (2, across_ref)):
         place_rows(mix_ref, part[...].astype(F32), y_order(me ^ flip))
+    for flip, part in ((1, near_peer_ref), (3, across_peer_ref)):
+        value = part[...].astype(F32)
+        place_rows(mix_ref, jnp.concatenate([value[:, 128:256], value[:, 0:128]], axis=1), y_order(me ^ flip))
     mix = mix_ref[...].astype(BF)
-    for flip, block in enumerate(blocks):
-        at = lax.rem(me ^ flip, 4)
-        order = [4 * place + (at ^ side) for place in range(4) for side in (0, 2)]
-        place_rows(update_ref, dot_nn(block[...], mix), order)
+    for place, block in enumerate(blocks):
+        product = dot_nn(block[3 * HD : 5 * HD], mix)
+        rows = slice(2 * HD * place, 2 * HD * (place + 1))
+        own_ref[rows, :] = product[:, 0:128]
+        peer_ref[rows, :] = product[:, 128:256]
+
+
+def final_kernel(own_ref, peer_ref, hidden_ref, latents_ref, mod_ref, final_ref, velocity_ref, updated_ref, update_ref):
+    me = lax.axis_index("seq")
+    place_rows(update_ref, own_ref[...], pair_order(me))
+    place_rows(update_ref, peer_ref[...], pair_order(me ^ 1))
     gate, shift, scale = modulation_columns(mod_ref[...], (5, 6, 7))
     hidden = hidden_ref[...] + gate * update_ref[...]
     inner = (normalize(hidden) * (1.0 + scale) + shift).astype(BF)
@@ -317,16 +324,11 @@
     )(after, *blocks)
 
 
-def gate(held, after, name):
-    return pl.pallas_call(
-        gate_kernel,
-        out_shape=jax.ShapeDtypeStruct(held.shape, held.dtype),
-        in_specs=[ANY, ANY],
-        out_specs=ANY,
-        input_output_aliases={1: 0},
-        cost_estimate=takes(0.2),
-        name=name,
-    )(after, held)
+def gate(held, *rows):
+    there = rows[0].astype(F32) <= 3e38
+    for row in rows[1:]:
+        there = there & (row.astype(F32) <= 3e38)
+    return jnp.where(there, held, jnp.zeros_like(held))
 
 
 def shards(
@@ -345,48 +347,35 @@
     lat = latents.transpose(0, 2, 1)
     spatial_w = spatial_qkv.transpose(1, 0, 2)
     out_w = spatial_out.transpose(1, 0)
-    temporal_w = temporal_qkv.transpose(1, 2, 0).reshape(3 * HD, D)
+    temporal_w = temporal_qkv.transpose(1, 2, 0)
     last_w = temporal_out.transpose(1, 0)
     final_t = final_w.transpose(1, 0)
 
-    packed = pl.pallas_call(
+    with jax.named_scope("last_x"):
+        last_across = over_x(last_w)
+    packed, scaled = pl.pallas_call(
         pack_kernel,
-        out_shape=jax.ShapeDtypeStruct((16, 40, 128), F32),
-        in_specs=[SMEM, VMEM, VMEM, VMEM],
-        out_specs=VMEM,
+        out_shape=(
+            jax.ShapeDtypeStruct((16, 40, 128), F32),
+            jax.ShapeDtypeStruct((16, 128), F32),
+        ),
+        in_specs=[SMEM, VMEM, VMEM, VMEM, ANY],
+        out_specs=(VMEM, VMEM),
         cost_estimate=takes(2),
         name="pack",
-    )(levels, lat, embed_w, level_mod)
+    )(levels, lat, embed_w, level_mod, last_across)
     everyone = lax.all_to_all(packed, "seq", split_axis=0, concat_axis=0, tiled=True)
     with jax.named_scope("out_y"):
-        out_own = jnp.stack([out_w, y_up(out_w), y_down(out_w), y_far(out_w)])
+        out_far = y_far(out_w)
+        out_own = jnp.stack([out_w, y_up(out_w), y_down(out_w), out_far])
     with jax.named_scope("out_x"):
         out_across = over_x(out_own)
     with jax.named_scope("out_core"):
         out_peer = other_core(out_own)
-    qkv_copy = pl.pallas_call(
-        lay_kernel,
-        out_shape=jax.ShapeDtypeStruct((3 * HD, D), BF),
-        in_specs=[ANY, VMEM],
-        out_specs=VMEM,
-        cost_estimate=takes(1.5),
-        name="lay",
-    )(out_own, temporal_w)
-    with jax.named_scope("qkv_y"):
-        below, above, far = y_up(qkv_copy), y_down(qkv_copy), y_far(qkv_copy)
-    with jax.named_scope("last_x"):
-        last_pair = jnp.stack([last_w, over_x(last_w)])
-    last_held = gate(last_pair, far, "gate_pair")
-    with jax.named_scope("last_y"):
-        rings = [[4 * y + i for y in range(4)] for i in range(4)]
-        last_own = lax.all_to_all(
-            jnp.broadcast_to(last_held[None], (4, 2, HD, D)),
-            "seq",
-            split_axis=0,
-            concat_axis=0,
-            tiled=True,
-            axis_index_groups=rings,
-        )
+    five = lax.dynamic_update_slice(jnp.zeros((5, HD, D), BF), gate(temporal_w, out_far[0]), (0, 0, 0))
+    five = lax.dynamic_update_slice(five, jnp.stack([last_w, last_across]), (3, 0, 0))
+    with jax.named_scope("five_y"):
+        below, above, far = y_up(five), y_down(five), y_far(five)
 
     coef, mod, tokens = pl.pallas_call(
         coefficient_kernel,
@@ -416,11 +405,11 @@
             compiler_params=params(24),
             cost_estimate=takes(1),
             name="attend",
-        )(packed[0], tokens, coef, *after)
+        )(scaled, tokens, coef, *after)
 
     first = attend(0)
-    second = attend(1, first, below, above, last_pair)
-    out_across = gate(out_across, second, "gate_out")
+    second = attend(1, first)
+    out_across = gate(out_across, second[0], below[0, 0], above[0, 0])
     with jax.named_scope("out_core"):
         out_both = other_core(out_across)
 
@@ -445,34 +434,45 @@
     with jax.named_scope("inner_core"):
         tokens_four = [inner, other_core(inner), across, other_core(across)]
         following_four = [following, other_core(following), following_across, other_core(following_across)]
+    blocks = [one.reshape(5 * HD, D) for one in (five, below, above, far)]
     parts = pl.pallas_call(
         temporal_kernel,
-        out_shape=(jax.ShapeDtypeStruct((4 * HD, 128), BF),) * 4,
+        out_shape=(jax.ShapeDtypeStruct((4 * HD, 256), BF),) * 2,
         in_specs=[SMEM] + [ANY] * 4 + [VMEM] * 8,
-        out_specs=(VMEM,) * 4,
-        scratch_shapes=[pltpu.VMEM((4, 3 * HD, D), BF), pltpu.SemaphoreType.DMA((4,))],
+        out_specs=(VMEM,) * 2,
+        scratch_shapes=[pltpu.VMEM((4, 5 * HD, D), BF), pltpu.SemaphoreType.DMA((4,))],
         compiler_params=params(48),
         cost_estimate=takes(4),
         name="temporal",
-    )(advance, qkv_copy, below, above, far, *tokens_four, *following_four)
-    last_own = gate(last_own, parts[0], "gate_last")
-    with jax.named_scope("last_core"):
-        last_all = [one.reshape(8 * HD, D) for one in (last_own, other_core(last_own))]
+    )(advance, *blocks, *following_four[2:], *following_four[:2], *tokens_four[2:], *tokens_four[:2])
     with jax.named_scope("back"):
-        mix_all = [parts[0], other_core(parts[1]), over_x(parts[2]), over_both(parts[3])]
+        near, across = parts[0], over_x(parts[1])
+        near_peer, across_peer = other_core(near), other_core(across)
+    update_own, update_peer = pl.pallas_call(
+        output_kernel,
+        out_shape=(jax.ShapeDtypeStruct((8 * HD, 128), F32),) * 2,
+        in_specs=[VMEM] * 8,
+        out_specs=(VMEM,) * 2,
+        scratch_shapes=[pltpu.VMEM((D, 256), F32)],
+        compiler_params=params(24),
+        cost_estimate=takes(1),
+        name="output",
+    )(near, across, near_peer, across_peer, *blocks)
+    with jax.named_scope("update"):
+        update_peer = other_core(update_peer)
     velocity, updated = pl.pallas_call(
         final_kernel,
         out_shape=(
             jax.ShapeDtypeStruct((2, C, 64), F32),
             jax.ShapeDtypeStruct((2, C, 64), F32),
         ),
-        in_specs=[VMEM] * 10,
+        in_specs=[VMEM] * 6,
         out_specs=(VMEM, VMEM),
-        scratch_shapes=[pltpu.VMEM((D, 128), F32), pltpu.VMEM((D, 128), F32)],
+        scratch_shapes=[pltpu.VMEM((D, 128), F32)],
         compiler_params=params(24),
-        cost_estimate=takes(2.4),
+        cost_estimate=takes(2),
         name="final",
-    )(hidden, lat, mod, final_t, *mix_all, *last_all)
+    )(update_own, update_peer, hidden, lat, mod, final_t)
     incoming = from_next(updated[0])
     is_last = lax.axis_index("queue") == lax.axis_size("queue") - 1
     tail = jnp.where(is_last, fresh_noise.transpose(1, 0), incoming)

time: 108 us -> 101 us (0.935)
  local copies, waits for them, and re-layouts: 16.2 us -> 2.16 us
  waiting for transfers between devices: 17.2 us -> 27.1 us
  Pallas kernels: 25.5 us -> 23 us
  other arithmetic: 2.52 us -> 4.25 us
  starting transfers between devices: 43.7 us -> 42.1 us
    unnamed x68 -> x18, local copies, waits for them, and re-layouts: 13.3 us -> 2.15 us
    ppermute x19, waiting for transfers between devices: 8.7 us -> 17.3 us  [along_seq(): return lax.ppermute(array, 'seq', [(i, to(i)) for i in range(16)])]
    ppermute x2, waiting for transfers between devices: 1.34 us -> 6.9 us  [from_next(): return lax.ppermute(array, 'queue', [(i, i - 1) for i in range(1, 16)])]
    all_to_all x1 -> x0, waiting for transfers between devices: 5.36 us -> none  [shards(): lax.all_to_all(jnp.broadcast_to(last_held[None], (4, 2, HD, D)), 'seq', s...]
    ppermute x1, starting transfers between devices: 3.7 us -> 8.62 us  [shards(): following_across = lax.ppermute(inner, ('queue', 'seq'), pairs)]
    all_to_all x1 -> x0, starting transfers between devices: 3.67 us -> none  [shards(): lax.all_to_all(jnp.broadcast_to(last_held[None], (4, 2, HD, D)), 'seq', s...]
    ppermute x2, starting transfers between devices: 12.8 us -> 10.5 us  [from_next(): return lax.ppermute(array, 'queue', [(i, i - 1) for i in range(1, 16)])]
    broadcast_in_dim x1 -> x0, local copies, waits for them, and re-layouts: 2.16 us -> none  [shards(): jnp.broadcast_to(last_held[None], (4, 2, HD, D))]
  transfers between devices with their start and end apart: 24 -> 23, of which waited for: 11 -> 12; matrix products, arithmetic and copies ran while one was open for 4% -> 4% of each run, Pallas kernels for 22% -> 17%
where the time goes in v3:
time: 101 us; the launch traced here: 100 us
  starting transfers between devices  42.1 us (42%)
  waiting for transfers between devices  27.1 us (27%)
  Pallas kernels  23 us (23%)
  other arithmetic  4.25 us (4%)
  local copies, waits for them, and re-layouts  2.16 us (2%)
  between operations  1.52 us (2%)
    ppermute x19, starting transfers between devices, along_seq(): return lax.ppermute(array, 'seq', [(i, to(i)) for i in range(16)])  17.7 us
    ppermute x19, waiting for transfers between devices, along_seq(): return lax.ppermute(array, 'seq', [(i, to(i)) for i in range(16)])  17.3 us
    ppermute x2, starting transfers between devices, from_next(): return lax.ppermute(array, 'queue', [(i, i - 1) for i in range(1, 16)])  10.5 us
    ppermute x1, starting transfers between devices, shards(): following_across = lax.ppermute(inner, ('queue', 'seq'), pairs)  8.62 us
    pallas_call x2, Pallas kernels, attend(): pl.pallas_call(functools.partial(attend_kernel, frame), out_shape=jax.Sha...  8.13 us
    ppermute x2, waiting for transfers between devices, from_next(): return lax.ppermute(array, 'queue', [(i, i - 1) for i in range(1, 16)])  6.9 us
    all_to_all x1, starting transfers between devices, shards(): lax.all_to_all(packed, 'seq', split_axis=0, concat_axis=0, tiled=True)  5.27 us
    pallas_call x1, Pallas kernels, shards(): pl.pallas_call(coefficient_kernel, out_shape=(jax.ShapeDtypeStruct((2, 3,...  4.01 us
  transfers between devices with their start and end apart: 23, of which 12 were waited for; matrix products, arithmetic and copies ran while one was open for 4% of the time, Pallas kernels for 17%

profile of v3, /device:TPU:2, one launch (start us, length us, event | category | flops | bytes accessed | tf_op | source)
XLA Modules:
  0.0 100.1 jit_solution(2048754865708364767)
XLA Ops:
  0.7 2.2 %collective-permute-start.1 = (bf16[72,1152]{1,0:T(8,128)(2,1)}, bf16[72,1152]{1,0:T(8,128)(2,1)S(1)}, u32[]{:S(2)}, u32[]{:S(2)}) collective-permute-start(bf16[72,1152]{1,0:T(8,128)(2,1)} %bitcast.50), channel_id=1, source_target_pairs={{0,2},{1,3},{2,0},{3,1},{4,6},{5,7},{6,4},{7,5},{8,10},{9,11},{10,... | collective-permute-start | bytes 497672 | tf_op jit(solution)/shard_map/last_x/ppermute | solution.py:285
  2.9 3.2 %collective-permute-start = (bf16[72,1152]{1,0:T(8,128)(2,1)}, bf16[72,1152]{1,0:T(8,128)(2,1)S(1)}, u32[]{:S(2)}, u32[]{:S(2)}) collective-permute-start(bf16[72,1152]{1,0:T(8,128)(2,1)} %bitcast.53), channel_id=1, source_target_pairs={{0,8},{1,9},{2,10},{3,11},{4,12},{5,13},{6,14},{7,15},{8,0},{9,1},... | collective-permute-start | bytes 497672 | tf_op jit(solution)/shard_map/out_y/ppermute | solution.py:285
  6.7 2.6 %collective-permute-start.6 = (bf16[72,1152]{1,0:T(8,128)(2,1)}, bf16[72,1152]{1,0:T(8,128)(2,1)}, u32[]{:S(2)}, u32[]{:S(2)}) collective-permute-start(bf16[72,1152]{1,0:T(8,128)(2,1)} %bitcast.55), channel_id=1, source_target_pairs={{0,12},{1,13},{2,14},{3,15},{4,0},{5,1},{6,2},{7,3},{8,4},{9,5},{1... | collective-permute-start | bytes 497672 | tf_op jit(solution)/shard_map/out_y/ppermute | solution.py:285
  10.0 2.1 %pack.1 = (f32[16,40,128]{2,1,0:T(8,128)}, f32[16,128]{1,0:T(8,128)}) custom-call(s32[2]{0:T(128)} %levels_ref.1, f32[2,16,64]{2,1,0:T(8,128)} %bitcast.46, f32[16,1152]{1,0:T(8,128)} %embed_ref.5, f32[32,8,72]{2,1,0:T(8,128)} %table_ref.1, bf16[72,1152]{1,0:T(8,128)(2,1)} %copy-done.7), custom_call_target="tpu_custom_call" | custom-call | flops 2300000000 | bytes 1000 | tf_op jit(solution)/shard_map/pack/pallas_call | solution.py:356
  12.1 5.3 %all-to-all-start = ((f32[16,40,128]{2,1,0:T(8,128)}), f32[16,40,128]{2,1,0:T(8,128)S(1)}, u32[]{:S(2)}, u32[]{:S(2)}) async-start(f32[16,40,128]{2,1,0:T(8,128)} %get-tuple-element.16), calls=%async_computation | async-start | bytes 655360 | tf_op jit(solution)/shard_map/all_to_all | solution.py:367
  18.1 1.0 %pad_maximum_fusion = bf16[5,72,1152]{2,1,0:T(8,128)(2,1)S(1)} fusion(bf16[1,72,1152]{2,1,0:T(8,128)(2,1)} %bitcast.52, bf16[1,72,1152]{2,1,0:T(8,128)(2,1)S(1)} %bitcast.51, bf16[3,72,1152]{2,1,0:T(8,128)(2,1)S(1)} %select_bitcast_fusion), kind=kLoop, calls=%fused_computation | loop fusion | flops 829440 | bytes 1658880 | tf_op jit(solution)/shard_map/dynamic_update_slice | solution.py:376
  19.1 3.2 %collective-permute-start.3 = (bf16[5,72,1152]{2,1,0:T(8,128)(2,1)S(1)}, bf16[5,72,1152]{2,1,0:T(8,128)(2,1)S(1)}, u32[]{:S(2)}, u32[]{:S(2)}) collective-permute-start(bf16[5,72,1152]{2,1,0:T(8,128)(2,1)S(1)} %pad_maximum_fusion), channel_id=1, source_target_pairs={{0,12},{1,13},{2,14},{3,15},{4,0},{5,1},{6,2},{7,3},{8,4},{9,5},{1... | collective-permute-start | bytes 2488328 | tf_op jit(solution)/shard_map/five_y/ppermute | solution.py:285
  22.3 1.3 %pad_maximum_fusion.1 = bf16[4,72,1152]{2,1,0:T(8,128)(2,1)S(1)} fusion(bf16[1,72,1152]{2,1,0:T(8,128)(2,1)} %bitcast.49, bf16[1,72,1152]{2,1,0:T(8,128)(2,1)} %bitcast.13, bf16[1,72,1152]{2,1,0:T(8,128)(2,1)} %bitcast.12, bf16[1,72,1152]{2,1,0:T(8,128)(2,1)} %bitcast.56), kind=kLoop, calls=%fused_computation.1 | loop fusion | flops 995328 | bytes 1327104 | tf_op jit(solution)/shard_map/out_y/stack | solution.py:370
  23.6 3.1 %collective-permute-start.8 = (bf16[4,72,1152]{2,1,0:T(8,128)(2,1)S(1)}, bf16[4,72,1152]{2,1,0:T(8,128)(2,1)}, u32[]{:S(2)}, u32[]{:S(2)}) collective-permute-start(bf16[4,72,1152]{2,1,0:T(8,128)(2,1)S(1)} %pad_maximum_fusion.1), channel_id=1, source_target_pairs={{0,2},{1,3},{2,0},{3,1},{4,6},{5,7},{6,4},{7,5},{8,10},{9,11},{10,... | collective-permute-start | bytes 1990664 | tf_op jit(solution)/shard_map/out_x/ppermute | solution.py:285
  26.7 1.0 %all-to-all-done.all_ref = f32[16,40,128]{2,1,0:T(8,128)S(1)} async-done(((f32[16,40,128]{2,1,0:T(8,128)}), f32[16,40,128]{2,1,0:T(8,128)S(1)}, u32[]{:S(2)}, u32[]{:S(2)}) %all-to-all-start) | async-done | bytes 327712 | tf_op jit(solution)/shard_map/all_to_all | solution.py:367
  28.6 4.0 %coefficients.1 = (f32[2,3,32,1152]{3,2,1,0:T(8,128)S(1)}, f32[16,1152]{1,0:T(8,128)S(1)}, f32[2,16,1024]{2,1,0:T(8,128)S(1)}) custom-call(f32[16,40,128]{2,1,0:T(8,128)S(1)} %all-to-all-done.all_ref, f32[16,1152]{1,0:T(8,128)S(1)} %copy-done, bf16[3,1152,1152]{2,1,0:T(8,128)(2,1)} %bitcast.57), custom_call_target="tpu_custom_call" | custom-call | flops 23000000512 | bytes 1000 | tf_op jit(solution)/shard_map/coefficients/pallas_call | solution.py:380
  32.6 4.1 %attend.2.refs_0_.first_ref = bf16[64,1152]{1,0:T(8,128)(2,1)S(1)} custom-call(f32[16,128]{1,0:T(8,128)S(1)} %copy-done.3, f32[2,16,1024]{2,1,0:T(8,128)S(1)} %get-tuple-element.17.tokens_ref, f32[2,3,32,1152]{3,2,1,0:T(8,128)S(1)} %get-tuple-element.18.coef_ref), custom_call_target="tpu_custom_call" | custom-call | flops 1150000000 | bytes 1000 | tf_op jit(solution)/shard_map/attend/pallas_call | solution.py:396
  36.7 4.1 %attend.3.second_ref = bf16[64,1152]{1,0:T(8,128)(2,1)S(1)} custom-call(f32[16,128]{1,0:T(8,128)S(1)} %copy-done.3, f32[2,16,1024]{2,1,0:T(8,128)S(1)} %get-tuple-element.17.tokens_ref, f32[2,3,32,1152]{3,2,1,0:T(8,128)S(1)} %get-tuple-element.18.coef_ref, bf16[64,1152]{1,0:T(8,128)(2,1)S(1)} %attend.2.refs_0_.first_ref), custom_call_target="tpu_custom_call" | custom-call | flops 1150000000 | bytes 1000 | tf_op jit(solution)/shard_map/attend/pallas_call | solution.py:396
  40.8 1.0 %collective-permute-done.3 = bf16[5,72,1152]{2,1,0:T(8,128)(2,1)S(1)} collective-permute-done((bf16[5,72,1152]{2,1,0:T(8,128)(2,1)S(1)}, bf16[5,72,1152]{2,1,0:T(8,128)(2,1)S(1)}, u32[]{:S(2)}, u32[]{:S(2)}) %collective-permute-start.3) | collective-permute-done | bytes 829472 | tf_op jit(solution)/shard_map/five_y/ppermute | solution.py:285
  41.8 2.9 %collective-permute-done.2 = bf16[5,72,1152]{2,1,0:T(8,128)(2,1)S(1)} collective-permute-done((bf16[5,72,1152]{2,1,0:T(8,128)(2,1)S(1)}, bf16[5,72,1152]{2,1,0:T(8,128)(2,1)S(1)}, u32[]{:S(2)}, u32[]{:S(2)}) %collective-permute-start.2) | collective-permute-done | bytes 829472 | tf_op jit(solution)/shard_map/five_y/ppermute | solution.py:285
  44.7 1.2 %broadcast_select_fusion = bf16[4,72,1152]{2,1,0:T(8,128)(2,1)S(1)} fusion(bf16[4,72,1152]{2,1,0:T(8,128)(2,1)} %collective-permute-done.8, pred[1152]{0:T(1024)(128)(4,1)S(1)} %and_and_fusion), kind=kLoop, calls=%fused_computation.2 | loop fusion | flops 331776 | bytes 1328256 | tf_op jit(solution)/shard_map/jit(_where)/select_n | solution.py:331
  46.3 1.8 %collective-permute-done.9 = bf16[4,72,1152]{2,1,0:T(8,128)(2,1)S(1)} collective-permute-done((bf16[4,72,1152]{2,1,0:T(8,128)(2,1)S(1)}, bf16[4,72,1152]{2,1,0:T(8,128)(2,1)S(1)}, u32[]{:S(2)}, u32[]{:S(2)}) %collective-permute-start.9) | collective-permute-done | bytes 663584 | tf_op jit(solution)/shard_map/out_core/ppermute | solution.py:285
  48.1 2.6 %hidden.1 = (f32[1152,128]{1,0:T(8,128)S(1)}, bf16[1152,128]{1,0:T(8,128)(2,1)S(1)}) custom-call(bf16[64,1152]{1,0:T(8,128)(2,1)S(1)} %attend.2.refs_0_.first_ref, bf16[64,1152]{1,0:T(8,128)(2,1)S(1)} %attend.3.second_ref, f32[2,16,64]{2,1,0:T(8,128)S(1)} %bitcast.47, f32[16,1152]{1,0:T(8,128)S(1)} %copy-done, f32[16,1152]{1,0:T(8,128)S(1)} %get-tuple-element.19.mod_ref, ...), custom_call_target="tpu_custom_call" | custom-call | flops 2300000000 | bytes 1000 | tf_op jit(solution)/shard_map/hidden/pallas_call | solution.py:416
  50.7 8.6 %collective-permute-start.10 = (bf16[1152,128]{1,0:T(8,128)(2,1)S(1)}, bf16[1152,128]{1,0:T(8,128)(2,1)S(1)}, u32[]{:S(2)}, u32[]{:S(2)}) collective-permute-start(bf16[1152,128]{1,0:T(8,128)(2,1)S(1)} %get-tuple-element.20.refs_10_), channel_id=1, source_target_pairs={{16,2},{17,3},{18,0},{19,1},{20,6},{21,7},{22,4},{23,5},{24,10},{2... | collective-permute-start | bytes 884744 | tf_op jit(solution)/shard_map/inner/ppermute | solution.py:431
  59.3 4.4 %collective-permute-start.12 = (bf16[1152,128]{1,0:T(8,128)(2,1)S(1)}, bf16[1152,128]{1,0:T(8,128)(2,1)S(1)}, u32[]{:S(2)}, u32[]{:S(2)}) collective-permute-start(bf16[1152,128]{1,0:T(8,128)(2,1)S(1)} %get-tuple-element.20.refs_10_), channel_id=1, source_target_pairs={{16,0},{32,16},{48,32},{64,48},{80,64},{96,80},{112,96},{128,112},... | collective-permute-start | bytes 884744 | tf_op jit(solution)/shard_map/inner/ppermute | solution.py:305
  63.8 1.0 collective-permute-start.14
  64.7 2.0 %collective-permute-done.10.refs_4_ = bf16[1152,128]{1,0:T(8,128)(2,1)S(1)} collective-permute-done((bf16[1152,128]{1,0:T(8,128)(2,1)S(1)}, bf16[1152,128]{1,0:T(8,128)(2,1)S(1)}, u32[]{:S(2)}, u32[]{:S(2)}) %collective-permute-start.10) | collective-permute-done | bytes 294944 | tf_op jit(solution)/shard_map/inner/ppermute | solution.py:431
  66.7 5.6 %collective-permute-done.12.refs_6_ = bf16[1152,128]{1,0:T(8,128)(2,1)S(1)} collective-permute-done((bf16[1152,128]{1,0:T(8,128)(2,1)S(1)}, bf16[1152,128]{1,0:T(8,128)(2,1)S(1)}, u32[]{:S(2)}, u32[]{:S(2)}) %collective-permute-start.12) | collective-permute-done | bytes 294944 | tf_op jit(solution)/shard_map/inner/ppermute | solution.py:305
  72.3 1.6 %collective-permute-done.14.refs_8_ = bf16[1152,128]{1,0:T(8,128)(2,1)S(1)} collective-permute-done((bf16[1152,128]{1,0:T(8,128)(2,1)S(1)}, bf16[1152,128]{1,0:T(8,128)(2,1)S(1)}, u32[]{:S(2)}, u32[]{:S(2)}) %collective-permute-start.14) | collective-permute-done | bytes 294944 | tf_op jit(solution)/shard_map/inner/ppermute | solution.py:285
  75.4 3.8 %temporal.1 = (bf16[288,256]{1,0:T(8,128)(2,1)S(1)}, bf16[288,256]{1,0:T(8,128)(2,1)S(1)}) custom-call(s32[1]{0:T(128)S(6)} %copy.13.advance_ref, bf16[360,1152]{1,0:T(8,128)(2,1)S(1)} %bitcast.34, bf16[360,1152]{1,0:T(8,128)(2,1)S(1)} %bitcast.40, bf16[360,1152]{1,0:T(8,128)(2,1)S(1)} %bitcast.38, bf16[360,1152]{1,0:T(8,128)(2,1)S(1)} %bitcast.42, ...), custom_call_target="tpu_custom_call" | custom-call | flops 4600000000 | bytes 1000 | tf_op jit(solution)/shard_map/temporal/pallas_call | solution.py:438
  79.2 1.1 %collective-permute-start.17 = (bf16[288,256]{1,0:T(8,128)(2,1)S(1)}, bf16[288,256]{1,0:T(8,128)(2,1)S(1)}, u32[]{:S(2)}, u32[]{:S(2)}) collective-permute-start(bf16[288,256]{1,0:T(8,128)(2,1)S(1)} %get-tuple-element.22), channel_id=1, source_target_pairs={{0,2},{1,3},{2,0},{3,1},{4,6},{5,7},{6,4},{7,5},{8,10},{9,11},{10,... | collective-permute-start | bytes 442376 | tf_op jit(solution)/shard_map/back/ppermute | solution.py:285
  80.4 6.3 %collective-permute-done.17.across_ref = bf16[288,256]{1,0:T(8,128)(2,1)S(1)} collective-permute-done((bf16[288,256]{1,0:T(8,128)(2,1)S(1)}, bf16[288,256]{1,0:T(8,128)(2,1)S(1)}, u32[]{:S(2)}, u32[]{:S(2)}) %collective-permute-start.17) | collective-permute-done | bytes 147488 | tf_op jit(solution)/shard_map/back/ppermute | solution.py:285
  86.7 1.4 %collective-permute-done.19.across_peer_ref = bf16[288,256]{1,0:T(8,128)(2,1)S(1)} collective-permute-done((bf16[288,256]{1,0:T(8,128)(2,1)S(1)}, bf16[288,256]{1,0:T(8,128)(2,1)S(1)}, u32[]{:S(2)}, u32[]{:S(2)}) %collective-permute-start.19) | collective-permute-done | bytes 147488 | tf_op jit(solution)/shard_map/back/ppermute | solution.py:285
  89.0 1.4 %collective-permute-done.20.peer_ref = f32[576,128]{1,0:T(8,128)S(1)} collective-permute-done((f32[576,128]{1,0:T(8,128)S(1)}, f32[576,128]{1,0:T(8,128)S(1)}, u32[]{:S(2)}, u32[]{:S(2)}) %collective-permute-start.20) | collective-permute-done | bytes 294944 | tf_op jit(solution)/shard_map/update/ppermute | solution.py:285
  90.4 1.7 %final.1 = (f32[2,16,64]{2,1,0:T(8,128)}, f32[2,16,64]{2,1,0:T(8,128)S(1)}) custom-call(f32[576,128]{1,0:T(8,128)S(1)} %get-tuple-element.23.own_ref, f32[576,128]{1,0:T(8,128)S(1)} %collective-permute-done.20.peer_ref, f32[1152,128]{1,0:T(8,128)S(1)} %get-tuple-element.25.hidden_ref, f32[2,16,64]{2,1,0:T(8,128)S(1)} %bitcast.48, ...), custom_call_target="tpu_custom_call" | custom-call | flops 2300000000 | bytes 1000 | tf_op jit(solution)/shard_map/final/pallas_call | solution.py:463
  92.1 6.1 %collective-permute-start.21 = (f32[16,64]{1,0:T(8,128)S(1)}, f32[16,64]{1,0:T(8,128)S(1)}, u32[]{:S(2)}, u32[]{:S(2)}) collective-permute-start(f32[16,64]{1,0:T(8,128)S(1)} %get-tuple-element.29), channel_id=1, source_target_pairs={{16,0},{32,16},{48,32},{64,48},{80,64},{96,80},{112,96},{128,112},... | collective-permute-start | bytes 12296 | tf_op jit(solution)/shard_map/ppermute | solution.py:305
  98.2 1.3 %collective-permute-done.21 = f32[16,64]{1,0:T(8,128)S(1)} collective-permute-done((f32[16,64]{1,0:T(8,128)S(1)}, f32[16,64]{1,0:T(8,128)S(1)}, u32[]{:S(2)}, u32[]{:S(2)}) %collective-permute-start.21) | collective-permute-done | bytes 4128 | tf_op jit(solution)/shard_map/ppermute | solution.py:305
  (52 shorter events, 5.9 us)
Async XLA Ops:
  0.6 17.4 %copy-start.6 = (bf16[1152,72]{0,1:T(8,128)(2,1)S(1)}, bf16[1152,72]{0,1:T(8,128)(2,1)}, u32[]{:S(2)}) copy-start(bf16[1152,72]{0,1:T(8,128)(2,1)} %param.20) | copy-start | bytes 497668
  0.6 16.8 %copy-start.4 = (bf16[1152,3,72]{0,2,1:T(8,128)(2,1)S(1)}, bf16[1152,3,72]{0,2,1:T(8,128)(2,1)}, u32[]{:S(2)}) copy-start(bf16[1152,3,72]{0,2,1:T(8,128)(2,1)} %param.19) | copy-start | bytes 1492996
  0.7 8.6 %collective-permute-start.1 = (bf16[72,1152]{1,0:T(8,128)(2,1)}, bf16[72,1152]{1,0:T(8,128)(2,1)S(1)}, u32[]{:S(2)}, u32[]{:S(2)}) collective-permute-start(bf16[72,1152]{1,0:T(8,128)(2,1)} %bitcast.50), channel_id=1, source_target_pairs={{0,2},{1,3},{2,0},{3,1},{4,6},{5,7},{6,4},{7,5},{8,10},{9,11},{10,... | collective-permute-start | bytes 497672 | tf_op jit(solution)/shard_map/last_x/ppermute | solution.py:285
  2.9 14.5 %collective-permute-start = (bf16[72,1152]{1,0:T(8,128)(2,1)}, bf16[72,1152]{1,0:T(8,128)(2,1)S(1)}, u32[]{:S(2)}, u32[]{:S(2)}) collective-permute-start(bf16[72,1152]{1,0:T(8,128)(2,1)} %bitcast.53), channel_id=1, source_target_pairs={{0,8},{1,9},{2,10},{3,11},{4,12},{5,13},{6,14},{7,15},{8,0},{9,1},... | collective-permute-start | bytes 497672 | tf_op jit(solution)/shard_map/out_y/ppermute | solution.py:285
  6.1 16.3 %collective-permute-start.5 = (bf16[72,1152]{1,0:T(8,128)(2,1)}, bf16[72,1152]{1,0:T(8,128)(2,1)}, u32[]{:S(2)}, u32[]{:S(2)}) collective-permute-start(bf16[72,1152]{1,0:T(8,128)(2,1)} %bitcast.54), channel_id=1, source_target_pairs={{0,4},{1,5},{2,6},{3,7},{4,8},{5,9},{6,10},{7,11},{8,12},{9,13},{1... | collective-permute-start | bytes 497672 | tf_op jit(solution)/shard_map/out_y/ppermute | solution.py:285
  6.7 15.6 %collective-permute-start.6 = (bf16[72,1152]{1,0:T(8,128)(2,1)}, bf16[72,1152]{1,0:T(8,128)(2,1)}, u32[]{:S(2)}, u32[]{:S(2)}) collective-permute-start(bf16[72,1152]{1,0:T(8,128)(2,1)} %bitcast.55), channel_id=1, source_target_pairs={{0,12},{1,13},{2,14},{3,15},{4,0},{5,1},{6,2},{7,3},{8,4},{9,5},{1... | collective-permute-start | bytes 497672 | tf_op jit(solution)/shard_map/out_y/ppermute | solution.py:285
  9.3 0.7 copy-start.7
  12.1 15.6 %all-to-all-start = ((f32[16,40,128]{2,1,0:T(8,128)}), f32[16,40,128]{2,1,0:T(8,128)S(1)}, u32[]{:S(2)}, u32[]{:S(2)}) async-start(f32[16,40,128]{2,1,0:T(8,128)} %get-tuple-element.16), calls=%async_computation | async-start | bytes 655360 | tf_op jit(solution)/shard_map/all_to_all | solution.py:367
  17.4 0.7 copy-start.5
  19.1 22.7 %collective-permute-start.3 = (bf16[5,72,1152]{2,1,0:T(8,128)(2,1)S(1)}, bf16[5,72,1152]{2,1,0:T(8,128)(2,1)S(1)}, u32[]{:S(2)}, u32[]{:S(2)}) collective-permute-start(bf16[5,72,1152]{2,1,0:T(8,128)(2,1)S(1)} %pad_maximum_fusion), channel_id=1, source_target_pairs={{0,12},{1,13},{2,14},{3,15},{4,0},{5,1},{6,2},{7,3},{8,4},{9,5},{1... | collective-permute-start | bytes 2488328 | tf_op jit(solution)/shard_map/five_y/ppermute | solution.py:285
  22.3 22.4 %collective-permute-start.2 = (bf16[5,72,1152]{2,1,0:T(8,128)(2,1)S(1)}, bf16[5,72,1152]{2,1,0:T(8,128)(2,1)S(1)}, u32[]{:S(2)}, u32[]{:S(2)}) collective-permute-start(bf16[5,72,1152]{2,1,0:T(8,128)(2,1)S(1)} %pad_maximum_fusion), channel_id=1, source_target_pairs={{0,4},{1,5},{2,6},{3,7},{4,8},{5,9},{6,10},{7,11},{8,12},{9,13},{1... | collective-permute-start | bytes 2488328 | tf_op jit(solution)/shard_map/five_y/ppermute | solution.py:285
  23.6 21.1 %collective-permute-start.8 = (bf16[4,72,1152]{2,1,0:T(8,128)(2,1)S(1)}, bf16[4,72,1152]{2,1,0:T(8,128)(2,1)}, u32[]{:S(2)}, u32[]{:S(2)}) collective-permute-start(bf16[4,72,1152]{2,1,0:T(8,128)(2,1)S(1)} %pad_maximum_fusion.1), channel_id=1, source_target_pairs={{0,2},{1,3},{2,0},{3,1},{4,6},{5,7},{6,4},{7,5},{8,10},{9,11},{10,... | collective-permute-start | bytes 1990664 | tf_op jit(solution)/shard_map/out_x/ppermute | solution.py:285
  26.7 19.7 %collective-permute-start.7 = (bf16[4,72,1152]{2,1,0:T(8,128)(2,1)S(1)}, bf16[4,72,1152]{2,1,0:T(8,128)(2,1)}, u32[]{:S(2)}, u32[]{:S(2)}) collective-permute-start(bf16[4,72,1152]{2,1,0:T(8,128)(2,1)S(1)} %pad_maximum_fusion.1), channel_id=1, source_target_pairs={{0,1},{1,0},{2,3},{3,2},{4,5},{5,4},{6,7},{7,6},{8,9},{9,8},{10,11... | collective-permute-start | bytes 1990664 | tf_op jit(solution)/shard_map/out_core/ppermute | solution.py:285
  27.7 0.9 copy-start
  28.6 4.0 %copy-start.3 = (f32[16,128]{1,0:T(8,128)S(1)}, f32[16,128]{1,0:T(8,128)}, u32[]{:S(2)}) copy-start(f32[16,128]{1,0:T(8,128)} %get-tuple-element.15.own_ref) | copy-start | bytes 24580
  32.6 15.5 %copy-start.2 = (f32[2,64,16]{1,2,0:T(8,128)S(1)}, f32[2,64,16]{1,2,0:T(8,128)}, u32[]{:S(2)}) copy-start(f32[2,64,16]{1,2,0:T(8,128)} %param.11) | copy-start | bytes 24580
  45.9 2.2 %collective-permute-start.9 = (bf16[4,72,1152]{2,1,0:T(8,128)(2,1)S(1)}, bf16[4,72,1152]{2,1,0:T(8,128)(2,1)S(1)}, u32[]{:S(2)}, u32[]{:S(2)}) collective-permute-start(bf16[4,72,1152]{2,1,0:T(8,128)(2,1)S(1)} %broadcast_select_fusion), channel_id=1, source_target_pairs={{0,1},{1,0},{2,3},{3,2},{4,5},{5,4},{6,7},{7,6},{8,9},{9,8},{10,11... | collective-permute-start | bytes 1990664 | tf_op jit(solution)/shard_map/out_core/ppermute | solution.py:285
  46.0 28.5 %collective-permute-start.4 = (bf16[5,72,1152]{2,1,0:T(8,128)(2,1)S(1)}, bf16[5,72,1152]{2,1,0:T(8,128)(2,1)S(1)}, u32[]{:S(2)}, u32[]{:S(2)}) collective-permute-start(bf16[5,72,1152]{2,1,0:T(8,128)(2,1)S(1)} %pad_maximum_fusion), channel_id=1, source_target_pairs={{0,8},{1,9},{2,10},{3,11},{4,12},{5,13},{6,14},{7,15},{8,0},{9,1},... | collective-permute-start | bytes 2488328 | tf_op jit(solution)/shard_map/five_y/ppermute | solution.py:285
  50.7 16.0 %collective-permute-start.10 = (bf16[1152,128]{1,0:T(8,128)(2,1)S(1)}, bf16[1152,128]{1,0:T(8,128)(2,1)S(1)}, u32[]{:S(2)}, u32[]{:S(2)}) collective-permute-start(bf16[1152,128]{1,0:T(8,128)(2,1)S(1)} %get-tuple-element.20.refs_10_), channel_id=1, source_target_pairs={{16,2},{17,3},{18,0},{19,1},{20,6},{21,7},{22,4},{23,5},{24,10},{2... | collective-permute-start | bytes 884744 | tf_op jit(solution)/shard_map/inner/ppermute | solution.py:431
  59.3 12.9 %collective-permute-start.12 = (bf16[1152,128]{1,0:T(8,128)(2,1)S(1)}, bf16[1152,128]{1,0:T(8,128)(2,1)S(1)}, u32[]{:S(2)}, u32[]{:S(2)}) collective-permute-start(bf16[1152,128]{1,0:T(8,128)(2,1)S(1)} %get-tuple-element.20.refs_10_), channel_id=1, source_target_pairs={{16,0},{32,16},{48,32},{64,48},{80,64},{96,80},{112,96},{128,112},... | collective-permute-start | bytes 884744 | tf_op jit(solution)/shard_map/inner/ppermute | solution.py:305
  63.8 10.1 %collective-permute-start.14 = (bf16[1152,128]{1,0:T(8,128)(2,1)S(1)}, bf16[1152,128]{1,0:T(8,128)(2,1)S(1)}, u32[]{:S(2)}, u32[]{:S(2)}) collective-permute-start(bf16[1152,128]{1,0:T(8,128)(2,1)S(1)} %get-tuple-element.20.refs_10_), channel_id=1, source_target_pairs={{0,2},{1,3},{2,0},{3,1},{4,6},{5,7},{6,4},{7,5},{8,10},{9,11},{10,... | collective-permute-start | bytes 884744 | tf_op jit(solution)/shard_map/inner/ppermute | solution.py:285
  64.7 9.8 %collective-permute-start.16 = (bf16[1152,128]{1,0:T(8,128)(2,1)S(1)}, bf16[1152,128]{1,0:T(8,128)(2,1)S(1)}, u32[]{:S(2)}, u32[]{:S(2)}) collective-permute-start(bf16[1152,128]{1,0:T(8,128)(2,1)S(1)} %get-tuple-element.20.refs_10_), channel_id=1, source_target_pairs={{0,1},{1,0},{2,3},{3,2},{4,5},{5,4},{6,7},{7,6},{8,9},{9,8},{10,11... | collective-permute-start | bytes 884744 | tf_op jit(solution)/shard_map/inner_core/ppermute | solution.py:285
  66.7 7.8 %collective-permute-start.11 = (bf16[1152,128]{1,0:T(8,128)(2,1)S(1)}, bf16[1152,128]{1,0:T(8,128)(2,1)S(1)}, u32[]{:S(2)}, u32[]{:S(2)}) collective-permute-start(bf16[1152,128]{1,0:T(8,128)(2,1)S(1)} %collective-permute-done.10.refs_4_), channel_id=1, source_target_pairs={{0,1},{1,0},{2,3},{3,2},{4,5},{5,4},{6,7},{7,6},{8,9},{9,8},{10,11... | collective-permute-start | bytes 884744 | tf_op jit(solution)/shard_map/inner_core/ppermute | solution.py:285
  72.3 2.3 %collective-permute-start.13 = (bf16[1152,128]{1,0:T(8,128)(2,1)S(1)}, bf16[1152,128]{1,0:T(8,128)(2,1)S(1)}, u32[]{:S(2)}, u32[]{:S(2)}) collective-permute-start(bf16[1152,128]{1,0:T(8,128)(2,1)S(1)} %collective-permute-done.12.refs_6_), channel_id=1, source_target_pairs={{0,1},{1,0},{2,3},{3,2},{4,5},{5,4},{6,7},{7,6},{8,9},{9,8},{10,11... | collective-permute-start | bytes 884744 | tf_op jit(solution)/shard_map/inner_core/ppermute | solution.py:285
  73.8 1.6 %collective-permute-start.15 = (bf16[1152,128]{1,0:T(8,128)(2,1)S(1)}, bf16[1152,128]{1,0:T(8,128)(2,1)S(1)}, u32[]{:S(2)}, u32[]{:S(2)}) collective-permute-start(bf16[1152,128]{1,0:T(8,128)(2,1)S(1)} %collective-permute-done.14.refs_8_), channel_id=1, source_target_pairs={{0,1},{1,0},{2,3},{3,2},{4,5},{5,4},{6,7},{7,6},{8,9},{9,8},{10,11... | collective-permute-start | bytes 884744 | tf_op jit(solution)/shard_map/inner_core/ppermute | solution.py:285
  75.4 15.0 %copy-start.1 = (bf16[1152,16]{0,1:T(8,128)(2,1)S(1)}, bf16[1152,16]{0,1:T(8,128)(2,1)}, u32[]{:S(2)}) copy-start(bf16[1152,16]{0,1:T(8,128)(2,1)} %param.21) | copy-start | bytes 110596
  79.2 20.3 %copy-start.8 = (f32[64,16]{0,1:T(8,128)S(1)}, f32[64,16]{0,1:T(8,128)}, u32[]{:S(2)}) copy-start(f32[64,16]{0,1:T(8,128)} %param.14) | copy-start | bytes 12292
  79.2 7.5 %collective-permute-start.17 = (bf16[288,256]{1,0:T(8,128)(2,1)S(1)}, bf16[288,256]{1,0:T(8,128)(2,1)S(1)}, u32[]{:S(2)}, u32[]{:S(2)}) collective-permute-start(bf16[288,256]{1,0:T(8,128)(2,1)S(1)} %get-tuple-element.22), channel_id=1, source_target_pairs={{0,2},{1,3},{2,0},{3,1},{4,6},{5,7},{6,4},{7,5},{8,10},{9,11},{10,... | collective-permute-start | bytes 442376 | tf_op jit(solution)/shard_map/back/ppermute | solution.py:285
  80.4 6.3 %collective-permute-start.18 = (bf16[288,256]{1,0:T(8,128)(2,1)S(1)}, bf16[288,256]{1,0:T(8,128)(2,1)S(1)}, u32[]{:S(2)}, u32[]{:S(2)}) collective-permute-start(bf16[288,256]{1,0:T(8,128)(2,1)S(1)} %get-tuple-element.21.near_ref), channel_id=1, source_target_pairs={{0,1},{1,0},{2,3},{3,2},{4,5},{5,4},{6,7},{7,6},{8,9},{9,8},{10,11... | collective-permute-start | bytes 442376 | tf_op jit(solution)/shard_map/back/ppermute | solution.py:285
  86.7 1.4 %collective-permute-start.19 = (bf16[288,256]{1,0:T(8,128)(2,1)S(1)}, bf16[288,256]{1,0:T(8,128)(2,1)S(1)}, u32[]{:S(2)}, u32[]{:S(2)}) collective-permute-start(bf16[288,256]{1,0:T(8,128)(2,1)S(1)} %collective-permute-done.17.across_ref), channel_id=1, source_target_pairs={{0,1},{1,0},{2,3},{3,2},{4,5},{5,4},{6,7},{7,6},{8,9},{9,8},{10,11... | collective-permute-start | bytes 442376 | tf_op jit(solution)/shard_map/back/ppermute | solution.py:285
  88.7 1.7 %collective-permute-start.20 = (f32[576,128]{1,0:T(8,128)S(1)}, f32[576,128]{1,0:T(8,128)S(1)}, u32[]{:S(2)}, u32[]{:S(2)}) collective-permute-start(f32[576,128]{1,0:T(8,128)S(1)} %get-tuple-element.24), channel_id=1, source_target_pairs={{0,1},{1,0},{2,3},{3,2},{4,5},{5,4},{6,7},{7,6},{8,9},{9,8},{10,11... | collective-permute-start | bytes 884744 | tf_op jit(solution)/shard_map/update/ppermute | solution.py:285
  92.1 7.4 %collective-permute-start.21 = (f32[16,64]{1,0:T(8,128)S(1)}, f32[16,64]{1,0:T(8,128)S(1)}, u32[]{:S(2)}, u32[]{:S(2)}) collective-permute-start(f32[16,64]{1,0:T(8,128)S(1)} %get-tuple-element.29), channel_id=1, source_target_pairs={{16,0},{32,16},{48,32},{64,48},{80,64},{96,80},{112,96},{128,112},... | collective-permute-start | bytes 12296 | tf_op jit(solution)/shard_map/ppermute | solution.py:305

commit v4 on v3

--- a/solution.py
+++ b/solution.py
@@ -188,8 +188,9 @@
     *blocks, hidden_ref, inner_ref, update_ref = rest
     mix = jnp.concatenate([first_ref[...], second_ref[...]], axis=0).T
     me = lax.axis_index("seq")
-    for flip, block in enumerate(blocks):
-        place_rows(update_ref, dot_nn(block[...], mix), y_order(me ^ flip))
+    orders = [y_order(me), y_order(me ^ 1), y_order(me ^ 2), y_order(me ^ 3)[:2], y_order(me ^ 3)[2:]]
+    for block, order in zip(blocks, orders):
+        place_rows(update_ref, dot_nn(block[...], mix), order)
     embedded = product_tn(embed_ref[...], both_frames(latents_ref))
     gate, shift, scale = modulation_columns(mod_ref[...], (2, 3, 4))
     hidden = embedded + gate * update_ref[...]
@@ -198,29 +199,22 @@
 
 
 def temporal_kernel(advance_ref, *refs):
-    sources, outs, (held_ref, sems) = refs[:4], refs[12:14], refs[14:]
-    copies = [
-        pltpu.make_async_copy(source, held_ref.at[place], sems.at[place]) for place, source in enumerate(sources)
-    ]
-    for copy in copies:
-        copy.start()
-    arrived = [one[...] for one in refs[4:12]]
-    following = jnp.concatenate(arrived[2:4] + arrived[0:2], axis=1)
-    tokens = jnp.concatenate(arrived[6:8] + arrived[4:6], axis=1)
+    blocks, out_ref = refs[:4], refs[8]
+    following = jnp.concatenate([one[...] for one in refs[4:6]], axis=1)
+    tokens = jnp.concatenate([one[...] for one in refs[6:8]], axis=1)
     last = lax.axis_index("queue") == lax.axis_size("queue") - 1
     limit = jnp.where(last, 0, advance_ref[0])
     frame = lax.broadcasted_iota(jnp.int32, (1, 128), 1) // 64
     keep_same = frame < limit
     keep_other = (1 - frame) < limit
     scale = math.log2(math.e) / math.sqrt(HD)
-    for place, copy in enumerate(copies):
-        copy.wait()
-        block = held_ref[place, 0 : 3 * HD]
+    for place, block_ref in enumerate(blocks):
+        block = block_ref[0 : 3 * HD]
         both = dot_nn(block, tokens)
         ahead = dot_nn(block[HD : 3 * HD], following)
         query, key, value = (both[HD * index : HD * (index + 1)] for index in range(3))
         key_next, value_next = ahead[0:HD], ahead[HD : 2 * HD]
-        for side in range(4):
+        for side in range(2):
             lanes = slice(128 * side, 128 * (side + 1))
             asked = query[:, lanes] * scale
             keys = [key[:, lanes], key_next[:, lanes]]
@@ -234,7 +228,7 @@
             weights = [jnp.exp2(one - top) for one in scores]
             inverse = 1.0 / (weights[0] + weights[1] + weights[2] + weights[3])
             mixed = sum(w * inverse * v for w, v in zip(weights, values))
-            outs[side // 2][HD * place : HD * (place + 1), 128 * (side % 2) : 128 * (side % 2 + 1)] = mixed.astype(BF)
+            out_ref[HD * place : HD * (place + 1), lanes] = mixed.astype(BF)
 
 
 def pair_order(me):
@@ -325,9 +319,9 @@
 
 
 def gate(held, *rows):
-    there = rows[0].astype(F32) <= 3e38
+    there = rows[0].astype(F32) <= jnp.inf
     for row in rows[1:]:
-        there = there & (row.astype(F32) <= 3e38)
+        there = there & (row.astype(F32) <= jnp.inf)
     return jnp.where(there, held, jnp.zeros_like(held))
 
 
@@ -359,7 +353,7 @@
             jax.ShapeDtypeStruct((16, 40, 128), F32),
             jax.ShapeDtypeStruct((16, 128), F32),
         ),
-        in_specs=[SMEM, VMEM, VMEM, VMEM, ANY],
+        in_specs=[SMEM, VMEM, VMEM, VMEM, VMEM],
         out_specs=(VMEM, VMEM),
         cost_estimate=takes(2),
         name="pack",
@@ -375,7 +369,7 @@
     five = lax.dynamic_update_slice(jnp.zeros((5, HD, D), BF), gate(temporal_w, out_far[0]), (0, 0, 0))
     five = lax.dynamic_update_slice(five, jnp.stack([last_w, last_across]), (3, 0, 0))
     with jax.named_scope("five_y"):
-        below, above, far = y_up(five), y_down(five), y_far(five)
+        below, above = y_up(five), y_down(five)
 
     coef, mod, tokens = pl.pallas_call(
         coefficient_kernel,
@@ -387,7 +381,7 @@
         in_specs=[VMEM] * 2 + [ANY],
         out_specs=(VMEM, VMEM, VMEM),
         scratch_shapes=[pltpu.VMEM((3, D, D), BF), pltpu.SemaphoreType.DMA((3, 4))],
-        compiler_params=params(48),
+        compiler_params=params(45),
         cost_estimate=takes(20),
         name="coefficients",
     )(everyone, embed_w, spatial_w)
@@ -403,15 +397,17 @@
                 pltpu.VMEM((HEADS * CP, 64), F32),
             ],
             compiler_params=params(24),
-            cost_estimate=takes(1),
+            cost_estimate=takes(0.1),
             name="attend",
         )(scaled, tokens, coef, *after)
 
     first = attend(0)
     second = attend(1, first)
-    out_across = gate(out_across, second[0], below[0, 0], above[0, 0])
     with jax.named_scope("out_core"):
-        out_both = other_core(out_across)
+        out_both = [other_core(gate(out_across[half : half + 2], second[0])) for half in (0, 2)]
+    first = gate(first, below[0, 0], above[0, 0])
+    with jax.named_scope("five_far"):
+        far = y_far(gate(five, first[0]))
 
     hidden, inner = pl.pallas_call(
         hidden_kernel,
@@ -419,13 +415,13 @@
             jax.ShapeDtypeStruct((D, 128), F32),
             jax.ShapeDtypeStruct((D, 128), BF),
         ),
-        in_specs=[VMEM] * 9,
+        in_specs=[VMEM] * 10,
         out_specs=(VMEM, VMEM),
         scratch_shapes=[pltpu.VMEM((D, 128), F32)],
         compiler_params=params(24),
         cost_estimate=takes(2),
         name="hidden",
-    )(first, second, lat, embed_w, mod, *(one.reshape(4 * HD, D) for one in (out_own, out_peer, out_across, out_both)))
+    )(first, second, lat, embed_w, mod, *(one.reshape(-1, D) for one in (out_own, out_peer, out_across, *out_both)))
     with jax.named_scope("inner"):
         pairs = [(16 * q + j, 16 * (q - 1) + (j ^ 2)) for q in range(1, 16) for j in range(16)]
         following_across = lax.ppermute(inner, ("queue", "seq"), pairs)
@@ -434,19 +430,23 @@
     with jax.named_scope("inner_core"):
         tokens_four = [inner, other_core(inner), across, other_core(across)]
         following_four = [following, other_core(following), following_across, other_core(following_across)]
-    blocks = [one.reshape(5 * HD, D) for one in (five, below, above, far)]
-    parts = pl.pallas_call(
-        temporal_kernel,
-        out_shape=(jax.ShapeDtypeStruct((4 * HD, 256), BF),) * 2,
-        in_specs=[SMEM] + [ANY] * 4 + [VMEM] * 8,
-        out_specs=(VMEM,) * 2,
-        scratch_shapes=[pltpu.VMEM((4, 5 * HD, D), BF), pltpu.SemaphoreType.DMA((4,))],
-        compiler_params=params(48),
-        cost_estimate=takes(4),
-        name="temporal",
-    )(advance, *blocks, *following_four[2:], *following_four[:2], *tokens_four[2:], *tokens_four[:2])
+    blocks = [one.reshape(5 * HD, D) for one in (five, below, gate(above, far[0, 0]), far)]
+
+    def temporal(name, *tokens):
+        return pl.pallas_call(
+            temporal_kernel,
+            out_shape=jax.ShapeDtypeStruct((4 * HD, 256), BF),
+            in_specs=[SMEM] + [VMEM] * 8,
+            out_specs=VMEM,
+            compiler_params=params(24),
+            cost_estimate=takes(2),
+            name=name,
+        )(advance, *blocks, *tokens)
+
+    across = temporal("temporal_across", *following_four[2:], *tokens_four[2:])
+    near = temporal("temporal_near", *following_four[:2], *tokens_four[:2])
     with jax.named_scope("back"):
-        near, across = parts[0], over_x(parts[1])
+        across = over_x(across)
         near_peer, across_peer = other_core(near), other_core(across)
     update_own, update_peer = pl.pallas_call(
         output_kernel,

time: 101 us -> 96.9 us (0.959)
  waiting for transfers between devices: 27.1 us -> 19.9 us
  starting transfers between devices: 42.1 us -> 46.4 us
    ppermute x19 -> x20, waiting for transfers between devices: 17.3 us -> 11.7 us  [along_seq(): return lax.ppermute(array, 'seq', [(i, to(i)) for i in range(16)])]
    ppermute x19 -> x20, starting transfers between devices: 17.7 us -> 22.2 us  [along_seq(): return lax.ppermute(array, 'seq', [(i, to(i)) for i in range(16)])]
    ppermute x2, waiting for transfers between devices: 6.9 us -> 5.36 us  [from_next(): return lax.ppermute(array, 'queue', [(i, i - 1) for i in range(1, 16)])]
    pallas_call x1 -> x2, Pallas kernels: 3.78 us -> 2.64 us  [temporal(): pl.pallas_call(temporal_kernel, out_shape=jax.ShapeDtypeStruct((4 * HD, 2...]
    unnamed x18 -> x26, local copies, waits for them, and re-layouts: 2.15 us -> 1.5 us
  transfers between devices with their start and end apart: 23 -> 24, of which waited for: 12 -> 10; matrix products, arithmetic and copies ran while one was open for 4% -> 5% of each run, Pallas kernels for 17% -> 20%
where the time goes in v4:
time: 96.9 us; the launch traced here: 96.4 us
  starting transfers between devices  46.4 us (48%)
  Pallas kernels  22 us (23%)
  waiting for transfers between devices  19.9 us (21%)
  other arithmetic  5.05 us (5%)
  between operations  1.59 us (2%)
  local copies, waits for them, and re-layouts  1.5 us (2%)
    ppermute x20, starting transfers between devices, along_seq(): return lax.ppermute(array, 'seq', [(i, to(i)) for i in range(16)])  22.2 us
    ppermute x20, waiting for transfers between devices, along_seq(): return lax.ppermute(array, 'seq', [(i, to(i)) for i in range(16)])  11.7 us
    ppermute x2, starting transfers between devices, from_next(): return lax.ppermute(array, 'queue', [(i, i - 1) for i in range(1, 16)])  10.3 us
    ppermute x1, starting transfers between devices, shards(): following_across = lax.ppermute(inner, ('queue', 'seq'), pairs)  8.64 us
    pallas_call x2, Pallas kernels, attend(): pl.pallas_call(functools.partial(attend_kernel, frame), out_shape=jax.Sha...  8.14 us
    ppermute x2, waiting for transfers between devices, from_next(): return lax.ppermute(array, 'queue', [(i, i - 1) for i in range(1, 16)])  5.36 us
    all_to_all x1, starting transfers between devices, shards(): lax.all_to_all(packed, 'seq', split_axis=0, concat_axis=0, tiled=True)  5.27 us
    pallas_call x1, Pallas kernels, shards(): pl.pallas_call(coefficient_kernel, out_shape=(jax.ShapeDtypeStruct((2, 3,...  4.06 us
  transfers between devices with their start and end apart: 24, of which 10 were waited for; matrix products, arithmetic and copies ran while one was open for 5% of the time, Pallas kernels for 20%

profile of v4, /device:TPU:2, one launch (start us, length us, event | category | flops | bytes accessed | tf_op | source)
XLA Modules:
  0.0 96.4 jit_solution(9977675279818268993)
XLA Ops:
  0.7 2.2 %collective-permute-start.1 = (bf16[72,1152]{1,0:T(8,128)(2,1)}, bf16[72,1152]{1,0:T(8,128)(2,1)S(1)}, u32[]{:S(2)}, u32[]{:S(2)}) collective-permute-start(bf16[72,1152]{1,0:T(8,128)(2,1)} %bitcast.55), channel_id=1, source_target_pairs={{0,2},{1,3},{2,0},{3,1},{4,6},{5,7},{6,4},{7,5},{8,10},{9,11},{10,... | collective-permute-start | bytes 497672 | tf_op jit(solution)/shard_map/last_x/ppermute | solution.py:279
  2.9 3.2 %collective-permute-start = (bf16[72,1152]{1,0:T(8,128)(2,1)}, bf16[72,1152]{1,0:T(8,128)(2,1)S(1)}, u32[]{:S(2)}, u32[]{:S(2)}) collective-permute-start(bf16[72,1152]{1,0:T(8,128)(2,1)} %bitcast.61), channel_id=1, source_target_pairs={{0,8},{1,9},{2,10},{3,11},{4,12},{5,13},{6,14},{7,15},{8,0},{9,1},... | collective-permute-start | bytes 497672 | tf_op jit(solution)/shard_map/out_y/ppermute | solution.py:279
  6.8 2.6 %collective-permute-start.6 = (bf16[72,1152]{1,0:T(8,128)(2,1)}, bf16[72,1152]{1,0:T(8,128)(2,1)}, u32[]{:S(2)}, u32[]{:S(2)}) collective-permute-start(bf16[72,1152]{1,0:T(8,128)(2,1)} %bitcast.63), channel_id=1, source_target_pairs={{0,12},{1,13},{2,14},{3,15},{4,0},{5,1},{6,2},{7,3},{8,4},{9,5},{1... | collective-permute-start | bytes 497672 | tf_op jit(solution)/shard_map/out_y/ppermute | solution.py:279
  10.0 2.2 %pack.1 = (f32[16,40,128]{2,1,0:T(8,128)}, f32[16,128]{1,0:T(8,128)}) custom-call(s32[2]{0:T(128)} %levels_ref.1, f32[2,16,64]{2,1,0:T(8,128)} %bitcast.52, f32[16,1152]{1,0:T(8,128)} %embed_ref.5, f32[32,8,72]{2,1,0:T(8,128)} %table_ref.1, bf16[72,1152]{1,0:T(8,128)(2,1)} %copy-done.8), custom_call_target="tpu_custom_call" | custom-call | flops 2300000000 | bytes 1000 | tf_op jit(solution)/shard_map/pack/pallas_call | solution.py:350
  12.2 5.3 %all-to-all-start = ((f32[16,40,128]{2,1,0:T(8,128)}), f32[16,40,128]{2,1,0:T(8,128)S(1)}, u32[]{:S(2)}, u32[]{:S(2)}) async-start(f32[16,40,128]{2,1,0:T(8,128)} %get-tuple-element.14), calls=%async_computation | async-start | bytes 655360 | tf_op jit(solution)/shard_map/all_to_all | solution.py:361
  18.4 1.0 %pad_maximum_fusion = bf16[5,72,1152]{2,1,0:T(8,128)(2,1)S(1)} fusion(bf16[1,72,1152]{2,1,0:T(8,128)(2,1)} %bitcast.58, bf16[1,72,1152]{2,1,0:T(8,128)(2,1)S(1)} %bitcast.56, bf16[3,72,1152]{2,1,0:T(8,128)(2,1)S(1)} %select_bitcast_fusion), kind=kLoop, calls=%fused_computation | loop fusion | flops 829440 | bytes 1658880 | tf_op jit(solution)/shard_map/dynamic_update_slice | solution.py:370
  19.4 2.0 %collective-permute-start.2 = (bf16[5,72,1152]{2,1,0:T(8,128)(2,1)S(1)}, bf16[5,72,1152]{2,1,0:T(8,128)(2,1)S(1)}, u32[]{:S(2)}, u32[]{:S(2)}) collective-permute-start(bf16[5,72,1152]{2,1,0:T(8,128)(2,1)S(1)} %pad_maximum_fusion), channel_id=1, source_target_pairs={{0,4},{1,5},{2,6},{3,7},{4,8},{5,9},{6,10},{7,11},{8,12},{9,13},{1... | collective-permute-start | bytes 2488328 | tf_op jit(solution)/shard_map/five_y/ppermute | solution.py:279
  21.4 1.3 %collective-permute-start.3 = (bf16[5,72,1152]{2,1,0:T(8,128)(2,1)S(1)}, bf16[5,72,1152]{2,1,0:T(8,128)(2,1)}, u32[]{:S(2)}, u32[]{:S(2)}) collective-permute-start(bf16[5,72,1152]{2,1,0:T(8,128)(2,1)S(1)} %pad_maximum_fusion), channel_id=1, source_target_pairs={{0,12},{1,13},{2,14},{3,15},{4,0},{5,1},{6,2},{7,3},{8,4},{9,5},{1... | collective-permute-start | bytes 2488328 | tf_op jit(solution)/shard_map/five_y/ppermute | solution.py:279
  22.7 1.0 %pad_maximum_fusion.1 = bf16[4,72,1152]{2,1,0:T(8,128)(2,1)S(1)} fusion(bf16[1,72,1152]{2,1,0:T(8,128)(2,1)S(1)} %bitcast.60, bf16[1,72,1152]{2,1,0:T(8,128)(2,1)} %bitcast.13, bf16[1,72,1152]{2,1,0:T(8,128)(2,1)S(1)} %bitcast.65, bf16[1,72,1152]{2,1,0:T(8,128)(2,1)S(1)} %bitcast.64), kind=kLoop, calls=%fused_computation.3 | loop fusion | flops 995328 | bytes 1327104 | tf_op jit(solution)/shard_map/out_y/stack | solution.py:364
  23.7 3.5 %collective-permute-start.8 = (bf16[4,72,1152]{2,1,0:T(8,128)(2,1)S(1)}, bf16[4,72,1152]{2,1,0:T(8,128)(2,1)S(1)}, u32[]{:S(2)}, u32[]{:S(2)}) collective-permute-start(bf16[4,72,1152]{2,1,0:T(8,128)(2,1)S(1)} %pad_maximum_fusion.1), channel_id=1, source_target_pairs={{0,2},{1,3},{2,0},{3,1},{4,6},{5,7},{6,4},{7,5},{8,10},{9,11},{10,... | collective-permute-start | bytes 1990664 | tf_op jit(solution)/shard_map/out_x/ppermute | solution.py:279
  27.8 4.1 %coefficients.1 = (f32[2,3,32,1152]{3,2,1,0:T(8,128)S(1)}, f32[16,1152]{1,0:T(8,128)S(1)}, f32[2,16,1024]{2,1,0:T(8,128)S(1)}) custom-call(f32[16,40,128]{2,1,0:T(8,128)S(1)} %all-to-all-done.all_ref, f32[16,1152]{1,0:T(8,128)S(1)} %copy-done.1, bf16[3,1152,1152]{2,1,0:T(8,128)(2,1)} %bitcast.66), custom_call_target="tpu_custom_call" | custom-call | flops 23000000512 | bytes 1000 | tf_op jit(solution)/shard_map/coefficients/pallas_call | solution.py:374
  31.9 4.1 %attend.2.refs_0_ = bf16[64,1152]{1,0:T(8,128)(2,1)S(1)} custom-call(f32[16,128]{1,0:T(8,128)S(1)} %copy-done, f32[2,16,1024]{2,1,0:T(8,128)S(1)} %get-tuple-element.15.tokens_ref, f32[2,3,32,1152]{3,2,1,0:T(8,128)S(1)} %get-tuple-element.16.coef_ref), custom_call_target="tpu_custom_call" | custom-call | flops 115000000 | bytes 1000 | tf_op jit(solution)/shard_map/attend/pallas_call | solution.py:390
  35.9 4.1 %attend.3.second_ref = bf16[64,1152]{1,0:T(8,128)(2,1)S(1)} custom-call(f32[16,128]{1,0:T(8,128)S(1)} %copy-done, f32[2,16,1024]{2,1,0:T(8,128)S(1)} %get-tuple-element.15.tokens_ref, f32[2,3,32,1152]{3,2,1,0:T(8,128)S(1)} %get-tuple-element.16.coef_ref, bf16[64,1152]{1,0:T(8,128)(2,1)S(1)} %attend.2.refs_0_), custom_call_target="tpu_custom_call" | custom-call | flops 115000000 | bytes 1000 | tf_op jit(solution)/shard_map/attend/pallas_call | solution.py:390
  40.0 2.0 %collective-permute-done.8 = bf16[4,72,1152]{2,1,0:T(8,128)(2,1)S(1)} collective-permute-done((bf16[4,72,1152]{2,1,0:T(8,128)(2,1)S(1)}, bf16[4,72,1152]{2,1,0:T(8,128)(2,1)S(1)}, u32[]{:S(2)}, u32[]{:S(2)}) %collective-permute-start.8) | collective-permute-done | bytes 663584 | tf_op jit(solution)/shard_map/out_x/ppermute | solution.py:279
  44.4 2.2 %collective-permute-start.4 = (bf16[5,72,1152]{2,1,0:T(8,128)(2,1)S(1)}, bf16[5,72,1152]{2,1,0:T(8,128)(2,1)S(1)}, u32[]{:S(2)}, u32[]{:S(2)}) collective-permute-start(bf16[5,72,1152]{2,1,0:T(8,128)(2,1)S(1)} %broadcast_select_fusion.1), channel_id=1, source_target_pairs={{0,8},{1,9},{2,10},{3,11},{4,12},{5,13},{6,14},{7,15},{8,0},{9,1},... | collective-permute-start | bytes 2488328 | tf_op jit(solution)/shard_map/five_far/ppermute | solution.py:279
  46.6 2.6 %hidden.1 = (f32[1152,128]{1,0:T(8,128)S(1)}, bf16[1152,128]{1,0:T(8,128)(2,1)S(1)}) custom-call(bf16[64,1152]{1,0:T(8,128)(2,1)S(1)} %broadcast_select_fusion.2.first_ref, bf16[64,1152]{1,0:T(8,128)(2,1)S(1)} %attend.3.second_ref, f32[2,16,64]{2,1,0:T(8,128)S(1)} %bitcast.53, f32[16,1152]{1,0:T(8,128)S(1)} %copy-done.1, ...), custom_call_target="tpu_custom_call" | custom-call | flops 2300000000 | bytes 1000 | tf_op jit(solution)/shard_map/hidden/pallas_call | solution.py:412
  49.3 8.6 %collective-permute-start.14 = (bf16[1152,128]{1,0:T(8,128)(2,1)S(1)}, bf16[1152,128]{1,0:T(8,128)(2,1)S(1)}, u32[]{:S(2)}, u32[]{:S(2)}) collective-permute-start(bf16[1152,128]{1,0:T(8,128)(2,1)S(1)} %get-tuple-element.18.refs_6_), channel_id=1, source_target_pairs={{16,2},{17,3},{18,0},{19,1},{20,6},{21,7},{22,4},{23,5},{24,10},{2... | collective-permute-start | bytes 884744 | tf_op jit(solution)/shard_map/inner/ppermute | solution.py:427
  57.9 2.1 %collective-permute-start.16 = (bf16[1152,128]{1,0:T(8,128)(2,1)S(1)}, bf16[1152,128]{1,0:T(8,128)(2,1)S(1)}, u32[]{:S(2)}, u32[]{:S(2)}) collective-permute-start(bf16[1152,128]{1,0:T(8,128)(2,1)S(1)} %get-tuple-element.18.refs_6_), channel_id=1, source_target_pairs={{0,2},{1,3},{2,0},{3,1},{4,6},{5,7},{6,4},{7,5},{8,10},{9,11},{10,... | collective-permute-start | bytes 884744 | tf_op jit(solution)/shard_map/inner/ppermute | solution.py:279
  60.1 3.8 %collective-permute-start.11 = (bf16[1152,128]{1,0:T(8,128)(2,1)S(1)}, bf16[1152,128]{1,0:T(8,128)(2,1)S(1)}, u32[]{:S(2)}, u32[]{:S(2)}) collective-permute-start(bf16[1152,128]{1,0:T(8,128)(2,1)S(1)} %get-tuple-element.18.refs_6_), channel_id=1, source_target_pairs={{16,0},{32,16},{48,32},{64,48},{80,64},{96,80},{112,96},{128,112},... | collective-permute-start | bytes 884744 | tf_op jit(solution)/shard_map/inner/ppermute | solution.py:299
  64.6 2.4 %collective-permute-done.14.refs_4_ = bf16[1152,128]{1,0:T(8,128)(2,1)S(1)} collective-permute-done((bf16[1152,128]{1,0:T(8,128)(2,1)S(1)}, bf16[1152,128]{1,0:T(8,128)(2,1)S(1)}, u32[]{:S(2)}, u32[]{:S(2)}) %collective-permute-start.14) | collective-permute-done | bytes 294944 | tf_op jit(solution)/shard_map/inner/ppermute | solution.py:427
  67.0 1.1 %collective-permute-done.16.refs_6_ = bf16[1152,128]{1,0:T(8,128)(2,1)S(1)} collective-permute-done((bf16[1152,128]{1,0:T(8,128)(2,1)S(1)}, bf16[1152,128]{1,0:T(8,128)(2,1)S(1)}, u32[]{:S(2)}, u32[]{:S(2)}) %collective-permute-start.16) | collective-permute-done | bytes 294944 | tf_op jit(solution)/shard_map/inner/ppermute | solution.py:279
  68.1 4.0 %collective-permute-done.11.refs_4_ = bf16[1152,128]{1,0:T(8,128)(2,1)S(1)} collective-permute-done((bf16[1152,128]{1,0:T(8,128)(2,1)S(1)}, bf16[1152,128]{1,0:T(8,128)(2,1)S(1)}, u32[]{:S(2)}, u32[]{:S(2)}) %collective-permute-start.11) | collective-permute-done | bytes 294944 | tf_op jit(solution)/shard_map/inner/ppermute | solution.py:299
  72.2 1.2 %broadcast_select_fusion = bf16[5,72,1152]{2,1,0:T(8,128)(2,1)S(1)} fusion(bf16[5,72,1152]{2,1,0:T(8,128)(2,1)} %collective-permute-done.3, pred[1152]{0:T(1024)(128)(4,1)S(1)} %compare_reduce_fusion.1), kind=kLoop, calls=%fused_computation.1 | loop fusion | flops 414720 | bytes 1660032 | tf_op jit(solution)/shard_map/jit(_where)/select_n | solution.py:325
  73.4 1.3 %temporal_across.1 = bf16[288,256]{1,0:T(8,128)(2,1)S(1)} custom-call(s32[1]{0:T(128)S(6)} %copy.13.advance_ref, bf16[360,1152]{1,0:T(8,128)(2,1)S(1)} %bitcast.35, bf16[360,1152]{1,0:T(8,128)(2,1)S(1)} %bitcast.43, bf16[360,1152]{1,0:T(8,128)(2,1)S(1)} %bitcast.38, bf16[360,1152]{1,0:T(8,128)(2,1)S(1)} %bitcast.46, ...), custom_call_target="tpu_custom_call" | custom-call | flops 2300000000 | bytes 1000 | tf_op jit(solution)/shard_map/temporal_across/pallas_call | solution.py:436
  74.8 1.1 %collective-permute-start.18 = (bf16[288,256]{1,0:T(8,128)(2,1)S(1)}, bf16[288,256]{1,0:T(8,128)(2,1)S(1)}, u32[]{:S(2)}, u32[]{:S(2)}) collective-permute-start(bf16[288,256]{1,0:T(8,128)(2,1)S(1)} %temporal_across.1), channel_id=1, source_target_pairs={{0,2},{1,3},{2,0},{3,1},{4,6},{5,7},{6,4},{7,5},{8,10},{9,11},{10,... | collective-permute-start | bytes 442376 | tf_op jit(solution)/shard_map/back/ppermute | solution.py:279
  75.9 1.3 %temporal_near.1.near_ref = bf16[288,256]{1,0:T(8,128)(2,1)S(1)} custom-call(s32[1]{0:T(128)S(6)} %copy.13.advance_ref, bf16[360,1152]{1,0:T(8,128)(2,1)S(1)} %bitcast.36, bf16[360,1152]{1,0:T(8,128)(2,1)S(1)} %bitcast.44, bf16[360,1152]{1,0:T(8,128)(2,1)S(1)} %bitcast.39, bf16[360,1152]{1,0:T(8,128)(2,1)S(1)} %bitcast.47, ...), custom_call_target="tpu_custom_call" | custom-call | flops 2300000000 | bytes 1000 | tf_op jit(solution)/shard_map/temporal_near/pallas_call | solution.py:436
  77.6 5.1 %collective-permute-done.18.across_ref = bf16[288,256]{1,0:T(8,128)(2,1)S(1)} collective-permute-done((bf16[288,256]{1,0:T(8,128)(2,1)S(1)}, bf16[288,256]{1,0:T(8,128)(2,1)S(1)}, u32[]{:S(2)}, u32[]{:S(2)}) %collective-permute-start.18) | collective-permute-done | bytes 147488 | tf_op jit(solution)/shard_map/back/ppermute | solution.py:279
  82.6 1.4 %collective-permute-done.20.across_peer_ref = bf16[288,256]{1,0:T(8,128)(2,1)S(1)} collective-permute-done((bf16[288,256]{1,0:T(8,128)(2,1)S(1)}, bf16[288,256]{1,0:T(8,128)(2,1)S(1)}, u32[]{:S(2)}, u32[]{:S(2)}) %collective-permute-start.20) | collective-permute-done | bytes 147488 | tf_op jit(solution)/shard_map/back/ppermute | solution.py:279
  84.9 1.4 %collective-permute-done.21.peer_ref = f32[576,128]{1,0:T(8,128)S(1)} collective-permute-done((f32[576,128]{1,0:T(8,128)S(1)}, f32[576,128]{1,0:T(8,128)S(1)}, u32[]{:S(2)}, u32[]{:S(2)}) %collective-permute-start.21) | collective-permute-done | bytes 294944 | tf_op jit(solution)/shard_map/update/ppermute | solution.py:279
  86.3 1.7 %final.1 = (f32[2,16,64]{2,1,0:T(8,128)}, f32[2,16,64]{2,1,0:T(8,128)S(1)}) custom-call(f32[576,128]{1,0:T(8,128)S(1)} %get-tuple-element.19.own_ref, f32[576,128]{1,0:T(8,128)S(1)} %collective-permute-done.21.peer_ref, f32[1152,128]{1,0:T(8,128)S(1)} %get-tuple-element.21.hidden_ref, f32[2,16,64]{2,1,0:T(8,128)S(1)} %bitcast.54, ...), custom_call_target="tpu_custom_call" | custom-call | flops 2300000000 | bytes 1000 | tf_op jit(solution)/shard_map/final/pallas_call | solution.py:463
  88.0 6.5 %collective-permute-start.22 = (f32[16,64]{1,0:T(8,128)S(1)}, f32[16,64]{1,0:T(8,128)S(1)}, u32[]{:S(2)}, u32[]{:S(2)}) collective-permute-start(f32[16,64]{1,0:T(8,128)S(1)} %get-tuple-element.27), channel_id=1, source_target_pairs={{16,0},{32,16},{48,32},{64,48},{80,64},{96,80},{112,96},{128,112},... | collective-permute-start | bytes 12296 | tf_op jit(solution)/shard_map/ppermute | solution.py:299
  94.5 1.3 %collective-permute-done.22 = f32[16,64]{1,0:T(8,128)S(1)} collective-permute-done((f32[16,64]{1,0:T(8,128)S(1)}, f32[16,64]{1,0:T(8,128)S(1)}, u32[]{:S(2)}, u32[]{:S(2)}) %collective-permute-start.22) | collective-permute-done | bytes 4128 | tf_op jit(solution)/shard_map/ppermute | solution.py:299
  (66 shorter events, 7.0 us)
Async XLA Ops:
  0.6 17.7 %copy-start.6 = (bf16[1152,72]{0,1:T(8,128)(2,1)S(1)}, bf16[1152,72]{0,1:T(8,128)(2,1)}, u32[]{:S(2)}) copy-start(bf16[1152,72]{0,1:T(8,128)(2,1)} %param.20) | copy-start | bytes 497668
  0.6 22.1 %copy-start.11 = (bf16[1152,72]{0,1:T(8,128)(2,1)S(1)}, bf16[1152,72]{0,1:T(8,128)(2,1)}, u32[]{:S(2)}) copy-start(bf16[1152,72]{0,1:T(8,128)(2,1)} %param.18) | copy-start | bytes 497668
  0.7 27.1 %copy-start.1 = (f32[16,1152]{1,0:T(8,128)S(1)}, f32[16,1152]{1,0:T(8,128)}, u32[]{:S(2)}) copy-start(f32[16,1152]{1,0:T(8,128)} %embed_ref.5) | copy-start | bytes 221188
  0.7 16.8 %copy-start.10 = (bf16[1152,3,72]{0,2,1:T(8,128)(2,1)S(1)}, bf16[1152,3,72]{0,2,1:T(8,128)(2,1)}, u32[]{:S(2)}) copy-start(bf16[1152,3,72]{0,2,1:T(8,128)(2,1)} %param.19) | copy-start | bytes 1492996
  0.7 8.6 %collective-permute-start.1 = (bf16[72,1152]{1,0:T(8,128)(2,1)}, bf16[72,1152]{1,0:T(8,128)(2,1)S(1)}, u32[]{:S(2)}, u32[]{:S(2)}) collective-permute-start(bf16[72,1152]{1,0:T(8,128)(2,1)} %bitcast.55), channel_id=1, source_target_pairs={{0,2},{1,3},{2,0},{3,1},{4,6},{5,7},{6,4},{7,5},{8,10},{9,11},{10,... | collective-permute-start | bytes 497672 | tf_op jit(solution)/shard_map/last_x/ppermute | solution.py:279
  2.9 14.6 %collective-permute-start = (bf16[72,1152]{1,0:T(8,128)(2,1)}, bf16[72,1152]{1,0:T(8,128)(2,1)S(1)}, u32[]{:S(2)}, u32[]{:S(2)}) collective-permute-start(bf16[72,1152]{1,0:T(8,128)(2,1)} %bitcast.61), channel_id=1, source_target_pairs={{0,8},{1,9},{2,10},{3,11},{4,12},{5,13},{6,14},{7,15},{8,0},{9,1},... | collective-permute-start | bytes 497672 | tf_op jit(solution)/shard_map/out_y/ppermute | solution.py:279
  6.1 16.6 %collective-permute-start.5 = (bf16[72,1152]{1,0:T(8,128)(2,1)}, bf16[72,1152]{1,0:T(8,128)(2,1)S(1)}, u32[]{:S(2)}, u32[]{:S(2)}) collective-permute-start(bf16[72,1152]{1,0:T(8,128)(2,1)} %bitcast.62), channel_id=1, source_target_pairs={{0,4},{1,5},{2,6},{3,7},{4,8},{5,9},{6,10},{7,11},{8,12},{9,13},{1... | collective-permute-start | bytes 497672 | tf_op jit(solution)/shard_map/out_y/ppermute | solution.py:279
  6.8 16.0 %collective-permute-start.6 = (bf16[72,1152]{1,0:T(8,128)(2,1)}, bf16[72,1152]{1,0:T(8,128)(2,1)}, u32[]{:S(2)}, u32[]{:S(2)}) collective-permute-start(bf16[72,1152]{1,0:T(8,128)(2,1)} %bitcast.63), channel_id=1, source_target_pairs={{0,12},{1,13},{2,14},{3,15},{4,0},{5,1},{6,2},{7,3},{8,4},{9,5},{1... | collective-permute-start | bytes 497672 | tf_op jit(solution)/shard_map/out_y/ppermute | solution.py:279
  12.2 15.6 %all-to-all-start = ((f32[16,40,128]{2,1,0:T(8,128)}), f32[16,40,128]{2,1,0:T(8,128)S(1)}, u32[]{:S(2)}, u32[]{:S(2)}) async-start(f32[16,40,128]{2,1,0:T(8,128)} %get-tuple-element.14), calls=%async_computation | async-start | bytes 655360 | tf_op jit(solution)/shard_map/all_to_all | solution.py:361
  19.4 24.0 %collective-permute-start.2 = (bf16[5,72,1152]{2,1,0:T(8,128)(2,1)S(1)}, bf16[5,72,1152]{2,1,0:T(8,128)(2,1)S(1)}, u32[]{:S(2)}, u32[]{:S(2)}) collective-permute-start(bf16[5,72,1152]{2,1,0:T(8,128)(2,1)S(1)} %pad_maximum_fusion), channel_id=1, source_target_pairs={{0,4},{1,5},{2,6},{3,7},{4,8},{5,9},{6,10},{7,11},{8,12},{9,13},{1... | collective-permute-start | bytes 2488328 | tf_op jit(solution)/shard_map/five_y/ppermute | solution.py:279
  21.4 22.0 %collective-permute-start.3 = (bf16[5,72,1152]{2,1,0:T(8,128)(2,1)S(1)}, bf16[5,72,1152]{2,1,0:T(8,128)(2,1)}, u32[]{:S(2)}, u32[]{:S(2)}) collective-permute-start(bf16[5,72,1152]{2,1,0:T(8,128)(2,1)S(1)} %pad_maximum_fusion), channel_id=1, source_target_pairs={{0,12},{1,13},{2,14},{3,15},{4,0},{5,1},{6,2},{7,3},{8,4},{9,5},{1... | collective-permute-start | bytes 2488328 | tf_op jit(solution)/shard_map/five_y/ppermute | solution.py:279
  23.7 18.3 %collective-permute-start.8 = (bf16[4,72,1152]{2,1,0:T(8,128)(2,1)S(1)}, bf16[4,72,1152]{2,1,0:T(8,128)(2,1)S(1)}, u32[]{:S(2)}, u32[]{:S(2)}) collective-permute-start(bf16[4,72,1152]{2,1,0:T(8,128)(2,1)S(1)} %pad_maximum_fusion.1), channel_id=1, source_target_pairs={{0,2},{1,3},{2,0},{3,1},{4,6},{5,7},{6,4},{7,5},{8,10},{9,11},{10,... | collective-permute-start | bytes 1990664 | tf_op jit(solution)/shard_map/out_x/ppermute | solution.py:279
  27.3 19.4 %collective-permute-start.7 = (bf16[4,72,1152]{2,1,0:T(8,128)(2,1)S(1)}, bf16[4,72,1152]{2,1,0:T(8,128)(2,1)}, u32[]{:S(2)}, u32[]{:S(2)}) collective-permute-start(bf16[4,72,1152]{2,1,0:T(8,128)(2,1)S(1)} %pad_maximum_fusion.1), channel_id=1, source_target_pairs={{0,1},{1,0},{2,3},{3,2},{4,5},{5,4},{6,7},{7,6},{8,9},{9,8},{10,11... | collective-permute-start | bytes 1990664 | tf_op jit(solution)/shard_map/out_core/ppermute | solution.py:279
  27.7 16.5 %copy-start.7 = (bf16[1152,72]{0,1:T(8,128)(2,1)S(1)}, bf16[1152,72]{0,1:T(8,128)(2,1)}, u32[]{:S(2)}) copy-start(bf16[1152,72]{0,1:T(8,128)(2,1)} %param.20) | copy-start | bytes 497668
  27.8 16.5 %copy-start.9 = (bf16[72,1152]{1,0:T(8,128)(2,1)S(1)}, bf16[72,1152]{1,0:T(8,128)(2,1)}, u32[]{:S(2)}) copy-start(bf16[72,1152]{1,0:T(8,128)(2,1)} %copy-done.8) | copy-start | bytes 497668
  27.8 18.9 %copy-start.3 = (f32[2,64,16]{1,2,0:T(8,128)S(1)}, f32[2,64,16]{1,2,0:T(8,128)}, u32[]{:S(2)}) copy-start(f32[2,64,16]{1,2,0:T(8,128)} %param.11) | copy-start | bytes 24580
  42.1 4.5 %collective-permute-start.9 = (bf16[2,72,1152]{2,1,0:T(8,128)(2,1)S(1)}, bf16[2,72,1152]{2,1,0:T(8,128)(2,1)S(1)}, u32[]{:S(2)}, u32[]{:S(2)}) collective-permute-start(bf16[2,72,1152]{2,1,0:T(8,128)(2,1)S(1)} %get-tuple-element.25), channel_id=1, source_target_pairs={{0,1},{1,0},{2,3},{3,2},{4,5},{5,4},{6,7},{7,6},{8,9},{9,8},{10,11... | collective-permute-start | bytes 995336 | tf_op jit(solution)/shard_map/out_core/ppermute | solution.py:279
  42.2 4.4 %collective-permute-start.10 = (bf16[2,72,1152]{2,1,0:T(8,128)(2,1)S(1)}, bf16[2,72,1152]{2,1,0:T(8,128)(2,1)S(1)}, u32[]{:S(2)}, u32[]{:S(2)}) collective-permute-start(bf16[2,72,1152]{2,1,0:T(8,128)(2,1)S(1)} %get-tuple-element.24), channel_id=1, source_target_pairs={{0,1},{1,0},{2,3},{3,2},{4,5},{5,4},{6,7},{7,6},{8,9},{9,8},{10,11... | collective-permute-start | bytes 995336 | tf_op jit(solution)/shard_map/out_core/ppermute | solution.py:279
  44.4 27.8 %collective-permute-start.4 = (bf16[5,72,1152]{2,1,0:T(8,128)(2,1)S(1)}, bf16[5,72,1152]{2,1,0:T(8,128)(2,1)S(1)}, u32[]{:S(2)}, u32[]{:S(2)}) collective-permute-start(bf16[5,72,1152]{2,1,0:T(8,128)(2,1)S(1)} %broadcast_select_fusion.1), channel_id=1, source_target_pairs={{0,8},{1,9},{2,10},{3,11},{4,12},{5,13},{6,14},{7,15},{8,0},{9,1},... | collective-permute-start | bytes 2488328 | tf_op jit(solution)/shard_map/five_far/ppermute | solution.py:279
  49.3 17.7 %collective-permute-start.14 = (bf16[1152,128]{1,0:T(8,128)(2,1)S(1)}, bf16[1152,128]{1,0:T(8,128)(2,1)S(1)}, u32[]{:S(2)}, u32[]{:S(2)}) collective-permute-start(bf16[1152,128]{1,0:T(8,128)(2,1)S(1)} %get-tuple-element.18.refs_6_), channel_id=1, source_target_pairs={{16,2},{17,3},{18,0},{19,1},{20,6},{21,7},{22,4},{23,5},{24,10},{2... | collective-permute-start | bytes 884744 | tf_op jit(solution)/shard_map/inner/ppermute | solution.py:427
  57.9 10.2 %collective-permute-start.16 = (bf16[1152,128]{1,0:T(8,128)(2,1)S(1)}, bf16[1152,128]{1,0:T(8,128)(2,1)S(1)}, u32[]{:S(2)}, u32[]{:S(2)}) collective-permute-start(bf16[1152,128]{1,0:T(8,128)(2,1)S(1)} %get-tuple-element.18.refs_6_), channel_id=1, source_target_pairs={{0,2},{1,3},{2,0},{3,1},{4,6},{5,7},{6,4},{7,5},{8,10},{9,11},{10,... | collective-permute-start | bytes 884744 | tf_op jit(solution)/shard_map/inner/ppermute | solution.py:279
  60.1 12.1 %collective-permute-start.11 = (bf16[1152,128]{1,0:T(8,128)(2,1)S(1)}, bf16[1152,128]{1,0:T(8,128)(2,1)S(1)}, u32[]{:S(2)}, u32[]{:S(2)}) collective-permute-start(bf16[1152,128]{1,0:T(8,128)(2,1)S(1)} %get-tuple-element.18.refs_6_), channel_id=1, source_target_pairs={{16,0},{32,16},{48,32},{64,48},{80,64},{96,80},{112,96},{128,112},... | collective-permute-start | bytes 884744 | tf_op jit(solution)/shard_map/inner/ppermute | solution.py:299
  64.5 11.3 %collective-permute-start.13 = (bf16[1152,128]{1,0:T(8,128)(2,1)S(1)}, bf16[1152,128]{1,0:T(8,128)(2,1)S(1)}, u32[]{:S(2)}, u32[]{:S(2)}) collective-permute-start(bf16[1152,128]{1,0:T(8,128)(2,1)S(1)} %get-tuple-element.18.refs_6_), channel_id=1, source_target_pairs={{0,1},{1,0},{2,3},{3,2},{4,5},{5,4},{6,7},{7,6},{8,9},{9,8},{10,11... | collective-permute-start | bytes 884744 | tf_op jit(solution)/shard_map/inner_core/ppermute | solution.py:279
  67.0 6.4 %collective-permute-start.15 = (bf16[1152,128]{1,0:T(8,128)(2,1)S(1)}, bf16[1152,128]{1,0:T(8,128)(2,1)S(1)}, u32[]{:S(2)}, u32[]{:S(2)}) collective-permute-start(bf16[1152,128]{1,0:T(8,128)(2,1)S(1)} %collective-permute-done.14.refs_4_), channel_id=1, source_target_pairs={{0,1},{1,0},{2,3},{3,2},{4,5},{5,4},{6,7},{7,6},{8,9},{9,8},{10,11... | collective-permute-start | bytes 884744 | tf_op jit(solution)/shard_map/inner_core/ppermute | solution.py:279
  68.1 5.3 %collective-permute-start.17 = (bf16[1152,128]{1,0:T(8,128)(2,1)S(1)}, bf16[1152,128]{1,0:T(8,128)(2,1)S(1)}, u32[]{:S(2)}, u32[]{:S(2)}) collective-permute-start(bf16[1152,128]{1,0:T(8,128)(2,1)S(1)} %collective-permute-done.16.refs_6_), channel_id=1, source_target_pairs={{0,1},{1,0},{2,3},{3,2},{4,5},{5,4},{6,7},{7,6},{8,9},{9,8},{10,11... | collective-permute-start | bytes 884744 | tf_op jit(solution)/shard_map/inner_core/ppermute | solution.py:279
  72.1 3.7 %collective-permute-start.12 = (bf16[1152,128]{1,0:T(8,128)(2,1)S(1)}, bf16[1152,128]{1,0:T(8,128)(2,1)S(1)}, u32[]{:S(2)}, u32[]{:S(2)}) collective-permute-start(bf16[1152,128]{1,0:T(8,128)(2,1)S(1)} %collective-permute-done.11.refs_4_), channel_id=1, source_target_pairs={{0,1},{1,0},{2,3},{3,2},{4,5},{5,4},{6,7},{7,6},{8,9},{9,8},{10,11... | collective-permute-start | bytes 884744 | tf_op jit(solution)/shard_map/inner_core/ppermute | solution.py:279
  74.8 7.9 %collective-permute-start.18 = (bf16[288,256]{1,0:T(8,128)(2,1)S(1)}, bf16[288,256]{1,0:T(8,128)(2,1)S(1)}, u32[]{:S(2)}, u32[]{:S(2)}) collective-permute-start(bf16[288,256]{1,0:T(8,128)(2,1)S(1)} %temporal_across.1), channel_id=1, source_target_pairs={{0,2},{1,3},{2,0},{3,1},{4,6},{5,7},{6,4},{7,5},{8,10},{9,11},{10,... | collective-permute-start | bytes 442376 | tf_op jit(solution)/shard_map/back/ppermute | solution.py:279
  77.2 18.6 %copy-start.12 = (f32[64,16]{0,1:T(8,128)S(1)}, f32[64,16]{0,1:T(8,128)}, u32[]{:S(2)}) copy-start(f32[64,16]{0,1:T(8,128)} %param.14) | copy-start | bytes 12292
  77.2 5.4 %collective-permute-start.19 = (bf16[288,256]{1,0:T(8,128)(2,1)S(1)}, bf16[288,256]{1,0:T(8,128)(2,1)S(1)}, u32[]{:S(2)}, u32[]{:S(2)}) collective-permute-start(bf16[288,256]{1,0:T(8,128)(2,1)S(1)} %temporal_near.1.near_ref), channel_id=1, source_target_pairs={{0,1},{1,0},{2,3},{3,2},{4,5},{5,4},{6,7},{7,6},{8,9},{9,8},{10,11... | collective-permute-start | bytes 442376 | tf_op jit(solution)/shard_map/back/ppermute | solution.py:279
  82.6 1.4 %collective-permute-start.20 = (bf16[288,256]{1,0:T(8,128)(2,1)S(1)}, bf16[288,256]{1,0:T(8,128)(2,1)S(1)}, u32[]{:S(2)}, u32[]{:S(2)}) collective-permute-start(bf16[288,256]{1,0:T(8,128)(2,1)S(1)} %collective-permute-done.18.across_ref), channel_id=1, source_target_pairs={{0,1},{1,0},{2,3},{3,2},{4,5},{5,4},{6,7},{7,6},{8,9},{9,8},{10,11... | collective-permute-start | bytes 442376 | tf_op jit(solution)/shard_map/back/ppermute | solution.py:279
  84.6 1.7 %collective-permute-start.21 = (f32[576,128]{1,0:T(8,128)S(1)}, f32[576,128]{1,0:T(8,128)S(1)}, u32[]{:S(2)}, u32[]{:S(2)}) collective-permute-start(f32[576,128]{1,0:T(8,128)S(1)} %get-tuple-element.20), channel_id=1, source_target_pairs={{0,1},{1,0},{2,3},{3,2},{4,5},{5,4},{6,7},{7,6},{8,9},{9,8},{10,11... | collective-permute-start | bytes 884744 | tf_op jit(solution)/shard_map/update/ppermute | solution.py:279
  88.0 7.8 %collective-permute-start.22 = (f32[16,64]{1,0:T(8,128)S(1)}, f32[16,64]{1,0:T(8,128)S(1)}, u32[]{:S(2)}, u32[]{:S(2)}) collective-permute-start(f32[16,64]{1,0:T(8,128)S(1)} %get-tuple-element.27), channel_id=1, source_target_pairs={{16,0},{32,16},{48,32},{64,48},{80,64},{96,80},{112,96},{128,112},... | collective-permute-start | bytes 12296 | tf_op jit(solution)/shard_map/ppermute | solution.py:299
  (5 other events, 33.6 us)

commit v5 on v4

--- a/solution.py
+++ b/solution.py
@@ -405,7 +405,7 @@
     second = attend(1, first)
     with jax.named_scope("out_core"):
         out_both = [other_core(gate(out_across[half : half + 2], second[0])) for half in (0, 2)]
-    first = gate(first, below[0, 0], above[0, 0])
+    first, second = gate(first, below[0, 0]), gate(second, above[0, 0])
     with jax.named_scope("five_far"):
         far = y_far(gate(five, first[0]))
 
@@ -427,10 +427,12 @@
         following_across = lax.ppermute(inner, ("queue", "seq"), pairs)
         across = over_x(inner)
         following = from_next(inner)
+    above = gate(above, below[0, 0])
+    following_across = gate(following_across, above[0, 0, 0:128])
     with jax.named_scope("inner_core"):
         tokens_four = [inner, other_core(inner), across, other_core(across)]
         following_four = [following, other_core(following), following_across, other_core(following_across)]
-    blocks = [one.reshape(5 * HD, D) for one in (five, below, gate(above, far[0, 0]), far)]
+    blocks = [one.reshape(5 * HD, D) for one in (five, below, above, far)]
 
     def temporal(name, *tokens):
         return pl.pallas_call(

time: 96.9 us -> 96.2 us (level)
  starting transfers between devices: 46.4 us -> 44.7 us
    ppermute x20, starting transfers between devices: 22.2 us -> 19.6 us  [along_seq(): return lax.ppermute(array, 'seq', [(i, to(i)) for i in range(16)])]
    ppermute x20, waiting for transfers between devices: 11.7 us -> 14 us  [along_seq(): return lax.ppermute(array, 'seq', [(i, to(i)) for i in range(16)])]
    ppermute x2, waiting for transfers between devices: 5.36 us -> 3.3 us  [from_next(): return lax.ppermute(array, 'queue', [(i, i - 1) for i in range(1, 16)])]
  transfers between devices with their start and end apart: 24 -> 24, of which waited for: 10 -> 10; matrix products, arithmetic and copies ran while one was open for 5% -> 5% of each run, Pallas kernels for 20% -> 21%
where the time goes in v5:
time: 96.2 us; the launch traced here: 95.5 us
  starting transfers between devices  44.7 us (46%)
  Pallas kernels  22 us (23%)
  waiting for transfers between devices  20.5 us (21%)
  other arithmetic  5.28 us (5%)
  between operations  1.66 us (2%)
  local copies, waits for them, and re-layouts  1.4 us (1%)
    ppermute x20, starting transfers between devices, along_seq(): return lax.ppermute(array, 'seq', [(i, to(i)) for i in range(16)])  19.6 us
    ppermute x20, waiting for transfers between devices, along_seq(): return lax.ppermute(array, 'seq', [(i, to(i)) for i in range(16)])  14 us
    ppermute x2, starting transfers between devices, from_next(): return lax.ppermute(array, 'queue', [(i, i - 1) for i in range(1, 16)])  10.3 us
    ppermute x1, starting transfers between devices, shards(): following_across = lax.ppermute(inner, ('queue', 'seq'), pairs)  9.53 us
    pallas_call x2, Pallas kernels, attend(): pl.pallas_call(functools.partial(attend_kernel, frame), out_shape=jax.Sha...  8.13 us
    all_to_all x1, starting transfers between devices, shards(): lax.all_to_all(packed, 'seq', split_axis=0, concat_axis=0, tiled=True)  5.27 us
    pallas_call x1, Pallas kernels, shards(): pl.pallas_call(coefficient_kernel, out_shape=(jax.ShapeDtypeStruct((2, 3,...  4.06 us
    ppermute x2, waiting for transfers between devices, from_next(): return lax.ppermute(array, 'queue', [(i, i - 1) for i in range(1, 16)])  3.3 us
  transfers between devices with their start and end apart: 24, of which 10 were waited for; matrix products, arithmetic and copies ran while one was open for 5% of the time, Pallas kernels for 21%

profile of v5, /device:TPU:2, one launch (start us, length us, event | category | flops | bytes accessed | tf_op | source)
XLA Modules:
  0.0 95.5 jit_solution(5130479577669174937)
XLA Ops:
  0.7 2.2 %collective-permute-start.1 = (bf16[72,1152]{1,0:T(8,128)(2,1)}, bf16[72,1152]{1,0:T(8,128)(2,1)S(1)}, u32[]{:S(2)}, u32[]{:S(2)}) collective-permute-start(bf16[72,1152]{1,0:T(8,128)(2,1)} %bitcast.57), channel_id=1, source_target_pairs={{0,2},{1,3},{2,0},{3,1},{4,6},{5,7},{6,4},{7,5},{8,10},{9,11},{10,... | collective-permute-start | bytes 497672 | tf_op jit(solution)/shard_map/last_x/ppermute | solution.py:279
  2.9 3.2 %collective-permute-start = (bf16[72,1152]{1,0:T(8,128)(2,1)}, bf16[72,1152]{1,0:T(8,128)(2,1)S(1)}, u32[]{:S(2)}, u32[]{:S(2)}) collective-permute-start(bf16[72,1152]{1,0:T(8,128)(2,1)} %bitcast.63), channel_id=1, source_target_pairs={{0,8},{1,9},{2,10},{3,11},{4,12},{5,13},{6,14},{7,15},{8,0},{9,1},... | collective-permute-start | bytes 497672 | tf_op jit(solution)/shard_map/out_y/ppermute | solution.py:279
  6.8 2.6 %collective-permute-start.6 = (bf16[72,1152]{1,0:T(8,128)(2,1)}, bf16[72,1152]{1,0:T(8,128)(2,1)S(1)}, u32[]{:S(2)}, u32[]{:S(2)}) collective-permute-start(bf16[72,1152]{1,0:T(8,128)(2,1)} %bitcast.65), channel_id=1, source_target_pairs={{0,12},{1,13},{2,14},{3,15},{4,0},{5,1},{6,2},{7,3},{8,4},{9,5},{1... | collective-permute-start | bytes 497672 | tf_op jit(solution)/shard_map/out_y/ppermute | solution.py:279
  10.0 2.2 %pack.1 = (f32[16,40,128]{2,1,0:T(8,128)}, f32[16,128]{1,0:T(8,128)}) custom-call(s32[2]{0:T(128)} %levels_ref.1, f32[2,16,64]{2,1,0:T(8,128)} %bitcast.54, f32[16,1152]{1,0:T(8,128)} %embed_ref.5, f32[32,8,72]{2,1,0:T(8,128)} %table_ref.1, bf16[72,1152]{1,0:T(8,128)(2,1)} %copy-done.8), custom_call_target="tpu_custom_call" | custom-call | flops 2300000000 | bytes 1000 | tf_op jit(solution)/shard_map/pack/pallas_call | solution.py:350
  12.2 5.3 %all-to-all-start = ((f32[16,40,128]{2,1,0:T(8,128)}), f32[16,40,128]{2,1,0:T(8,128)S(1)}, u32[]{:S(2)}, u32[]{:S(2)}) async-start(f32[16,40,128]{2,1,0:T(8,128)} %get-tuple-element.14), calls=%async_computation | async-start | bytes 655360 | tf_op jit(solution)/shard_map/all_to_all | solution.py:361
  17.6 1.2 %pad_maximum_fusion = bf16[5,72,1152]{2,1,0:T(8,128)(2,1)S(1)} fusion(bf16[1,72,1152]{2,1,0:T(8,128)(2,1)} %bitcast.60, bf16[1,72,1152]{2,1,0:T(8,128)(2,1)S(1)} %bitcast.58, bf16[3,72,1152]{2,1,0:T(8,128)(2,1)S(1)} %select_bitcast_fusion), kind=kLoop, calls=%fused_computation | loop fusion | flops 829440 | bytes 1658880 | tf_op jit(solution)/shard_map/dynamic_update_slice | solution.py:370
  18.8 3.2 %collective-permute-start.3 = (bf16[5,72,1152]{2,1,0:T(8,128)(2,1)S(1)}, bf16[5,72,1152]{2,1,0:T(8,128)(2,1)}, u32[]{:S(2)}, u32[]{:S(2)}) collective-permute-start(bf16[5,72,1152]{2,1,0:T(8,128)(2,1)S(1)} %pad_maximum_fusion), channel_id=1, source_target_pairs={{0,12},{1,13},{2,14},{3,15},{4,0},{5,1},{6,2},{7,3},{8,4},{9,5},{1... | collective-permute-start | bytes 2488328 | tf_op jit(solution)/shard_map/five_y/ppermute | solution.py:279
  22.7 1.0 %pad_maximum_fusion.1 = bf16[4,72,1152]{2,1,0:T(8,128)(2,1)S(1)} fusion(bf16[1,72,1152]{2,1,0:T(8,128)(2,1)S(1)} %bitcast.62, bf16[1,72,1152]{2,1,0:T(8,128)(2,1)} %bitcast.68, bf16[1,72,1152]{2,1,0:T(8,128)(2,1)S(1)} %bitcast.67, bf16[1,72,1152]{2,1,0:T(8,128)(2,1)S(1)} %bitcast.66), kind=kLoop, calls=%fused_computation.3 | loop fusion | flops 995328 | bytes 1327104 | tf_op jit(solution)/shard_map/out_y/stack | solution.py:364
  23.8 3.1 %collective-permute-start.8 = (bf16[4,72,1152]{2,1,0:T(8,128)(2,1)S(1)}, bf16[4,72,1152]{2,1,0:T(8,128)(2,1)S(1)}, u32[]{:S(2)}, u32[]{:S(2)}) collective-permute-start(bf16[4,72,1152]{2,1,0:T(8,128)(2,1)S(1)} %pad_maximum_fusion.1), channel_id=1, source_target_pairs={{0,2},{1,3},{2,0},{3,1},{4,6},{5,7},{6,4},{7,5},{8,10},{9,11},{10,... | collective-permute-start | bytes 1990664 | tf_op jit(solution)/shard_map/out_x/ppermute | solution.py:279
  26.8 0.9 all-to-all-done.all_ref
  27.8 4.1 %coefficients.1 = (f32[2,3,32,1152]{3,2,1,0:T(8,128)S(1)}, f32[16,1152]{1,0:T(8,128)S(1)}, f32[2,16,1024]{2,1,0:T(8,128)S(1)}) custom-call(f32[16,40,128]{2,1,0:T(8,128)S(1)} %all-to-all-done.all_ref, f32[16,1152]{1,0:T(8,128)S(1)} %copy-done.1, bf16[3,1152,1152]{2,1,0:T(8,128)(2,1)} %bitcast.69), custom_call_target="tpu_custom_call" | custom-call | flops 23000000512 | bytes 1000 | tf_op jit(solution)/shard_map/coefficients/pallas_call | solution.py:374
  31.9 4.1 %attend.2.refs_0_ = bf16[64,1152]{1,0:T(8,128)(2,1)S(1)} custom-call(f32[16,128]{1,0:T(8,128)S(1)} %copy-done, f32[2,16,1024]{2,1,0:T(8,128)S(1)} %get-tuple-element.15.tokens_ref, f32[2,3,32,1152]{3,2,1,0:T(8,128)S(1)} %get-tuple-element.16.coef_ref), custom_call_target="tpu_custom_call" | custom-call | flops 115000000 | bytes 1000 | tf_op jit(solution)/shard_map/attend/pallas_call | solution.py:390
  35.9 4.1 %attend.3 = bf16[64,1152]{1,0:T(8,128)(2,1)S(1)} custom-call(f32[16,128]{1,0:T(8,128)S(1)} %copy-done, f32[2,16,1024]{2,1,0:T(8,128)S(1)} %get-tuple-element.15.tokens_ref, f32[2,3,32,1152]{3,2,1,0:T(8,128)S(1)} %get-tuple-element.16.coef_ref, bf16[64,1152]{1,0:T(8,128)(2,1)S(1)} %attend.2.refs_0_), custom_call_target="tpu_custom_call" | custom-call | flops 115000000 | bytes 1000 | tf_op jit(solution)/shard_map/attend/pallas_call | solution.py:390
  40.1 2.0 %collective-permute-done.8 = bf16[4,72,1152]{2,1,0:T(8,128)(2,1)S(1)} collective-permute-done((bf16[4,72,1152]{2,1,0:T(8,128)(2,1)S(1)}, bf16[4,72,1152]{2,1,0:T(8,128)(2,1)S(1)}, u32[]{:S(2)}, u32[]{:S(2)}) %collective-permute-start.8) | collective-permute-done | bytes 663584 | tf_op jit(solution)/shard_map/out_x/ppermute | solution.py:279
  42.7 1.9 %collective-permute-done.2 = bf16[5,72,1152]{2,1,0:T(8,128)(2,1)S(1)} collective-permute-done((bf16[5,72,1152]{2,1,0:T(8,128)(2,1)S(1)}, bf16[5,72,1152]{2,1,0:T(8,128)(2,1)S(1)}, u32[]{:S(2)}, u32[]{:S(2)}) %collective-permute-start.2) | collective-permute-done | bytes 829472 | tf_op jit(solution)/shard_map/five_y/ppermute | solution.py:279
  45.9 2.6 %hidden.1 = (f32[1152,128]{1,0:T(8,128)S(1)}, bf16[1152,128]{1,0:T(8,128)(2,1)S(1)}) custom-call(bf16[64,1152]{1,0:T(8,128)(2,1)S(1)} %broadcast_select_fusion.4.first_ref, bf16[64,1152]{1,0:T(8,128)(2,1)S(1)} %broadcast_select_fusion.3.second_ref, f32[2,16,64]{2,1,0:T(8,128)S(1)} %bitcast.55, f32[16,1152]{1,0:T(8,128)S(1)} %copy-done.1, ...), custom_call_target="tpu_custom_call" | custom-call | flops 2300000000 | bytes 1000 | tf_op jit(solution)/shard_map/hidden/pallas_call | solution.py:412
  48.6 9.5 %collective-permute-start.14 = (bf16[1152,128]{1,0:T(8,128)(2,1)S(1)}, bf16[1152,128]{1,0:T(8,128)(2,1)S(1)}, u32[]{:S(2)}, u32[]{:S(2)}) collective-permute-start(bf16[1152,128]{1,0:T(8,128)(2,1)S(1)} %get-tuple-element.18.refs_6_), channel_id=1, source_target_pairs={{16,2},{17,3},{18,0},{19,1},{20,6},{21,7},{22,4},{23,5},{24,10},{2... | collective-permute-start | bytes 884744 | tf_op jit(solution)/shard_map/inner/ppermute | solution.py:427
  58.1 1.2 %broadcast_select_fusion.1 = bf16[5,72,1152]{2,1,0:T(8,128)(2,1)S(1)} fusion(bf16[5,72,1152]{2,1,0:T(8,128)(2,1)} %collective-permute-done.3, pred[1152]{0:T(1024)(128)(4,1)S(1)} %compare_reduce_fusion.3), kind=kLoop, calls=%fused_computation.2 | loop fusion | flops 414720 | bytes 1660032 | tf_op jit(solution)/shard_map/jit(_where)/select_n | solution.py:325
  59.3 1.3 %collective-permute-start.16 = (bf16[1152,128]{1,0:T(8,128)(2,1)S(1)}, bf16[1152,128]{1,0:T(8,128)(2,1)S(1)}, u32[]{:S(2)}, u32[]{:S(2)}) collective-permute-start(bf16[1152,128]{1,0:T(8,128)(2,1)S(1)} %get-tuple-element.18.refs_6_), channel_id=1, source_target_pairs={{0,2},{1,3},{2,0},{3,1},{4,6},{5,7},{6,4},{7,5},{8,10},{9,11},{10,... | collective-permute-start | bytes 884744 | tf_op jit(solution)/shard_map/inner/ppermute | solution.py:279
  60.6 3.8 %collective-permute-start.11 = (bf16[1152,128]{1,0:T(8,128)(2,1)S(1)}, bf16[1152,128]{1,0:T(8,128)(2,1)S(1)}, u32[]{:S(2)}, u32[]{:S(2)}) collective-permute-start(bf16[1152,128]{1,0:T(8,128)(2,1)S(1)} %get-tuple-element.18.refs_6_), channel_id=1, source_target_pairs={{16,0},{32,16},{48,32},{64,48},{80,64},{96,80},{112,96},{128,112},... | collective-permute-start | bytes 884744 | tf_op jit(solution)/shard_map/inner/ppermute | solution.py:299
  64.4 2.3 %collective-permute-done.14 = bf16[1152,128]{1,0:T(8,128)(2,1)S(1)} collective-permute-done((bf16[1152,128]{1,0:T(8,128)(2,1)S(1)}, bf16[1152,128]{1,0:T(8,128)(2,1)S(1)}, u32[]{:S(2)}, u32[]{:S(2)}) %collective-permute-start.14) | collective-permute-done | bytes 294944 | tf_op jit(solution)/shard_map/inner/ppermute | solution.py:427
  67.0 2.3 %collective-permute-done.16.refs_6_ = bf16[1152,128]{1,0:T(8,128)(2,1)S(1)} collective-permute-done((bf16[1152,128]{1,0:T(8,128)(2,1)S(1)}, bf16[1152,128]{1,0:T(8,128)(2,1)S(1)}, u32[]{:S(2)}, u32[]{:S(2)}) %collective-permute-start.16) | collective-permute-done | bytes 294944 | tf_op jit(solution)/shard_map/inner/ppermute | solution.py:279
  69.9 2.0 %collective-permute-done.11.refs_4_ = bf16[1152,128]{1,0:T(8,128)(2,1)S(1)} collective-permute-done((bf16[1152,128]{1,0:T(8,128)(2,1)S(1)}, bf16[1152,128]{1,0:T(8,128)(2,1)S(1)}, u32[]{:S(2)}, u32[]{:S(2)}) %collective-permute-start.11) | collective-permute-done | bytes 294944 | tf_op jit(solution)/shard_map/inner/ppermute | solution.py:299
  72.5 1.3 %temporal_across.1 = bf16[288,256]{1,0:T(8,128)(2,1)S(1)} custom-call(s32[1]{0:T(128)S(6)} %copy.13.advance_ref, bf16[360,1152]{1,0:T(8,128)(2,1)S(1)} %bitcast.37, bf16[360,1152]{1,0:T(8,128)(2,1)S(1)} %bitcast.45, bf16[360,1152]{1,0:T(8,128)(2,1)S(1)} %bitcast.40, bf16[360,1152]{1,0:T(8,128)(2,1)S(1)} %bitcast.48, ...), custom_call_target="tpu_custom_call" | custom-call | flops 2300000000 | bytes 1000 | tf_op jit(solution)/shard_map/temporal_across/pallas_call | solution.py:438
  73.9 1.2 %collective-permute-start.18 = (bf16[288,256]{1,0:T(8,128)(2,1)S(1)}, bf16[288,256]{1,0:T(8,128)(2,1)S(1)}, u32[]{:S(2)}, u32[]{:S(2)}) collective-permute-start(bf16[288,256]{1,0:T(8,128)(2,1)S(1)} %temporal_across.1), channel_id=1, source_target_pairs={{0,2},{1,3},{2,0},{3,1},{4,6},{5,7},{6,4},{7,5},{8,10},{9,11},{10,... | collective-permute-start | bytes 442376 | tf_op jit(solution)/shard_map/back/ppermute | solution.py:279
  75.1 1.3 %temporal_near.1.near_ref = bf16[288,256]{1,0:T(8,128)(2,1)S(1)} custom-call(s32[1]{0:T(128)S(6)} %copy.13.advance_ref, bf16[360,1152]{1,0:T(8,128)(2,1)S(1)} %bitcast.38, bf16[360,1152]{1,0:T(8,128)(2,1)S(1)} %bitcast.46, bf16[360,1152]{1,0:T(8,128)(2,1)S(1)} %bitcast.41, bf16[360,1152]{1,0:T(8,128)(2,1)S(1)} %bitcast.49, ...), custom_call_target="tpu_custom_call" | custom-call | flops 2300000000 | bytes 1000 | tf_op jit(solution)/shard_map/temporal_near/pallas_call | solution.py:438
  76.8 5.0 %collective-permute-done.18.across_ref = bf16[288,256]{1,0:T(8,128)(2,1)S(1)} collective-permute-done((bf16[288,256]{1,0:T(8,128)(2,1)S(1)}, bf16[288,256]{1,0:T(8,128)(2,1)S(1)}, u32[]{:S(2)}, u32[]{:S(2)}) %collective-permute-start.18) | collective-permute-done | bytes 147488 | tf_op jit(solution)/shard_map/back/ppermute | solution.py:279
  81.7 1.4 %collective-permute-done.20.across_peer_ref = bf16[288,256]{1,0:T(8,128)(2,1)S(1)} collective-permute-done((bf16[288,256]{1,0:T(8,128)(2,1)S(1)}, bf16[288,256]{1,0:T(8,128)(2,1)S(1)}, u32[]{:S(2)}, u32[]{:S(2)}) %collective-permute-start.20) | collective-permute-done | bytes 147488 | tf_op jit(solution)/shard_map/back/ppermute | solution.py:279
  84.0 1.4 %collective-permute-done.21.peer_ref = f32[576,128]{1,0:T(8,128)S(1)} collective-permute-done((f32[576,128]{1,0:T(8,128)S(1)}, f32[576,128]{1,0:T(8,128)S(1)}, u32[]{:S(2)}, u32[]{:S(2)}) %collective-permute-start.21) | collective-permute-done | bytes 294944 | tf_op jit(solution)/shard_map/update/ppermute | solution.py:279
  85.4 1.7 %final.1 = (f32[2,16,64]{2,1,0:T(8,128)}, f32[2,16,64]{2,1,0:T(8,128)S(1)}) custom-call(f32[576,128]{1,0:T(8,128)S(1)} %get-tuple-element.19.own_ref, f32[576,128]{1,0:T(8,128)S(1)} %collective-permute-done.21.peer_ref, f32[1152,128]{1,0:T(8,128)S(1)} %get-tuple-element.21.hidden_ref, f32[2,16,64]{2,1,0:T(8,128)S(1)} %bitcast.56, ...), custom_call_target="tpu_custom_call" | custom-call | flops 2300000000 | bytes 1000 | tf_op jit(solution)/shard_map/final/pallas_call | solution.py:465
  87.1 6.5 %collective-permute-start.22 = (f32[16,64]{1,0:T(8,128)S(1)}, f32[16,64]{1,0:T(8,128)S(1)}, u32[]{:S(2)}, u32[]{:S(2)}) collective-permute-start(f32[16,64]{1,0:T(8,128)S(1)} %get-tuple-element.27), channel_id=1, source_target_pairs={{16,0},{32,16},{48,32},{64,48},{80,64},{96,80},{112,96},{128,112},... | collective-permute-start | bytes 12296 | tf_op jit(solution)/shard_map/ppermute | solution.py:299
  93.6 1.3 %collective-permute-done.22 = f32[16,64]{1,0:T(8,128)S(1)} collective-permute-done((f32[16,64]{1,0:T(8,128)S(1)}, f32[16,64]{1,0:T(8,128)S(1)}, u32[]{:S(2)}, u32[]{:S(2)}) %collective-permute-start.22) | collective-permute-done | bytes 4128 | tf_op jit(solution)/shard_map/ppermute | solution.py:299
  (71 shorter events, 6.8 us)
Async XLA Ops:
  0.6 17.0 %copy-start.6 = (bf16[1152,72]{0,1:T(8,128)(2,1)S(1)}, bf16[1152,72]{0,1:T(8,128)(2,1)}, u32[]{:S(2)}) copy-start(bf16[1152,72]{0,1:T(8,128)(2,1)} %param.20) | copy-start | bytes 497668
  0.6 22.1 %copy-start.11 = (bf16[1152,72]{0,1:T(8,128)(2,1)S(1)}, bf16[1152,72]{0,1:T(8,128)(2,1)}, u32[]{:S(2)}) copy-start(bf16[1152,72]{0,1:T(8,128)(2,1)} %param.18) | copy-start | bytes 497668
  0.7 27.1 %copy-start.1 = (f32[16,1152]{1,0:T(8,128)S(1)}, f32[16,1152]{1,0:T(8,128)}, u32[]{:S(2)}) copy-start(f32[16,1152]{1,0:T(8,128)} %embed_ref.5) | copy-start | bytes 221188
  0.7 8.6 %collective-permute-start.1 = (bf16[72,1152]{1,0:T(8,128)(2,1)}, bf16[72,1152]{1,0:T(8,128)(2,1)S(1)}, u32[]{:S(2)}, u32[]{:S(2)}) collective-permute-start(bf16[72,1152]{1,0:T(8,128)(2,1)} %bitcast.57), channel_id=1, source_target_pairs={{0,2},{1,3},{2,0},{3,1},{4,6},{5,7},{6,4},{7,5},{8,10},{9,11},{10,... | collective-permute-start | bytes 497672 | tf_op jit(solution)/shard_map/last_x/ppermute | solution.py:279
  2.9 14.6 %collective-permute-start = (bf16[72,1152]{1,0:T(8,128)(2,1)}, bf16[72,1152]{1,0:T(8,128)(2,1)S(1)}, u32[]{:S(2)}, u32[]{:S(2)}) collective-permute-start(bf16[72,1152]{1,0:T(8,128)(2,1)} %bitcast.63), channel_id=1, source_target_pairs={{0,8},{1,9},{2,10},{3,11},{4,12},{5,13},{6,14},{7,15},{8,0},{9,1},... | collective-permute-start | bytes 497672 | tf_op jit(solution)/shard_map/out_y/ppermute | solution.py:279
  6.1 16.0 %collective-permute-start.5 = (bf16[72,1152]{1,0:T(8,128)(2,1)}, bf16[72,1152]{1,0:T(8,128)(2,1)S(1)}, u32[]{:S(2)}, u32[]{:S(2)}) collective-permute-start(bf16[72,1152]{1,0:T(8,128)(2,1)} %bitcast.64), channel_id=1, source_target_pairs={{0,4},{1,5},{2,6},{3,7},{4,8},{5,9},{6,10},{7,11},{8,12},{9,13},{1... | collective-permute-start | bytes 497672 | tf_op jit(solution)/shard_map/out_y/ppermute | solution.py:279
  6.8 15.3 %collective-permute-start.6 = (bf16[72,1152]{1,0:T(8,128)(2,1)}, bf16[72,1152]{1,0:T(8,128)(2,1)S(1)}, u32[]{:S(2)}, u32[]{:S(2)}) collective-permute-start(bf16[72,1152]{1,0:T(8,128)(2,1)} %bitcast.65), channel_id=1, source_target_pairs={{0,12},{1,13},{2,14},{3,15},{4,0},{5,1},{6,2},{7,3},{8,4},{9,5},{1... | collective-permute-start | bytes 497672 | tf_op jit(solution)/shard_map/out_y/ppermute | solution.py:279
  12.2 15.6 %all-to-all-start = ((f32[16,40,128]{2,1,0:T(8,128)}), f32[16,40,128]{2,1,0:T(8,128)S(1)}, u32[]{:S(2)}, u32[]{:S(2)}) async-start(f32[16,40,128]{2,1,0:T(8,128)} %get-tuple-element.14), calls=%async_computation | async-start | bytes 655360 | tf_op jit(solution)/shard_map/all_to_all | solution.py:361
  18.8 26.3 %collective-permute-start.3 = (bf16[5,72,1152]{2,1,0:T(8,128)(2,1)S(1)}, bf16[5,72,1152]{2,1,0:T(8,128)(2,1)}, u32[]{:S(2)}, u32[]{:S(2)}) collective-permute-start(bf16[5,72,1152]{2,1,0:T(8,128)(2,1)S(1)} %pad_maximum_fusion), channel_id=1, source_target_pairs={{0,12},{1,13},{2,14},{3,15},{4,0},{5,1},{6,2},{7,3},{8,4},{9,5},{1... | collective-permute-start | bytes 2488328 | tf_op jit(solution)/shard_map/five_y/ppermute | solution.py:279
  22.0 22.5 %collective-permute-start.2 = (bf16[5,72,1152]{2,1,0:T(8,128)(2,1)S(1)}, bf16[5,72,1152]{2,1,0:T(8,128)(2,1)S(1)}, u32[]{:S(2)}, u32[]{:S(2)}) collective-permute-start(bf16[5,72,1152]{2,1,0:T(8,128)(2,1)S(1)} %pad_maximum_fusion), channel_id=1, source_target_pairs={{0,4},{1,5},{2,6},{3,7},{4,8},{5,9},{6,10},{7,11},{8,12},{9,13},{1... | collective-permute-start | bytes 2488328 | tf_op jit(solution)/shard_map/five_y/ppermute | solution.py:279
  23.8 18.3 %collective-permute-start.8 = (bf16[4,72,1152]{2,1,0:T(8,128)(2,1)S(1)}, bf16[4,72,1152]{2,1,0:T(8,128)(2,1)S(1)}, u32[]{:S(2)}, u32[]{:S(2)}) collective-permute-start(bf16[4,72,1152]{2,1,0:T(8,128)(2,1)S(1)} %pad_maximum_fusion.1), channel_id=1, source_target_pairs={{0,2},{1,3},{2,0},{3,1},{4,6},{5,7},{6,4},{7,5},{8,10},{9,11},{10,... | collective-permute-start | bytes 1990664 | tf_op jit(solution)/shard_map/out_x/ppermute | solution.py:279
  26.8 19.1 %collective-permute-start.7 = (bf16[4,72,1152]{2,1,0:T(8,128)(2,1)S(1)}, bf16[4,72,1152]{2,1,0:T(8,128)(2,1)}, u32[]{:S(2)}, u32[]{:S(2)}) collective-permute-start(bf16[4,72,1152]{2,1,0:T(8,128)(2,1)S(1)} %pad_maximum_fusion.1), channel_id=1, source_target_pairs={{0,1},{1,0},{2,3},{3,2},{4,5},{5,4},{6,7},{7,6},{8,9},{9,8},{10,11... | collective-permute-start | bytes 1990664 | tf_op jit(solution)/shard_map/out_core/ppermute | solution.py:279
  27.8 16.9 %copy-start.5 = (bf16[3,72,1152]{2,1,0:T(8,128)(2,1)S(1)}, bf16[3,72,1152]{2,1,0:T(8,128)(2,1)}, u32[]{:S(2)}) copy-start(bf16[3,72,1152]{2,1,0:T(8,128)(2,1)} %copy-done.4) | copy-start | bytes 1492996
  27.8 16.9 %copy-start.7 = (bf16[1152,72]{0,1:T(8,128)(2,1)S(1)}, bf16[1152,72]{0,1:T(8,128)(2,1)}, u32[]{:S(2)}) copy-start(bf16[1152,72]{0,1:T(8,128)(2,1)} %param.20) | copy-start | bytes 497668
  27.8 16.9 %copy-start.9 = (bf16[72,1152]{1,0:T(8,128)(2,1)S(1)}, bf16[72,1152]{1,0:T(8,128)(2,1)}, u32[]{:S(2)}) copy-start(bf16[72,1152]{1,0:T(8,128)(2,1)} %copy-done.8) | copy-start | bytes 497668
  27.8 18.1 %copy-start.3 = (f32[2,64,16]{1,2,0:T(8,128)S(1)}, f32[2,64,16]{1,2,0:T(8,128)}, u32[]{:S(2)}) copy-start(f32[2,64,16]{1,2,0:T(8,128)} %param.11) | copy-start | bytes 24580
  42.1 3.8 %collective-permute-start.9 = (bf16[2,72,1152]{2,1,0:T(8,128)(2,1)S(1)}, bf16[2,72,1152]{2,1,0:T(8,128)(2,1)S(1)}, u32[]{:S(2)}, u32[]{:S(2)}) collective-permute-start(bf16[2,72,1152]{2,1,0:T(8,128)(2,1)S(1)} %get-tuple-element.25), channel_id=1, source_target_pairs={{0,1},{1,0},{2,3},{3,2},{4,5},{5,4},{6,7},{7,6},{8,9},{9,8},{10,11... | collective-permute-start | bytes 995336 | tf_op jit(solution)/shard_map/out_core/ppermute | solution.py:279
  42.2 3.7 %collective-permute-start.10 = (bf16[2,72,1152]{2,1,0:T(8,128)(2,1)S(1)}, bf16[2,72,1152]{2,1,0:T(8,128)(2,1)S(1)}, u32[]{:S(2)}, u32[]{:S(2)}) collective-permute-start(bf16[2,72,1152]{2,1,0:T(8,128)(2,1)S(1)} %get-tuple-element.24), channel_id=1, source_target_pairs={{0,1},{1,0},{2,3},{3,2},{4,5},{5,4},{6,7},{7,6},{8,9},{9,8},{10,11... | collective-permute-start | bytes 995336 | tf_op jit(solution)/shard_map/out_core/ppermute | solution.py:279
  44.9 27.7 %collective-permute-start.4 = (bf16[5,72,1152]{2,1,0:T(8,128)(2,1)S(1)}, bf16[5,72,1152]{2,1,0:T(8,128)(2,1)S(1)}, u32[]{:S(2)}, u32[]{:S(2)}) collective-permute-start(bf16[5,72,1152]{2,1,0:T(8,128)(2,1)S(1)} %broadcast_select_fusion), channel_id=1, source_target_pairs={{0,8},{1,9},{2,10},{3,11},{4,12},{5,13},{6,14},{7,15},{8,0},{9,1},... | collective-permute-start | bytes 2488328 | tf_op jit(solution)/shard_map/five_far/ppermute | solution.py:279
  48.6 18.1 %collective-permute-start.14 = (bf16[1152,128]{1,0:T(8,128)(2,1)S(1)}, bf16[1152,128]{1,0:T(8,128)(2,1)S(1)}, u32[]{:S(2)}, u32[]{:S(2)}) collective-permute-start(bf16[1152,128]{1,0:T(8,128)(2,1)S(1)} %get-tuple-element.18.refs_6_), channel_id=1, source_target_pairs={{16,2},{17,3},{18,0},{19,1},{20,6},{21,7},{22,4},{23,5},{24,10},{2... | collective-permute-start | bytes 884744 | tf_op jit(solution)/shard_map/inner/ppermute | solution.py:427
  59.3 10.0 %collective-permute-start.16 = (bf16[1152,128]{1,0:T(8,128)(2,1)S(1)}, bf16[1152,128]{1,0:T(8,128)(2,1)S(1)}, u32[]{:S(2)}, u32[]{:S(2)}) collective-permute-start(bf16[1152,128]{1,0:T(8,128)(2,1)S(1)} %get-tuple-element.18.refs_6_), channel_id=1, source_target_pairs={{0,2},{1,3},{2,0},{3,1},{4,6},{5,7},{6,4},{7,5},{8,10},{9,11},{10,... | collective-permute-start | bytes 884744 | tf_op jit(solution)/shard_map/inner/ppermute | solution.py:279
  60.6 11.3 %collective-permute-start.11 = (bf16[1152,128]{1,0:T(8,128)(2,1)S(1)}, bf16[1152,128]{1,0:T(8,128)(2,1)S(1)}, u32[]{:S(2)}, u32[]{:S(2)}) collective-permute-start(bf16[1152,128]{1,0:T(8,128)(2,1)S(1)} %get-tuple-element.18.refs_6_), channel_id=1, source_target_pairs={{16,0},{32,16},{48,32},{64,48},{80,64},{96,80},{112,96},{128,112},... | collective-permute-start | bytes 884744 | tf_op jit(solution)/shard_map/inner/ppermute | solution.py:299
  66.7 5.8 %collective-permute-start.15 = (bf16[1152,128]{1,0:T(8,128)(2,1)S(1)}, bf16[1152,128]{1,0:T(8,128)(2,1)S(1)}, u32[]{:S(2)}, u32[]{:S(2)}) collective-permute-start(bf16[1152,128]{1,0:T(8,128)(2,1)S(1)} %broadcast_select_fusion.2.refs_4_), channel_id=1, source_target_pairs={{0,1},{1,0},{2,3},{3,2},{4,5},{5,4},{6,7},{7,6},{8,9},{9,8},{10,11... | collective-permute-start | bytes 884744 | tf_op jit(solution)/shard_map/inner_core/ppermute | solution.py:279
  69.4 3.1 %collective-permute-start.17 = (bf16[1152,128]{1,0:T(8,128)(2,1)S(1)}, bf16[1152,128]{1,0:T(8,128)(2,1)S(1)}, u32[]{:S(2)}, u32[]{:S(2)}) collective-permute-start(bf16[1152,128]{1,0:T(8,128)(2,1)S(1)} %collective-permute-done.16.refs_6_), channel_id=1, source_target_pairs={{0,1},{1,0},{2,3},{3,2},{4,5},{5,4},{6,7},{7,6},{8,9},{9,8},{10,11... | collective-permute-start | bytes 884744 | tf_op jit(solution)/shard_map/inner_core/ppermute | solution.py:279
  69.4 5.7 %collective-permute-start.13 = (bf16[1152,128]{1,0:T(8,128)(2,1)S(1)}, bf16[1152,128]{1,0:T(8,128)(2,1)S(1)}, u32[]{:S(2)}, u32[]{:S(2)}) collective-permute-start(bf16[1152,128]{1,0:T(8,128)(2,1)S(1)} %get-tuple-element.18.refs_6_), channel_id=1, source_target_pairs={{0,1},{1,0},{2,3},{3,2},{4,5},{5,4},{6,7},{7,6},{8,9},{9,8},{10,11... | collective-permute-start | bytes 884744 | tf_op jit(solution)/shard_map/inner_core/ppermute | solution.py:279
  71.8 3.3 %collective-permute-start.12 = (bf16[1152,128]{1,0:T(8,128)(2,1)S(1)}, bf16[1152,128]{1,0:T(8,128)(2,1)S(1)}, u32[]{:S(2)}, u32[]{:S(2)}) collective-permute-start(bf16[1152,128]{1,0:T(8,128)(2,1)S(1)} %collective-permute-done.11.refs_4_), channel_id=1, source_target_pairs={{0,1},{1,0},{2,3},{3,2},{4,5},{5,4},{6,7},{7,6},{8,9},{9,8},{10,11... | collective-permute-start | bytes 884744 | tf_op jit(solution)/shard_map/inner_core/ppermute | solution.py:279
  73.9 7.9 %collective-permute-start.18 = (bf16[288,256]{1,0:T(8,128)(2,1)S(1)}, bf16[288,256]{1,0:T(8,128)(2,1)S(1)}, u32[]{:S(2)}, u32[]{:S(2)}) collective-permute-start(bf16[288,256]{1,0:T(8,128)(2,1)S(1)} %temporal_across.1), channel_id=1, source_target_pairs={{0,2},{1,3},{2,0},{3,1},{4,6},{5,7},{6,4},{7,5},{8,10},{9,11},{10,... | collective-permute-start | bytes 442376 | tf_op jit(solution)/shard_map/back/ppermute | solution.py:279
  76.4 18.5 %copy-start.13 = (f32[64,16]{0,1:T(8,128)S(1)}, f32[64,16]{0,1:T(8,128)}, u32[]{:S(2)}) copy-start(f32[64,16]{0,1:T(8,128)} %param.14) | copy-start | bytes 12292
  76.4 5.3 %collective-permute-start.19 = (bf16[288,256]{1,0:T(8,128)(2,1)S(1)}, bf16[288,256]{1,0:T(8,128)(2,1)S(1)}, u32[]{:S(2)}, u32[]{:S(2)}) collective-permute-start(bf16[288,256]{1,0:T(8,128)(2,1)S(1)} %temporal_near.1.near_ref), channel_id=1, source_target_pairs={{0,1},{1,0},{2,3},{3,2},{4,5},{5,4},{6,7},{7,6},{8,9},{9,8},{10,11... | collective-permute-start | bytes 442376 | tf_op jit(solution)/shard_map/back/ppermute | solution.py:279
  81.7 1.4 %collective-permute-start.20 = (bf16[288,256]{1,0:T(8,128)(2,1)S(1)}, bf16[288,256]{1,0:T(8,128)(2,1)S(1)}, u32[]{:S(2)}, u32[]{:S(2)}) collective-permute-start(bf16[288,256]{1,0:T(8,128)(2,1)S(1)} %collective-permute-done.18.across_ref), channel_id=1, source_target_pairs={{0,1},{1,0},{2,3},{3,2},{4,5},{5,4},{6,7},{7,6},{8,9},{9,8},{10,11... | collective-permute-start | bytes 442376 | tf_op jit(solution)/shard_map/back/ppermute | solution.py:279
  83.7 1.7 %collective-permute-start.21 = (f32[576,128]{1,0:T(8,128)S(1)}, f32[576,128]{1,0:T(8,128)S(1)}, u32[]{:S(2)}, u32[]{:S(2)}) collective-permute-start(f32[576,128]{1,0:T(8,128)S(1)} %get-tuple-element.20), channel_id=1, source_target_pairs={{0,1},{1,0},{2,3},{3,2},{4,5},{5,4},{6,7},{7,6},{8,9},{9,8},{10,11... | collective-permute-start | bytes 884744 | tf_op jit(solution)/shard_map/update/ppermute | solution.py:279
  87.1 7.8 %collective-permute-start.22 = (f32[16,64]{1,0:T(8,128)S(1)}, f32[16,64]{1,0:T(8,128)S(1)}, u32[]{:S(2)}, u32[]{:S(2)}) collective-permute-start(f32[16,64]{1,0:T(8,128)S(1)} %get-tuple-element.27), channel_id=1, source_target_pairs={{16,0},{32,16},{48,32},{64,48},{80,64},{96,80},{112,96},{128,112},... | collective-permute-start | bytes 12296 | tf_op jit(solution)/shard_map/ppermute | solution.py:299
  (6 other events, 35.1 us)

commit v6 on v5

--- a/solution.py
+++ b/solution.py
@@ -248,13 +248,13 @@
         product = dot_nn(block[3 * HD : 5 * HD], mix)
         rows = slice(2 * HD * place, 2 * HD * (place + 1))
         own_ref[rows, :] = product[:, 0:128]
-        peer_ref[rows, :] = product[:, 128:256]
+        peer_ref[rows, :] = product[:, 128:256].astype(BF)
 
 
 def final_kernel(own_ref, peer_ref, hidden_ref, latents_ref, mod_ref, final_ref, velocity_ref, updated_ref, update_ref):
     me = lax.axis_index("seq")
     place_rows(update_ref, own_ref[...], pair_order(me))
-    place_rows(update_ref, peer_ref[...], pair_order(me ^ 1))
+    place_rows(update_ref, peer_ref[...].astype(F32), pair_order(me ^ 1))
     gate, shift, scale = modulation_columns(mod_ref[...], (5, 6, 7))
     hidden = hidden_ref[...] + gate * update_ref[...]
     inner = (normalize(hidden) * (1.0 + scale) + shift).astype(BF)
@@ -452,7 +452,7 @@
         near_peer, across_peer = other_core(near), other_core(across)
     update_own, update_peer = pl.pallas_call(
         output_kernel,
-        out_shape=(jax.ShapeDtypeStruct((8 * HD, 128), F32),) * 2,
+        out_shape=tuple(jax.ShapeDtypeStruct((8 * HD, 128), kind) for kind in (F32, BF)),
         in_specs=[VMEM] * 8,
         out_specs=(VMEM,) * 2,
         scratch_shapes=[pltpu.VMEM((D, 256), F32)],

time: 96.2 us -> 96 us (level)
  no operation moved by 1% of the time
where the time goes in v6:
time: 96 us; the launch traced here: 95.3 us
  starting transfers between devices  44.7 us (47%)
  Pallas kernels  22 us (23%)
  waiting for transfers between devices  20.3 us (21%)
  other arithmetic  5.28 us (6%)
  between operations  1.66 us (2%)
  local copies, waits for them, and re-layouts  1.4 us (1%)
    ppermute x20, starting transfers between devices, along_seq(): return lax.ppermute(array, 'seq', [(i, to(i)) for i in range(16)])  19.6 us
    ppermute x20, waiting for transfers between devices, along_seq(): return lax.ppermute(array, 'seq', [(i, to(i)) for i in range(16)])  13.8 us
    ppermute x2, starting transfers between devices, from_next(): return lax.ppermute(array, 'queue', [(i, i - 1) for i in range(1, 16)])  10.3 us
    ppermute x1, starting transfers between devices, shards(): following_across = lax.ppermute(inner, ('queue', 'seq'), pairs)  9.53 us
    pallas_call x2, Pallas kernels, attend(): pl.pallas_call(functools.partial(attend_kernel, frame), out_shape=jax.Sha...  8.13 us
    all_to_all x1, starting transfers between devices, shards(): lax.all_to_all(packed, 'seq', split_axis=0, concat_axis=0, tiled=True)  5.27 us
    pallas_call x1, Pallas kernels, shards(): pl.pallas_call(coefficient_kernel, out_shape=(jax.ShapeDtypeStruct((2, 3,...  4.06 us
    ppermute x2, waiting for transfers between devices, from_next(): return lax.ppermute(array, 'queue', [(i, i - 1) for i in range(1, 16)])  3.3 us
  transfers between devices with their start and end apart: 24, of which 10 were waited for; matrix products, arithmetic and copies ran while one was open for 5% of the time, Pallas kernels for 21%

profile of v6, /device:TPU:2, one launch (start us, length us, event | category | flops | bytes accessed | tf_op | source)
XLA Modules:
  0.0 95.3 jit_solution(12333532485519824612)
XLA Ops:
  0.7 2.2 %collective-permute-start.1 = (bf16[72,1152]{1,0:T(8,128)(2,1)}, bf16[72,1152]{1,0:T(8,128)(2,1)S(1)}, u32[]{:S(2)}, u32[]{:S(2)}) collective-permute-start(bf16[72,1152]{1,0:T(8,128)(2,1)} %bitcast.57), channel_id=1, source_target_pairs={{0,2},{1,3},{2,0},{3,1},{4,6},{5,7},{6,4},{7,5},{8,10},{9,11},{10,... | collective-permute-start | bytes 497672 | tf_op jit(solution)/shard_map/last_x/ppermute | solution.py:279
  2.9 3.2 %collective-permute-start = (bf16[72,1152]{1,0:T(8,128)(2,1)}, bf16[72,1152]{1,0:T(8,128)(2,1)S(1)}, u32[]{:S(2)}, u32[]{:S(2)}) collective-permute-start(bf16[72,1152]{1,0:T(8,128)(2,1)} %bitcast.63), channel_id=1, source_target_pairs={{0,8},{1,9},{2,10},{3,11},{4,12},{5,13},{6,14},{7,15},{8,0},{9,1},... | collective-permute-start | bytes 497672 | tf_op jit(solution)/shard_map/out_y/ppermute | solution.py:279
  6.8 2.6 %collective-permute-start.6 = (bf16[72,1152]{1,0:T(8,128)(2,1)}, bf16[72,1152]{1,0:T(8,128)(2,1)S(1)}, u32[]{:S(2)}, u32[]{:S(2)}) collective-permute-start(bf16[72,1152]{1,0:T(8,128)(2,1)} %bitcast.65), channel_id=1, source_target_pairs={{0,12},{1,13},{2,14},{3,15},{4,0},{5,1},{6,2},{7,3},{8,4},{9,5},{1... | collective-permute-start | bytes 497672 | tf_op jit(solution)/shard_map/out_y/ppermute | solution.py:279
  10.0 2.2 %pack.1 = (f32[16,40,128]{2,1,0:T(8,128)}, f32[16,128]{1,0:T(8,128)}) custom-call(s32[2]{0:T(128)} %levels_ref.1, f32[2,16,64]{2,1,0:T(8,128)} %bitcast.54, f32[16,1152]{1,0:T(8,128)} %embed_ref.5, f32[32,8,72]{2,1,0:T(8,128)} %table_ref.1, bf16[72,1152]{1,0:T(8,128)(2,1)} %copy-done.8), custom_call_target="tpu_custom_call" | custom-call | flops 2300000000 | bytes 1000 | tf_op jit(solution)/shard_map/pack/pallas_call | solution.py:350
  12.2 5.3 %all-to-all-start = ((f32[16,40,128]{2,1,0:T(8,128)}), f32[16,40,128]{2,1,0:T(8,128)S(1)}, u32[]{:S(2)}, u32[]{:S(2)}) async-start(f32[16,40,128]{2,1,0:T(8,128)} %get-tuple-element.14), calls=%async_computation | async-start | bytes 655360 | tf_op jit(solution)/shard_map/all_to_all | solution.py:361
  17.6 1.2 %pad_maximum_fusion = bf16[5,72,1152]{2,1,0:T(8,128)(2,1)S(1)} fusion(bf16[1,72,1152]{2,1,0:T(8,128)(2,1)} %bitcast.60, bf16[1,72,1152]{2,1,0:T(8,128)(2,1)S(1)} %bitcast.58, bf16[3,72,1152]{2,1,0:T(8,128)(2,1)S(1)} %select_bitcast_fusion), kind=kLoop, calls=%fused_computation | loop fusion | flops 829440 | bytes 1658880 | tf_op jit(solution)/shard_map/dynamic_update_slice | solution.py:370
  18.8 3.2 %collective-permute-start.3 = (bf16[5,72,1152]{2,1,0:T(8,128)(2,1)S(1)}, bf16[5,72,1152]{2,1,0:T(8,128)(2,1)}, u32[]{:S(2)}, u32[]{:S(2)}) collective-permute-start(bf16[5,72,1152]{2,1,0:T(8,128)(2,1)S(1)} %pad_maximum_fusion), channel_id=1, source_target_pairs={{0,12},{1,13},{2,14},{3,15},{4,0},{5,1},{6,2},{7,3},{8,4},{9,5},{1... | collective-permute-start | bytes 2488328 | tf_op jit(solution)/shard_map/five_y/ppermute | solution.py:279
  22.7 1.0 %pad_maximum_fusion.1 = bf16[4,72,1152]{2,1,0:T(8,128)(2,1)S(1)} fusion(bf16[1,72,1152]{2,1,0:T(8,128)(2,1)S(1)} %bitcast.62, bf16[1,72,1152]{2,1,0:T(8,128)(2,1)} %bitcast.68, bf16[1,72,1152]{2,1,0:T(8,128)(2,1)S(1)} %bitcast.67, bf16[1,72,1152]{2,1,0:T(8,128)(2,1)S(1)} %bitcast.66), kind=kLoop, calls=%fused_computation.3 | loop fusion | flops 995328 | bytes 1327104 | tf_op jit(solution)/shard_map/out_y/stack | solution.py:364
  23.8 3.1 %collective-permute-start.8 = (bf16[4,72,1152]{2,1,0:T(8,128)(2,1)S(1)}, bf16[4,72,1152]{2,1,0:T(8,128)(2,1)S(1)}, u32[]{:S(2)}, u32[]{:S(2)}) collective-permute-start(bf16[4,72,1152]{2,1,0:T(8,128)(2,1)S(1)} %pad_maximum_fusion.1), channel_id=1, source_target_pairs={{0,2},{1,3},{2,0},{3,1},{4,6},{5,7},{6,4},{7,5},{8,10},{9,11},{10,... | collective-permute-start | bytes 1990664 | tf_op jit(solution)/shard_map/out_x/ppermute | solution.py:279
  26.8 0.9 all-to-all-done.all_ref
  27.8 4.1 %coefficients.1 = (f32[2,3,32,1152]{3,2,1,0:T(8,128)S(1)}, f32[16,1152]{1,0:T(8,128)S(1)}, f32[2,16,1024]{2,1,0:T(8,128)S(1)}) custom-call(f32[16,40,128]{2,1,0:T(8,128)S(1)} %all-to-all-done.all_ref, f32[16,1152]{1,0:T(8,128)S(1)} %copy-done.1, bf16[3,1152,1152]{2,1,0:T(8,128)(2,1)} %bitcast.69), custom_call_target="tpu_custom_call" | custom-call | flops 23000000512 | bytes 1000 | tf_op jit(solution)/shard_map/coefficients/pallas_call | solution.py:374
  31.9 4.1 %attend.2.refs_0_ = bf16[64,1152]{1,0:T(8,128)(2,1)S(1)} custom-call(f32[16,128]{1,0:T(8,128)S(1)} %copy-done, f32[2,16,1024]{2,1,0:T(8,128)S(1)} %get-tuple-element.15.tokens_ref, f32[2,3,32,1152]{3,2,1,0:T(8,128)S(1)} %get-tuple-element.16.coef_ref), custom_call_target="tpu_custom_call" | custom-call | flops 115000000 | bytes 1000 | tf_op jit(solution)/shard_map/attend/pallas_call | solution.py:390
  35.9 4.1 %attend.3 = bf16[64,1152]{1,0:T(8,128)(2,1)S(1)} custom-call(f32[16,128]{1,0:T(8,128)S(1)} %copy-done, f32[2,16,1024]{2,1,0:T(8,128)S(1)} %get-tuple-element.15.tokens_ref, f32[2,3,32,1152]{3,2,1,0:T(8,128)S(1)} %get-tuple-element.16.coef_ref, bf16[64,1152]{1,0:T(8,128)(2,1)S(1)} %attend.2.refs_0_), custom_call_target="tpu_custom_call" | custom-call | flops 115000000 | bytes 1000 | tf_op jit(solution)/shard_map/attend/pallas_call | solution.py:390
  40.1 2.0 %collective-permute-done.8 = bf16[4,72,1152]{2,1,0:T(8,128)(2,1)S(1)} collective-permute-done((bf16[4,72,1152]{2,1,0:T(8,128)(2,1)S(1)}, bf16[4,72,1152]{2,1,0:T(8,128)(2,1)S(1)}, u32[]{:S(2)}, u32[]{:S(2)}) %collective-permute-start.8) | collective-permute-done | bytes 663584 | tf_op jit(solution)/shard_map/out_x/ppermute | solution.py:279
  42.7 1.9 %collective-permute-done.2 = bf16[5,72,1152]{2,1,0:T(8,128)(2,1)S(1)} collective-permute-done((bf16[5,72,1152]{2,1,0:T(8,128)(2,1)S(1)}, bf16[5,72,1152]{2,1,0:T(8,128)(2,1)S(1)}, u32[]{:S(2)}, u32[]{:S(2)}) %collective-permute-start.2) | collective-permute-done | bytes 829472 | tf_op jit(solution)/shard_map/five_y/ppermute | solution.py:279
  45.9 2.6 %hidden.1 = (f32[1152,128]{1,0:T(8,128)S(1)}, bf16[1152,128]{1,0:T(8,128)(2,1)S(1)}) custom-call(bf16[64,1152]{1,0:T(8,128)(2,1)S(1)} %broadcast_select_fusion.4.first_ref, bf16[64,1152]{1,0:T(8,128)(2,1)S(1)} %broadcast_select_fusion.3.second_ref, f32[2,16,64]{2,1,0:T(8,128)S(1)} %bitcast.55, f32[16,1152]{1,0:T(8,128)S(1)} %copy-done.1, ...), custom_call_target="tpu_custom_call" | custom-call | flops 2300000000 | bytes 1000 | tf_op jit(solution)/shard_map/hidden/pallas_call | solution.py:412
  48.6 9.5 %collective-permute-start.14 = (bf16[1152,128]{1,0:T(8,128)(2,1)S(1)}, bf16[1152,128]{1,0:T(8,128)(2,1)S(1)}, u32[]{:S(2)}, u32[]{:S(2)}) collective-permute-start(bf16[1152,128]{1,0:T(8,128)(2,1)S(1)} %get-tuple-element.18.refs_6_), channel_id=1, source_target_pairs={{16,2},{17,3},{18,0},{19,1},{20,6},{21,7},{22,4},{23,5},{24,10},{2... | collective-permute-start | bytes 884744 | tf_op jit(solution)/shard_map/inner/ppermute | solution.py:427
  58.1 1.2 %broadcast_select_fusion.1 = bf16[5,72,1152]{2,1,0:T(8,128)(2,1)S(1)} fusion(bf16[5,72,1152]{2,1,0:T(8,128)(2,1)} %collective-permute-done.3, pred[1152]{0:T(1024)(128)(4,1)S(1)} %compare_reduce_fusion.3), kind=kLoop, calls=%fused_computation.2 | loop fusion | flops 414720 | bytes 1660032 | tf_op jit(solution)/shard_map/jit(_where)/select_n | solution.py:325
  59.3 1.3 %collective-permute-start.16 = (bf16[1152,128]{1,0:T(8,128)(2,1)S(1)}, bf16[1152,128]{1,0:T(8,128)(2,1)S(1)}, u32[]{:S(2)}, u32[]{:S(2)}) collective-permute-start(bf16[1152,128]{1,0:T(8,128)(2,1)S(1)} %get-tuple-element.18.refs_6_), channel_id=1, source_target_pairs={{0,2},{1,3},{2,0},{3,1},{4,6},{5,7},{6,4},{7,5},{8,10},{9,11},{10,... | collective-permute-start | bytes 884744 | tf_op jit(solution)/shard_map/inner/ppermute | solution.py:279
  60.6 3.8 %collective-permute-start.11 = (bf16[1152,128]{1,0:T(8,128)(2,1)S(1)}, bf16[1152,128]{1,0:T(8,128)(2,1)S(1)}, u32[]{:S(2)}, u32[]{:S(2)}) collective-permute-start(bf16[1152,128]{1,0:T(8,128)(2,1)S(1)} %get-tuple-element.18.refs_6_), channel_id=1, source_target_pairs={{16,0},{32,16},{48,32},{64,48},{80,64},{96,80},{112,96},{128,112},... | collective-permute-start | bytes 884744 | tf_op jit(solution)/shard_map/inner/ppermute | solution.py:299
  64.4 2.3 %collective-permute-done.14 = bf16[1152,128]{1,0:T(8,128)(2,1)S(1)} collective-permute-done((bf16[1152,128]{1,0:T(8,128)(2,1)S(1)}, bf16[1152,128]{1,0:T(8,128)(2,1)S(1)}, u32[]{:S(2)}, u32[]{:S(2)}) %collective-permute-start.14) | collective-permute-done | bytes 294944 | tf_op jit(solution)/shard_map/inner/ppermute | solution.py:427
  67.0 2.3 %collective-permute-done.16.refs_6_ = bf16[1152,128]{1,0:T(8,128)(2,1)S(1)} collective-permute-done((bf16[1152,128]{1,0:T(8,128)(2,1)S(1)}, bf16[1152,128]{1,0:T(8,128)(2,1)S(1)}, u32[]{:S(2)}, u32[]{:S(2)}) %collective-permute-start.16) | collective-permute-done | bytes 294944 | tf_op jit(solution)/shard_map/inner/ppermute | solution.py:279
  69.9 2.0 %collective-permute-done.11.refs_4_ = bf16[1152,128]{1,0:T(8,128)(2,1)S(1)} collective-permute-done((bf16[1152,128]{1,0:T(8,128)(2,1)S(1)}, bf16[1152,128]{1,0:T(8,128)(2,1)S(1)}, u32[]{:S(2)}, u32[]{:S(2)}) %collective-permute-start.11) | collective-permute-done | bytes 294944 | tf_op jit(solution)/shard_map/inner/ppermute | solution.py:299
  72.5 1.3 %temporal_across.1 = bf16[288,256]{1,0:T(8,128)(2,1)S(1)} custom-call(s32[1]{0:T(128)S(6)} %copy.13.advance_ref, bf16[360,1152]{1,0:T(8,128)(2,1)S(1)} %bitcast.37, bf16[360,1152]{1,0:T(8,128)(2,1)S(1)} %bitcast.45, bf16[360,1152]{1,0:T(8,128)(2,1)S(1)} %bitcast.40, bf16[360,1152]{1,0:T(8,128)(2,1)S(1)} %bitcast.48, ...), custom_call_target="tpu_custom_call" | custom-call | flops 2300000000 | bytes 1000 | tf_op jit(solution)/shard_map/temporal_across/pallas_call | solution.py:438
  73.9 1.2 %collective-permute-start.18 = (bf16[288,256]{1,0:T(8,128)(2,1)S(1)}, bf16[288,256]{1,0:T(8,128)(2,1)S(1)}, u32[]{:S(2)}, u32[]{:S(2)}) collective-permute-start(bf16[288,256]{1,0:T(8,128)(2,1)S(1)} %temporal_across.1), channel_id=1, source_target_pairs={{0,2},{1,3},{2,0},{3,1},{4,6},{5,7},{6,4},{7,5},{8,10},{9,11},{10,... | collective-permute-start | bytes 442376 | tf_op jit(solution)/shard_map/back/ppermute | solution.py:279
  75.1 1.3 %temporal_near.1.near_ref = bf16[288,256]{1,0:T(8,128)(2,1)S(1)} custom-call(s32[1]{0:T(128)S(6)} %copy.13.advance_ref, bf16[360,1152]{1,0:T(8,128)(2,1)S(1)} %bitcast.38, bf16[360,1152]{1,0:T(8,128)(2,1)S(1)} %bitcast.46, bf16[360,1152]{1,0:T(8,128)(2,1)S(1)} %bitcast.41, bf16[360,1152]{1,0:T(8,128)(2,1)S(1)} %bitcast.49, ...), custom_call_target="tpu_custom_call" | custom-call | flops 2300000000 | bytes 1000 | tf_op jit(solution)/shard_map/temporal_near/pallas_call | solution.py:438
  76.8 5.0 %collective-permute-done.18.across_ref = bf16[288,256]{1,0:T(8,128)(2,1)S(1)} collective-permute-done((bf16[288,256]{1,0:T(8,128)(2,1)S(1)}, bf16[288,256]{1,0:T(8,128)(2,1)S(1)}, u32[]{:S(2)}, u32[]{:S(2)}) %collective-permute-start.18) | collective-permute-done | bytes 147488 | tf_op jit(solution)/shard_map/back/ppermute | solution.py:279
  81.7 1.4 %collective-permute-done.20.across_peer_ref = bf16[288,256]{1,0:T(8,128)(2,1)S(1)} collective-permute-done((bf16[288,256]{1,0:T(8,128)(2,1)S(1)}, bf16[288,256]{1,0:T(8,128)(2,1)S(1)}, u32[]{:S(2)}, u32[]{:S(2)}) %collective-permute-start.20) | collective-permute-done | bytes 147488 | tf_op jit(solution)/shard_map/back/ppermute | solution.py:279
  84.0 1.2 %collective-permute-done.21.peer_ref = bf16[576,128]{1,0:T(8,128)(2,1)S(1)} collective-permute-done((bf16[576,128]{1,0:T(8,128)(2,1)S(1)}, bf16[576,128]{1,0:T(8,128)(2,1)S(1)}, u32[]{:S(2)}, u32[]{:S(2)}) %collective-permute-start.21) | collective-permute-done | bytes 147488 | tf_op jit(solution)/shard_map/update/ppermute | solution.py:279
  85.2 1.7 %final.1 = (f32[2,16,64]{2,1,0:T(8,128)}, f32[2,16,64]{2,1,0:T(8,128)S(1)}) custom-call(f32[576,128]{1,0:T(8,128)S(1)} %get-tuple-element.19.own_ref, bf16[576,128]{1,0:T(8,128)(2,1)S(1)} %collective-permute-done.21.peer_ref, f32[1152,128]{1,0:T(8,128)S(1)} %get-tuple-element.21.hidden_ref, f32[2,16,64]{2,1,0:T(8,128)S(1)} %bitcast.56, ...), custom_call_target="tpu_custom_call" | custom-call | flops 2300000000 | bytes 1000 | tf_op jit(solution)/shard_map/final/pallas_call | solution.py:465
  86.9 6.5 %collective-permute-start.22 = (f32[16,64]{1,0:T(8,128)S(1)}, f32[16,64]{1,0:T(8,128)S(1)}, u32[]{:S(2)}, u32[]{:S(2)}) collective-permute-start(f32[16,64]{1,0:T(8,128)S(1)} %get-tuple-element.27), channel_id=1, source_target_pairs={{16,0},{32,16},{48,32},{64,48},{80,64},{96,80},{112,96},{128,112},... | collective-permute-start | bytes 12296 | tf_op jit(solution)/shard_map/ppermute | solution.py:299
  93.4 1.3 %collective-permute-done.22 = f32[16,64]{1,0:T(8,128)S(1)} collective-permute-done((f32[16,64]{1,0:T(8,128)S(1)}, f32[16,64]{1,0:T(8,128)S(1)}, u32[]{:S(2)}, u32[]{:S(2)}) %collective-permute-start.22) | collective-permute-done | bytes 4128 | tf_op jit(solution)/shard_map/ppermute | solution.py:299
  (71 shorter events, 6.8 us)
Async XLA Ops:
  0.6 17.0 %copy-start.6 = (bf16[1152,72]{0,1:T(8,128)(2,1)S(1)}, bf16[1152,72]{0,1:T(8,128)(2,1)}, u32[]{:S(2)}) copy-start(bf16[1152,72]{0,1:T(8,128)(2,1)} %param.20) | copy-start | bytes 497668
  0.6 22.1 %copy-start.11 = (bf16[1152,72]{0,1:T(8,128)(2,1)S(1)}, bf16[1152,72]{0,1:T(8,128)(2,1)}, u32[]{:S(2)}) copy-start(bf16[1152,72]{0,1:T(8,128)(2,1)} %param.18) | copy-start | bytes 497668
  0.7 27.1 %copy-start.1 = (f32[16,1152]{1,0:T(8,128)S(1)}, f32[16,1152]{1,0:T(8,128)}, u32[]{:S(2)}) copy-start(f32[16,1152]{1,0:T(8,128)} %embed_ref.5) | copy-start | bytes 221188
  0.7 8.6 %collective-permute-start.1 = (bf16[72,1152]{1,0:T(8,128)(2,1)}, bf16[72,1152]{1,0:T(8,128)(2,1)S(1)}, u32[]{:S(2)}, u32[]{:S(2)}) collective-permute-start(bf16[72,1152]{1,0:T(8,128)(2,1)} %bitcast.57), channel_id=1, source_target_pairs={{0,2},{1,3},{2,0},{3,1},{4,6},{5,7},{6,4},{7,5},{8,10},{9,11},{10,... | collective-permute-start | bytes 497672 | tf_op jit(solution)/shard_map/last_x/ppermute | solution.py:279
  2.9 14.6 %collective-permute-start = (bf16[72,1152]{1,0:T(8,128)(2,1)}, bf16[72,1152]{1,0:T(8,128)(2,1)S(1)}, u32[]{:S(2)}, u32[]{:S(2)}) collective-permute-start(bf16[72,1152]{1,0:T(8,128)(2,1)} %bitcast.63), channel_id=1, source_target_pairs={{0,8},{1,9},{2,10},{3,11},{4,12},{5,13},{6,14},{7,15},{8,0},{9,1},... | collective-permute-start | bytes 497672 | tf_op jit(solution)/shard_map/out_y/ppermute | solution.py:279
  6.1 16.0 %collective-permute-start.5 = (bf16[72,1152]{1,0:T(8,128)(2,1)}, bf16[72,1152]{1,0:T(8,128)(2,1)S(1)}, u32[]{:S(2)}, u32[]{:S(2)}) collective-permute-start(bf16[72,1152]{1,0:T(8,128)(2,1)} %bitcast.64), channel_id=1, source_target_pairs={{0,4},{1,5},{2,6},{3,7},{4,8},{5,9},{6,10},{7,11},{8,12},{9,13},{1... | collective-permute-start | bytes 497672 | tf_op jit(solution)/shard_map/out_y/ppermute | solution.py:279
  6.8 15.3 %collective-permute-start.6 = (bf16[72,1152]{1,0:T(8,128)(2,1)}, bf16[72,1152]{1,0:T(8,128)(2,1)S(1)}, u32[]{:S(2)}, u32[]{:S(2)}) collective-permute-start(bf16[72,1152]{1,0:T(8,128)(2,1)} %bitcast.65), channel_id=1, source_target_pairs={{0,12},{1,13},{2,14},{3,15},{4,0},{5,1},{6,2},{7,3},{8,4},{9,5},{1... | collective-permute-start | bytes 497672 | tf_op jit(solution)/shard_map/out_y/ppermute | solution.py:279
  12.2 15.6 %all-to-all-start = ((f32[16,40,128]{2,1,0:T(8,128)}), f32[16,40,128]{2,1,0:T(8,128)S(1)}, u32[]{:S(2)}, u32[]{:S(2)}) async-start(f32[16,40,128]{2,1,0:T(8,128)} %get-tuple-element.14), calls=%async_computation | async-start | bytes 655360 | tf_op jit(solution)/shard_map/all_to_all | solution.py:361
  18.8 26.3 %collective-permute-start.3 = (bf16[5,72,1152]{2,1,0:T(8,128)(2,1)S(1)}, bf16[5,72,1152]{2,1,0:T(8,128)(2,1)}, u32[]{:S(2)}, u32[]{:S(2)}) collective-permute-start(bf16[5,72,1152]{2,1,0:T(8,128)(2,1)S(1)} %pad_maximum_fusion), channel_id=1, source_target_pairs={{0,12},{1,13},{2,14},{3,15},{4,0},{5,1},{6,2},{7,3},{8,4},{9,5},{1... | collective-permute-start | bytes 2488328 | tf_op jit(solution)/shard_map/five_y/ppermute | solution.py:279
  22.0 22.5 %collective-permute-start.2 = (bf16[5,72,1152]{2,1,0:T(8,128)(2,1)S(1)}, bf16[5,72,1152]{2,1,0:T(8,128)(2,1)S(1)}, u32[]{:S(2)}, u32[]{:S(2)}) collective-permute-start(bf16[5,72,1152]{2,1,0:T(8,128)(2,1)S(1)} %pad_maximum_fusion), channel_id=1, source_target_pairs={{0,4},{1,5},{2,6},{3,7},{4,8},{5,9},{6,10},{7,11},{8,12},{9,13},{1... | collective-permute-start | bytes 2488328 | tf_op jit(solution)/shard_map/five_y/ppermute | solution.py:279
  23.8 18.3 %collective-permute-start.8 = (bf16[4,72,1152]{2,1,0:T(8,128)(2,1)S(1)}, bf16[4,72,1152]{2,1,0:T(8,128)(2,1)S(1)}, u32[]{:S(2)}, u32[]{:S(2)}) collective-permute-start(bf16[4,72,1152]{2,1,0:T(8,128)(2,1)S(1)} %pad_maximum_fusion.1), channel_id=1, source_target_pairs={{0,2},{1,3},{2,0},{3,1},{4,6},{5,7},{6,4},{7,5},{8,10},{9,11},{10,... | collective-permute-start | bytes 1990664 | tf_op jit(solution)/shard_map/out_x/ppermute | solution.py:279
  26.8 19.1 %collective-permute-start.7 = (bf16[4,72,1152]{2,1,0:T(8,128)(2,1)S(1)}, bf16[4,72,1152]{2,1,0:T(8,128)(2,1)}, u32[]{:S(2)}, u32[]{:S(2)}) collective-permute-start(bf16[4,72,1152]{2,1,0:T(8,128)(2,1)S(1)} %pad_maximum_fusion.1), channel_id=1, source_target_pairs={{0,1},{1,0},{2,3},{3,2},{4,5},{5,4},{6,7},{7,6},{8,9},{9,8},{10,11... | collective-permute-start | bytes 1990664 | tf_op jit(solution)/shard_map/out_core/ppermute | solution.py:279
  27.8 16.9 %copy-start.5 = (bf16[3,72,1152]{2,1,0:T(8,128)(2,1)S(1)}, bf16[3,72,1152]{2,1,0:T(8,128)(2,1)}, u32[]{:S(2)}) copy-start(bf16[3,72,1152]{2,1,0:T(8,128)(2,1)} %copy-done.4) | copy-start | bytes 1492996
  27.8 16.9 %copy-start.7 = (bf16[1152,72]{0,1:T(8,128)(2,1)S(1)}, bf16[1152,72]{0,1:T(8,128)(2,1)}, u32[]{:S(2)}) copy-start(bf16[1152,72]{0,1:T(8,128)(2,1)} %param.20) | copy-start | bytes 497668
  27.8 16.9 %copy-start.9 = (bf16[72,1152]{1,0:T(8,128)(2,1)S(1)}, bf16[72,1152]{1,0:T(8,128)(2,1)}, u32[]{:S(2)}) copy-start(bf16[72,1152]{1,0:T(8,128)(2,1)} %copy-done.8) | copy-start | bytes 497668
  27.8 18.1 %copy-start.3 = (f32[2,64,16]{1,2,0:T(8,128)S(1)}, f32[2,64,16]{1,2,0:T(8,128)}, u32[]{:S(2)}) copy-start(f32[2,64,16]{1,2,0:T(8,128)} %param.11) | copy-start | bytes 24580
  42.1 3.8 %collective-permute-start.9 = (bf16[2,72,1152]{2,1,0:T(8,128)(2,1)S(1)}, bf16[2,72,1152]{2,1,0:T(8,128)(2,1)S(1)}, u32[]{:S(2)}, u32[]{:S(2)}) collective-permute-start(bf16[2,72,1152]{2,1,0:T(8,128)(2,1)S(1)} %get-tuple-element.25), channel_id=1, source_target_pairs={{0,1},{1,0},{2,3},{3,2},{4,5},{5,4},{6,7},{7,6},{8,9},{9,8},{10,11... | collective-permute-start | bytes 995336 | tf_op jit(solution)/shard_map/out_core/ppermute | solution.py:279
  42.2 3.7 %collective-permute-start.10 = (bf16[2,72,1152]{2,1,0:T(8,128)(2,1)S(1)}, bf16[2,72,1152]{2,1,0:T(8,128)(2,1)S(1)}, u32[]{:S(2)}, u32[]{:S(2)}) collective-permute-start(bf16[2,72,1152]{2,1,0:T(8,128)(2,1)S(1)} %get-tuple-element.24), channel_id=1, source_target_pairs={{0,1},{1,0},{2,3},{3,2},{4,5},{5,4},{6,7},{7,6},{8,9},{9,8},{10,11... | collective-permute-start | bytes 995336 | tf_op jit(solution)/shard_map/out_core/ppermute | solution.py:279
  44.9 27.7 %collective-permute-start.4 = (bf16[5,72,1152]{2,1,0:T(8,128)(2,1)S(1)}, bf16[5,72,1152]{2,1,0:T(8,128)(2,1)S(1)}, u32[]{:S(2)}, u32[]{:S(2)}) collective-permute-start(bf16[5,72,1152]{2,1,0:T(8,128)(2,1)S(1)} %broadcast_select_fusion), channel_id=1, source_target_pairs={{0,8},{1,9},{2,10},{3,11},{4,12},{5,13},{6,14},{7,15},{8,0},{9,1},... | collective-permute-start | bytes 2488328 | tf_op jit(solution)/shard_map/five_far/ppermute | solution.py:279
  48.6 18.1 %collective-permute-start.14 = (bf16[1152,128]{1,0:T(8,128)(2,1)S(1)}, bf16[1152,128]{1,0:T(8,128)(2,1)S(1)}, u32[]{:S(2)}, u32[]{:S(2)}) collective-permute-start(bf16[1152,128]{1,0:T(8,128)(2,1)S(1)} %get-tuple-element.18.refs_6_), channel_id=1, source_target_pairs={{16,2},{17,3},{18,0},{19,1},{20,6},{21,7},{22,4},{23,5},{24,10},{2... | collective-permute-start | bytes 884744 | tf_op jit(solution)/shard_map/inner/ppermute | solution.py:427
  59.3 10.0 %collective-permute-start.16 = (bf16[1152,128]{1,0:T(8,128)(2,1)S(1)}, bf16[1152,128]{1,0:T(8,128)(2,1)S(1)}, u32[]{:S(2)}, u32[]{:S(2)}) collective-permute-start(bf16[1152,128]{1,0:T(8,128)(2,1)S(1)} %get-tuple-element.18.refs_6_), channel_id=1, source_target_pairs={{0,2},{1,3},{2,0},{3,1},{4,6},{5,7},{6,4},{7,5},{8,10},{9,11},{10,... | collective-permute-start | bytes 884744 | tf_op jit(solution)/shard_map/inner/ppermute | solution.py:279
  60.6 11.3 %collective-permute-start.11 = (bf16[1152,128]{1,0:T(8,128)(2,1)S(1)}, bf16[1152,128]{1,0:T(8,128)(2,1)S(1)}, u32[]{:S(2)}, u32[]{:S(2)}) collective-permute-start(bf16[1152,128]{1,0:T(8,128)(2,1)S(1)} %get-tuple-element.18.refs_6_), channel_id=1, source_target_pairs={{16,0},{32,16},{48,32},{64,48},{80,64},{96,80},{112,96},{128,112},... | collective-permute-start | bytes 884744 | tf_op jit(solution)/shard_map/inner/ppermute | solution.py:299
  66.7 5.8 %collective-permute-start.15 = (bf16[1152,128]{1,0:T(8,128)(2,1)S(1)}, bf16[1152,128]{1,0:T(8,128)(2,1)S(1)}, u32[]{:S(2)}, u32[]{:S(2)}) collective-permute-start(bf16[1152,128]{1,0:T(8,128)(2,1)S(1)} %broadcast_select_fusion.2.refs_4_), channel_id=1, source_target_pairs={{0,1},{1,0},{2,3},{3,2},{4,5},{5,4},{6,7},{7,6},{8,9},{9,8},{10,11... | collective-permute-start | bytes 884744 | tf_op jit(solution)/shard_map/inner_core/ppermute | solution.py:279
  69.4 3.1 %collective-permute-start.17 = (bf16[1152,128]{1,0:T(8,128)(2,1)S(1)}, bf16[1152,128]{1,0:T(8,128)(2,1)S(1)}, u32[]{:S(2)}, u32[]{:S(2)}) collective-permute-start(bf16[1152,128]{1,0:T(8,128)(2,1)S(1)} %collective-permute-done.16.refs_6_), channel_id=1, source_target_pairs={{0,1},{1,0},{2,3},{3,2},{4,5},{5,4},{6,7},{7,6},{8,9},{9,8},{10,11... | collective-permute-start | bytes 884744 | tf_op jit(solution)/shard_map/inner_core/ppermute | solution.py:279
  69.4 5.7 %collective-permute-start.13 = (bf16[1152,128]{1,0:T(8,128)(2,1)S(1)}, bf16[1152,128]{1,0:T(8,128)(2,1)S(1)}, u32[]{:S(2)}, u32[]{:S(2)}) collective-permute-start(bf16[1152,128]{1,0:T(8,128)(2,1)S(1)} %get-tuple-element.18.refs_6_), channel_id=1, source_target_pairs={{0,1},{1,0},{2,3},{3,2},{4,5},{5,4},{6,7},{7,6},{8,9},{9,8},{10,11... | collective-permute-start | bytes 884744 | tf_op jit(solution)/shard_map/inner_core/ppermute | solution.py:279
  71.8 3.3 %collective-permute-start.12 = (bf16[1152,128]{1,0:T(8,128)(2,1)S(1)}, bf16[1152,128]{1,0:T(8,128)(2,1)S(1)}, u32[]{:S(2)}, u32[]{:S(2)}) collective-permute-start(bf16[1152,128]{1,0:T(8,128)(2,1)S(1)} %collective-permute-done.11.refs_4_), channel_id=1, source_target_pairs={{0,1},{1,0},{2,3},{3,2},{4,5},{5,4},{6,7},{7,6},{8,9},{9,8},{10,11... | collective-permute-start | bytes 884744 | tf_op jit(solution)/shard_map/inner_core/ppermute | solution.py:279
  73.9 7.9 %collective-permute-start.18 = (bf16[288,256]{1,0:T(8,128)(2,1)S(1)}, bf16[288,256]{1,0:T(8,128)(2,1)S(1)}, u32[]{:S(2)}, u32[]{:S(2)}) collective-permute-start(bf16[288,256]{1,0:T(8,128)(2,1)S(1)} %temporal_across.1), channel_id=1, source_target_pairs={{0,2},{1,3},{2,0},{3,1},{4,6},{5,7},{6,4},{7,5},{8,10},{9,11},{10,... | collective-permute-start | bytes 442376 | tf_op jit(solution)/shard_map/back/ppermute | solution.py:279
  76.4 18.3 %copy-start.13 = (f32[64,16]{0,1:T(8,128)S(1)}, f32[64,16]{0,1:T(8,128)}, u32[]{:S(2)}) copy-start(f32[64,16]{0,1:T(8,128)} %param.14) | copy-start | bytes 12292
  76.4 5.3 %collective-permute-start.19 = (bf16[288,256]{1,0:T(8,128)(2,1)S(1)}, bf16[288,256]{1,0:T(8,128)(2,1)S(1)}, u32[]{:S(2)}, u32[]{:S(2)}) collective-permute-start(bf16[288,256]{1,0:T(8,128)(2,1)S(1)} %temporal_near.1.near_ref), channel_id=1, source_target_pairs={{0,1},{1,0},{2,3},{3,2},{4,5},{5,4},{6,7},{7,6},{8,9},{9,8},{10,11... | collective-permute-start | bytes 442376 | tf_op jit(solution)/shard_map/back/ppermute | solution.py:279
  81.7 1.4 %collective-permute-start.20 = (bf16[288,256]{1,0:T(8,128)(2,1)S(1)}, bf16[288,256]{1,0:T(8,128)(2,1)S(1)}, u32[]{:S(2)}, u32[]{:S(2)}) collective-permute-start(bf16[288,256]{1,0:T(8,128)(2,1)S(1)} %collective-permute-done.18.across_ref), channel_id=1, source_target_pairs={{0,1},{1,0},{2,3},{3,2},{4,5},{5,4},{6,7},{7,6},{8,9},{9,8},{10,11... | collective-permute-start | bytes 442376 | tf_op jit(solution)/shard_map/back/ppermute | solution.py:279
  83.7 1.5 %collective-permute-start.21 = (bf16[576,128]{1,0:T(8,128)(2,1)S(1)}, bf16[576,128]{1,0:T(8,128)(2,1)S(1)}, u32[]{:S(2)}, u32[]{:S(2)}) collective-permute-start(bf16[576,128]{1,0:T(8,128)(2,1)S(1)} %get-tuple-element.20), channel_id=1, source_target_pairs={{0,1},{1,0},{2,3},{3,2},{4,5},{5,4},{6,7},{7,6},{8,9},{9,8},{10,11... | collective-permute-start | bytes 442376 | tf_op jit(solution)/shard_map/update/ppermute | solution.py:279
  86.9 7.8 %collective-permute-start.22 = (f32[16,64]{1,0:T(8,128)S(1)}, f32[16,64]{1,0:T(8,128)S(1)}, u32[]{:S(2)}, u32[]{:S(2)}) collective-permute-start(f32[16,64]{1,0:T(8,128)S(1)} %get-tuple-element.27), channel_id=1, source_target_pairs={{16,0},{32,16},{48,32},{64,48},{80,64},{96,80},{112,96},{128,112},... | collective-permute-start | bytes 12296 | tf_op jit(solution)/shard_map/ppermute | solution.py:299
  (6 other events, 34.9 us)

commit v7 on v6

--- a/solution.py
+++ b/solution.py
@@ -157,14 +157,14 @@
     token_high, token_low = split(jnp.concatenate([tokens_ref[frame], one_row_all], axis=0))
     keys = jnp.concatenate([token_high, token_high, token_low], axis=0)
     values = jnp.concatenate([token_high, token_low[0:16]], axis=0)
-    for chunk in range(4):
-        scores = dot_tn(keys, queries[:, 256 * chunk : 256 * (chunk + 1)])
+    for chunk in range(2):
+        scores = dot_tn(keys, queries[:, 512 * chunk : 512 * (chunk + 1)])
         top = jnp.max(scores, axis=0, keepdims=True)
         weights = jnp.exp2(scores - top).astype(BF)
         summed = dot_nn(values, weights)
         mixed = (summed[0:16] + summed[32:48]) / summed[16:17]
-        for sub in range(4):
-            head = 4 * chunk + sub
+        for sub in range(8):
+            head = 8 * chunk + sub
             part_ref[CP * head : CP * head + 16, :] = mixed[:, 64 * sub : 64 * (sub + 1)]
             part_ref[CP * head + 16 : CP * head + 32, :] = one_row
     value_heads = jnp.where(own_head, jnp.concatenate([coef_ref[frame, 2]] * HEADS, axis=0), 0.0).astype(BF)

time: 96 us -> 96 us (level)
  waiting for transfers between devices: 20.3 us -> 22.6 us
  Pallas kernels: 22 us -> 19.9 us
    ppermute x20, waiting for transfers between devices: 13.8 us -> 16.1 us  [along_seq(): return lax.ppermute(array, 'seq', [(i, to(i)) for i in range(16)])]
    pallas_call x2, Pallas kernels: 8.13 us -> 6.08 us  [attend(): pl.pallas_call(functools.partial(attend_kernel, frame), out_shape=jax.Sha...]
  transfers between devices with their start and end apart: 24 -> 24, of which waited for: 10 -> 10; matrix products, arithmetic and copies ran while one was open for 5% -> 5% of each run, Pallas kernels for 21% -> 18%
where the time goes in v7:
time: 96 us; the launch traced here: 95.3 us
  starting transfers between devices  44.5 us (46%)
  waiting for transfers between devices  22.6 us (24%)
  Pallas kernels  19.9 us (21%)
  other arithmetic  5.28 us (6%)
  between operations  1.66 us (2%)
  local copies, waits for them, and re-layouts  1.4 us (1%)
    ppermute x20, starting transfers between devices, along_seq(): return lax.ppermute(array, 'seq', [(i, to(i)) for i in range(16)])  19.4 us
    ppermute x20, waiting for transfers between devices, along_seq(): return lax.ppermute(array, 'seq', [(i, to(i)) for i in range(16)])  16.1 us
    ppermute x2, starting transfers between devices, from_next(): return lax.ppermute(array, 'queue', [(i, i - 1) for i in range(1, 16)])  10.3 us
    ppermute x1, starting transfers between devices, shards(): following_across = lax.ppermute(inner, ('queue', 'seq'), pairs)  9.53 us
    pallas_call x2, Pallas kernels, attend(): pl.pallas_call(functools.partial(attend_kernel, frame), out_shape=jax.Sha...  6.08 us
    all_to_all x1, starting transfers between devices, shards(): lax.all_to_all(packed, 'seq', split_axis=0, concat_axis=0, tiled=True)  5.27 us
    pallas_call x1, Pallas kernels, shards(): pl.pallas_call(coefficient_kernel, out_shape=(jax.ShapeDtypeStruct((2, 3,...  4.06 us
    ppermute x2, waiting for transfers between devices, from_next(): return lax.ppermute(array, 'queue', [(i, i - 1) for i in range(1, 16)])  3.3 us
  transfers between devices with their start and end apart: 24, of which 10 were waited for; matrix products, arithmetic and copies ran while one was open for 5% of the time, Pallas kernels for 18%

profile of v7, /device:TPU:2, one launch (start us, length us, event | category | flops | bytes accessed | tf_op | source)
XLA Modules:
  0.0 95.3 jit_solution(14566597438036913593)
XLA Ops:
  0.7 2.2 %collective-permute-start.1 = (bf16[72,1152]{1,0:T(8,128)(2,1)}, bf16[72,1152]{1,0:T(8,128)(2,1)S(1)}, u32[]{:S(2)}, u32[]{:S(2)}) collective-permute-start(bf16[72,1152]{1,0:T(8,128)(2,1)} %bitcast.57), channel_id=1, source_target_pairs={{0,2},{1,3},{2,0},{3,1},{4,6},{5,7},{6,4},{7,5},{8,10},{9,11},{10,... | collective-permute-start | bytes 497672 | tf_op jit(solution)/shard_map/last_x/ppermute | solution.py:279
  2.9 3.2 %collective-permute-start = (bf16[72,1152]{1,0:T(8,128)(2,1)}, bf16[72,1152]{1,0:T(8,128)(2,1)S(1)}, u32[]{:S(2)}, u32[]{:S(2)}) collective-permute-start(bf16[72,1152]{1,0:T(8,128)(2,1)} %bitcast.63), channel_id=1, source_target_pairs={{0,8},{1,9},{2,10},{3,11},{4,12},{5,13},{6,14},{7,15},{8,0},{9,1},... | collective-permute-start | bytes 497672 | tf_op jit(solution)/shard_map/out_y/ppermute | solution.py:279
  6.8 2.6 %collective-permute-start.6 = (bf16[72,1152]{1,0:T(8,128)(2,1)}, bf16[72,1152]{1,0:T(8,128)(2,1)S(1)}, u32[]{:S(2)}, u32[]{:S(2)}) collective-permute-start(bf16[72,1152]{1,0:T(8,128)(2,1)} %bitcast.65), channel_id=1, source_target_pairs={{0,12},{1,13},{2,14},{3,15},{4,0},{5,1},{6,2},{7,3},{8,4},{9,5},{1... | collective-permute-start | bytes 497672 | tf_op jit(solution)/shard_map/out_y/ppermute | solution.py:279
  10.0 2.2 %pack.1 = (f32[16,40,128]{2,1,0:T(8,128)}, f32[16,128]{1,0:T(8,128)}) custom-call(s32[2]{0:T(128)} %levels_ref.1, f32[2,16,64]{2,1,0:T(8,128)} %bitcast.54, f32[16,1152]{1,0:T(8,128)} %embed_ref.5, f32[32,8,72]{2,1,0:T(8,128)} %table_ref.1, bf16[72,1152]{1,0:T(8,128)(2,1)} %copy-done.8), custom_call_target="tpu_custom_call" | custom-call | flops 2300000000 | bytes 1000 | tf_op jit(solution)/shard_map/pack/pallas_call | solution.py:350
  12.2 5.3 %all-to-all-start = ((f32[16,40,128]{2,1,0:T(8,128)}), f32[16,40,128]{2,1,0:T(8,128)S(1)}, u32[]{:S(2)}, u32[]{:S(2)}) async-start(f32[16,40,128]{2,1,0:T(8,128)} %get-tuple-element.14), calls=%async_computation | async-start | bytes 655360 | tf_op jit(solution)/shard_map/all_to_all | solution.py:361
  17.6 1.2 %pad_maximum_fusion = bf16[5,72,1152]{2,1,0:T(8,128)(2,1)S(1)} fusion(bf16[1,72,1152]{2,1,0:T(8,128)(2,1)} %bitcast.60, bf16[1,72,1152]{2,1,0:T(8,128)(2,1)S(1)} %bitcast.58, bf16[3,72,1152]{2,1,0:T(8,128)(2,1)S(1)} %select_bitcast_fusion), kind=kLoop, calls=%fused_computation | loop fusion | flops 829440 | bytes 1658880 | tf_op jit(solution)/shard_map/dynamic_update_slice | solution.py:370
  18.8 3.2 %collective-permute-start.3 = (bf16[5,72,1152]{2,1,0:T(8,128)(2,1)S(1)}, bf16[5,72,1152]{2,1,0:T(8,128)(2,1)}, u32[]{:S(2)}, u32[]{:S(2)}) collective-permute-start(bf16[5,72,1152]{2,1,0:T(8,128)(2,1)S(1)} %pad_maximum_fusion), channel_id=1, source_target_pairs={{0,12},{1,13},{2,14},{3,15},{4,0},{5,1},{6,2},{7,3},{8,4},{9,5},{1... | collective-permute-start | bytes 2488328 | tf_op jit(solution)/shard_map/five_y/ppermute | solution.py:279
  22.7 1.0 %pad_maximum_fusion.1 = bf16[4,72,1152]{2,1,0:T(8,128)(2,1)S(1)} fusion(bf16[1,72,1152]{2,1,0:T(8,128)(2,1)S(1)} %bitcast.62, bf16[1,72,1152]{2,1,0:T(8,128)(2,1)} %bitcast.68, bf16[1,72,1152]{2,1,0:T(8,128)(2,1)S(1)} %bitcast.67, bf16[1,72,1152]{2,1,0:T(8,128)(2,1)S(1)} %bitcast.66), kind=kLoop, calls=%fused_computation.3 | loop fusion | flops 995328 | bytes 1327104 | tf_op jit(solution)/shard_map/out_y/stack | solution.py:364
  23.8 3.1 %collective-permute-start.8 = (bf16[4,72,1152]{2,1,0:T(8,128)(2,1)S(1)}, bf16[4,72,1152]{2,1,0:T(8,128)(2,1)S(1)}, u32[]{:S(2)}, u32[]{:S(2)}) collective-permute-start(bf16[4,72,1152]{2,1,0:T(8,128)(2,1)S(1)} %pad_maximum_fusion.1), channel_id=1, source_target_pairs={{0,2},{1,3},{2,0},{3,1},{4,6},{5,7},{6,4},{7,5},{8,10},{9,11},{10,... | collective-permute-start | bytes 1990664 | tf_op jit(solution)/shard_map/out_x/ppermute | solution.py:279
  26.8 0.9 all-to-all-done.all_ref
  27.8 4.1 %coefficients.1 = (f32[2,3,32,1152]{3,2,1,0:T(8,128)S(1)}, f32[16,1152]{1,0:T(8,128)S(1)}, f32[2,16,1024]{2,1,0:T(8,128)S(1)}) custom-call(f32[16,40,128]{2,1,0:T(8,128)S(1)} %all-to-all-done.all_ref, f32[16,1152]{1,0:T(8,128)S(1)} %copy-done.1, bf16[3,1152,1152]{2,1,0:T(8,128)(2,1)} %bitcast.69), custom_call_target="tpu_custom_call" | custom-call | flops 23000000512 | bytes 1000 | tf_op jit(solution)/shard_map/coefficients/pallas_call | solution.py:374
  31.9 3.0 %attend.2.refs_0_ = bf16[64,1152]{1,0:T(8,128)(2,1)S(1)} custom-call(f32[16,128]{1,0:T(8,128)S(1)} %copy-done, f32[2,16,1024]{2,1,0:T(8,128)S(1)} %get-tuple-element.15.tokens_ref, f32[2,3,32,1152]{3,2,1,0:T(8,128)S(1)} %get-tuple-element.16.coef_ref), custom_call_target="tpu_custom_call" | custom-call | flops 115000000 | bytes 1000 | tf_op jit(solution)/shard_map/attend/pallas_call | solution.py:390
  34.9 3.0 %attend.3 = bf16[64,1152]{1,0:T(8,128)(2,1)S(1)} custom-call(f32[16,128]{1,0:T(8,128)S(1)} %copy-done, f32[2,16,1024]{2,1,0:T(8,128)S(1)} %get-tuple-element.15.tokens_ref, f32[2,3,32,1152]{3,2,1,0:T(8,128)S(1)} %get-tuple-element.16.coef_ref, bf16[64,1152]{1,0:T(8,128)(2,1)S(1)} %attend.2.refs_0_), custom_call_target="tpu_custom_call" | custom-call | flops 115000000 | bytes 1000 | tf_op jit(solution)/shard_map/attend/pallas_call | solution.py:390
  38.0 4.0 %collective-permute-done.8 = bf16[4,72,1152]{2,1,0:T(8,128)(2,1)S(1)} collective-permute-done((bf16[4,72,1152]{2,1,0:T(8,128)(2,1)S(1)}, bf16[4,72,1152]{2,1,0:T(8,128)(2,1)S(1)}, u32[]{:S(2)}, u32[]{:S(2)}) %collective-permute-start.8) | collective-permute-done | bytes 663584 | tf_op jit(solution)/shard_map/out_x/ppermute | solution.py:279
  42.7 1.9 %collective-permute-done.2 = bf16[5,72,1152]{2,1,0:T(8,128)(2,1)S(1)} collective-permute-done((bf16[5,72,1152]{2,1,0:T(8,128)(2,1)S(1)}, bf16[5,72,1152]{2,1,0:T(8,128)(2,1)S(1)}, u32[]{:S(2)}, u32[]{:S(2)}) %collective-permute-start.2) | collective-permute-done | bytes 829472 | tf_op jit(solution)/shard_map/five_y/ppermute | solution.py:279
  45.9 2.6 %hidden.1 = (f32[1152,128]{1,0:T(8,128)S(1)}, bf16[1152,128]{1,0:T(8,128)(2,1)S(1)}) custom-call(bf16[64,1152]{1,0:T(8,128)(2,1)S(1)} %broadcast_select_fusion.4.first_ref, bf16[64,1152]{1,0:T(8,128)(2,1)S(1)} %broadcast_select_fusion.3.second_ref, f32[2,16,64]{2,1,0:T(8,128)S(1)} %bitcast.55, f32[16,1152]{1,0:T(8,128)S(1)} %copy-done.1, ...), custom_call_target="tpu_custom_call" | custom-call | flops 2300000000 | bytes 1000 | tf_op jit(solution)/shard_map/hidden/pallas_call | solution.py:412
  48.6 9.5 %collective-permute-start.14 = (bf16[1152,128]{1,0:T(8,128)(2,1)S(1)}, bf16[1152,128]{1,0:T(8,128)(2,1)S(1)}, u32[]{:S(2)}, u32[]{:S(2)}) collective-permute-start(bf16[1152,128]{1,0:T(8,128)(2,1)S(1)} %get-tuple-element.18.refs_6_), channel_id=1, source_target_pairs={{16,2},{17,3},{18,0},{19,1},{20,6},{21,7},{22,4},{23,5},{24,10},{2... | collective-permute-start | bytes 884744 | tf_op jit(solution)/shard_map/inner/ppermute | solution.py:427
  58.1 1.2 %broadcast_select_fusion.1 = bf16[5,72,1152]{2,1,0:T(8,128)(2,1)S(1)} fusion(bf16[5,72,1152]{2,1,0:T(8,128)(2,1)} %collective-permute-done.3, pred[1152]{0:T(1024)(128)(4,1)S(1)} %compare_reduce_fusion.3), kind=kLoop, calls=%fused_computation.2 | loop fusion | flops 414720 | bytes 1660032 | tf_op jit(solution)/shard_map/jit(_where)/select_n | solution.py:325
  59.3 1.3 %collective-permute-start.16 = (bf16[1152,128]{1,0:T(8,128)(2,1)S(1)}, bf16[1152,128]{1,0:T(8,128)(2,1)S(1)}, u32[]{:S(2)}, u32[]{:S(2)}) collective-permute-start(bf16[1152,128]{1,0:T(8,128)(2,1)S(1)} %get-tuple-element.18.refs_6_), channel_id=1, source_target_pairs={{0,2},{1,3},{2,0},{3,1},{4,6},{5,7},{6,4},{7,5},{8,10},{9,11},{10,... | collective-permute-start | bytes 884744 | tf_op jit(solution)/shard_map/inner/ppermute | solution.py:279
  60.6 3.8 %collective-permute-start.11 = (bf16[1152,128]{1,0:T(8,128)(2,1)S(1)}, bf16[1152,128]{1,0:T(8,128)(2,1)S(1)}, u32[]{:S(2)}, u32[]{:S(2)}) collective-permute-start(bf16[1152,128]{1,0:T(8,128)(2,1)S(1)} %get-tuple-element.18.refs_6_), channel_id=1, source_target_pairs={{16,0},{32,16},{48,32},{64,48},{80,64},{96,80},{112,96},{128,112},... | collective-permute-start | bytes 884744 | tf_op jit(solution)/shard_map/inner/ppermute | solution.py:299
  64.4 2.3 %collective-permute-done.14 = bf16[1152,128]{1,0:T(8,128)(2,1)S(1)} collective-permute-done((bf16[1152,128]{1,0:T(8,128)(2,1)S(1)}, bf16[1152,128]{1,0:T(8,128)(2,1)S(1)}, u32[]{:S(2)}, u32[]{:S(2)}) %collective-permute-start.14) | collective-permute-done | bytes 294944 | tf_op jit(solution)/shard_map/inner/ppermute | solution.py:427
  66.8 2.6 %collective-permute-done.16.refs_6_ = bf16[1152,128]{1,0:T(8,128)(2,1)S(1)} collective-permute-done((bf16[1152,128]{1,0:T(8,128)(2,1)S(1)}, bf16[1152,128]{1,0:T(8,128)(2,1)S(1)}, u32[]{:S(2)}, u32[]{:S(2)}) %collective-permute-start.16) | collective-permute-done | bytes 294944 | tf_op jit(solution)/shard_map/inner/ppermute | solution.py:279
  69.9 2.0 %collective-permute-done.11.refs_4_ = bf16[1152,128]{1,0:T(8,128)(2,1)S(1)} collective-permute-done((bf16[1152,128]{1,0:T(8,128)(2,1)S(1)}, bf16[1152,128]{1,0:T(8,128)(2,1)S(1)}, u32[]{:S(2)}, u32[]{:S(2)}) %collective-permute-start.11) | collective-permute-done | bytes 294944 | tf_op jit(solution)/shard_map/inner/ppermute | solution.py:299
  72.5 1.3 %temporal_across.1 = bf16[288,256]{1,0:T(8,128)(2,1)S(1)} custom-call(s32[1]{0:T(128)S(6)} %copy.13.advance_ref, bf16[360,1152]{1,0:T(8,128)(2,1)S(1)} %bitcast.37, bf16[360,1152]{1,0:T(8,128)(2,1)S(1)} %bitcast.45, bf16[360,1152]{1,0:T(8,128)(2,1)S(1)} %bitcast.40, bf16[360,1152]{1,0:T(8,128)(2,1)S(1)} %bitcast.48, ...), custom_call_target="tpu_custom_call" | custom-call | flops 2300000000 | bytes 1000 | tf_op jit(solution)/shard_map/temporal_across/pallas_call | solution.py:438
  73.9 1.2 %collective-permute-start.18 = (bf16[288,256]{1,0:T(8,128)(2,1)S(1)}, bf16[288,256]{1,0:T(8,128)(2,1)S(1)}, u32[]{:S(2)}, u32[]{:S(2)}) collective-permute-start(bf16[288,256]{1,0:T(8,128)(2,1)S(1)} %temporal_across.1), channel_id=1, source_target_pairs={{0,2},{1,3},{2,0},{3,1},{4,6},{5,7},{6,4},{7,5},{8,10},{9,11},{10,... | collective-permute-start | bytes 442376 | tf_op jit(solution)/shard_map/back/ppermute | solution.py:279
  75.1 1.3 %temporal_near.1.near_ref = bf16[288,256]{1,0:T(8,128)(2,1)S(1)} custom-call(s32[1]{0:T(128)S(6)} %copy.13.advance_ref, bf16[360,1152]{1,0:T(8,128)(2,1)S(1)} %bitcast.38, bf16[360,1152]{1,0:T(8,128)(2,1)S(1)} %bitcast.46, bf16[360,1152]{1,0:T(8,128)(2,1)S(1)} %bitcast.41, bf16[360,1152]{1,0:T(8,128)(2,1)S(1)} %bitcast.49, ...), custom_call_target="tpu_custom_call" | custom-call | flops 2300000000 | bytes 1000 | tf_op jit(solution)/shard_map/temporal_near/pallas_call | solution.py:438
  76.8 5.0 %collective-permute-done.18.across_ref = bf16[288,256]{1,0:T(8,128)(2,1)S(1)} collective-permute-done((bf16[288,256]{1,0:T(8,128)(2,1)S(1)}, bf16[288,256]{1,0:T(8,128)(2,1)S(1)}, u32[]{:S(2)}, u32[]{:S(2)}) %collective-permute-start.18) | collective-permute-done | bytes 147488 | tf_op jit(solution)/shard_map/back/ppermute | solution.py:279
  81.7 1.4 %collective-permute-done.20.across_peer_ref = bf16[288,256]{1,0:T(8,128)(2,1)S(1)} collective-permute-done((bf16[288,256]{1,0:T(8,128)(2,1)S(1)}, bf16[288,256]{1,0:T(8,128)(2,1)S(1)}, u32[]{:S(2)}, u32[]{:S(2)}) %collective-permute-start.20) | collective-permute-done | bytes 147488 | tf_op jit(solution)/shard_map/back/ppermute | solution.py:279
  84.0 1.2 %collective-permute-done.21.peer_ref = bf16[576,128]{1,0:T(8,128)(2,1)S(1)} collective-permute-done((bf16[576,128]{1,0:T(8,128)(2,1)S(1)}, bf16[576,128]{1,0:T(8,128)(2,1)S(1)}, u32[]{:S(2)}, u32[]{:S(2)}) %collective-permute-start.21) | collective-permute-done | bytes 147488 | tf_op jit(solution)/shard_map/update/ppermute | solution.py:279
  85.2 1.7 %final.1 = (f32[2,16,64]{2,1,0:T(8,128)}, f32[2,16,64]{2,1,0:T(8,128)S(1)}) custom-call(f32[576,128]{1,0:T(8,128)S(1)} %get-tuple-element.19.own_ref, bf16[576,128]{1,0:T(8,128)(2,1)S(1)} %collective-permute-done.21.peer_ref, f32[1152,128]{1,0:T(8,128)S(1)} %get-tuple-element.21.hidden_ref, f32[2,16,64]{2,1,0:T(8,128)S(1)} %bitcast.56, ...), custom_call_target="tpu_custom_call" | custom-call | flops 2300000000 | bytes 1000 | tf_op jit(solution)/shard_map/final/pallas_call | solution.py:465
  86.9 6.5 %collective-permute-start.22 = (f32[16,64]{1,0:T(8,128)S(1)}, f32[16,64]{1,0:T(8,128)S(1)}, u32[]{:S(2)}, u32[]{:S(2)}) collective-permute-start(f32[16,64]{1,0:T(8,128)S(1)} %get-tuple-element.27), channel_id=1, source_target_pairs={{16,0},{32,16},{48,32},{64,48},{80,64},{96,80},{112,96},{128,112},... | collective-permute-start | bytes 12296 | tf_op jit(solution)/shard_map/ppermute | solution.py:299
  93.4 1.3 %collective-permute-done.22 = f32[16,64]{1,0:T(8,128)S(1)} collective-permute-done((f32[16,64]{1,0:T(8,128)S(1)}, f32[16,64]{1,0:T(8,128)S(1)}, u32[]{:S(2)}, u32[]{:S(2)}) %collective-permute-start.22) | collective-permute-done | bytes 4128 | tf_op jit(solution)/shard_map/ppermute | solution.py:299
  (71 shorter events, 6.6 us)
Async XLA Ops:
  0.6 17.0 %copy-start.6 = (bf16[1152,72]{0,1:T(8,128)(2,1)S(1)}, bf16[1152,72]{0,1:T(8,128)(2,1)}, u32[]{:S(2)}) copy-start(bf16[1152,72]{0,1:T(8,128)(2,1)} %param.20) | copy-start | bytes 497668
  0.6 22.1 %copy-start.11 = (bf16[1152,72]{0,1:T(8,128)(2,1)S(1)}, bf16[1152,72]{0,1:T(8,128)(2,1)}, u32[]{:S(2)}) copy-start(bf16[1152,72]{0,1:T(8,128)(2,1)} %param.18) | copy-start | bytes 497668
  0.7 27.1 %copy-start.1 = (f32[16,1152]{1,0:T(8,128)S(1)}, f32[16,1152]{1,0:T(8,128)}, u32[]{:S(2)}) copy-start(f32[16,1152]{1,0:T(8,128)} %embed_ref.5) | copy-start | bytes 221188
  0.7 8.6 %collective-permute-start.1 = (bf16[72,1152]{1,0:T(8,128)(2,1)}, bf16[72,1152]{1,0:T(8,128)(2,1)S(1)}, u32[]{:S(2)}, u32[]{:S(2)}) collective-permute-start(bf16[72,1152]{1,0:T(8,128)(2,1)} %bitcast.57), channel_id=1, source_target_pairs={{0,2},{1,3},{2,0},{3,1},{4,6},{5,7},{6,4},{7,5},{8,10},{9,11},{10,... | collective-permute-start | bytes 497672 | tf_op jit(solution)/shard_map/last_x/ppermute | solution.py:279
  2.9 14.6 %collective-permute-start = (bf16[72,1152]{1,0:T(8,128)(2,1)}, bf16[72,1152]{1,0:T(8,128)(2,1)S(1)}, u32[]{:S(2)}, u32[]{:S(2)}) collective-permute-start(bf16[72,1152]{1,0:T(8,128)(2,1)} %bitcast.63), channel_id=1, source_target_pairs={{0,8},{1,9},{2,10},{3,11},{4,12},{5,13},{6,14},{7,15},{8,0},{9,1},... | collective-permute-start | bytes 497672 | tf_op jit(solution)/shard_map/out_y/ppermute | solution.py:279
  6.1 16.0 %collective-permute-start.5 = (bf16[72,1152]{1,0:T(8,128)(2,1)}, bf16[72,1152]{1,0:T(8,128)(2,1)S(1)}, u32[]{:S(2)}, u32[]{:S(2)}) collective-permute-start(bf16[72,1152]{1,0:T(8,128)(2,1)} %bitcast.64), channel_id=1, source_target_pairs={{0,4},{1,5},{2,6},{3,7},{4,8},{5,9},{6,10},{7,11},{8,12},{9,13},{1... | collective-permute-start | bytes 497672 | tf_op jit(solution)/shard_map/out_y/ppermute | solution.py:279
  6.8 15.3 %collective-permute-start.6 = (bf16[72,1152]{1,0:T(8,128)(2,1)}, bf16[72,1152]{1,0:T(8,128)(2,1)S(1)}, u32[]{:S(2)}, u32[]{:S(2)}) collective-permute-start(bf16[72,1152]{1,0:T(8,128)(2,1)} %bitcast.65), channel_id=1, source_target_pairs={{0,12},{1,13},{2,14},{3,15},{4,0},{5,1},{6,2},{7,3},{8,4},{9,5},{1... | collective-permute-start | bytes 497672 | tf_op jit(solution)/shard_map/out_y/ppermute | solution.py:279
  12.2 15.6 %all-to-all-start = ((f32[16,40,128]{2,1,0:T(8,128)}), f32[16,40,128]{2,1,0:T(8,128)S(1)}, u32[]{:S(2)}, u32[]{:S(2)}) async-start(f32[16,40,128]{2,1,0:T(8,128)} %get-tuple-element.14), calls=%async_computation | async-start | bytes 655360 | tf_op jit(solution)/shard_map/all_to_all | solution.py:361
  18.8 26.3 %collective-permute-start.3 = (bf16[5,72,1152]{2,1,0:T(8,128)(2,1)S(1)}, bf16[5,72,1152]{2,1,0:T(8,128)(2,1)}, u32[]{:S(2)}, u32[]{:S(2)}) collective-permute-start(bf16[5,72,1152]{2,1,0:T(8,128)(2,1)S(1)} %pad_maximum_fusion), channel_id=1, source_target_pairs={{0,12},{1,13},{2,14},{3,15},{4,0},{5,1},{6,2},{7,3},{8,4},{9,5},{1... | collective-permute-start | bytes 2488328 | tf_op jit(solution)/shard_map/five_y/ppermute | solution.py:279
  22.0 22.5 %collective-permute-start.2 = (bf16[5,72,1152]{2,1,0:T(8,128)(2,1)S(1)}, bf16[5,72,1152]{2,1,0:T(8,128)(2,1)S(1)}, u32[]{:S(2)}, u32[]{:S(2)}) collective-permute-start(bf16[5,72,1152]{2,1,0:T(8,128)(2,1)S(1)} %pad_maximum_fusion), channel_id=1, source_target_pairs={{0,4},{1,5},{2,6},{3,7},{4,8},{5,9},{6,10},{7,11},{8,12},{9,13},{1... | collective-permute-start | bytes 2488328 | tf_op jit(solution)/shard_map/five_y/ppermute | solution.py:279
  23.8 18.3 %collective-permute-start.8 = (bf16[4,72,1152]{2,1,0:T(8,128)(2,1)S(1)}, bf16[4,72,1152]{2,1,0:T(8,128)(2,1)S(1)}, u32[]{:S(2)}, u32[]{:S(2)}) collective-permute-start(bf16[4,72,1152]{2,1,0:T(8,128)(2,1)S(1)} %pad_maximum_fusion.1), channel_id=1, source_target_pairs={{0,2},{1,3},{2,0},{3,1},{4,6},{5,7},{6,4},{7,5},{8,10},{9,11},{10,... | collective-permute-start | bytes 1990664 | tf_op jit(solution)/shard_map/out_x/ppermute | solution.py:279
  26.8 19.1 %collective-permute-start.7 = (bf16[4,72,1152]{2,1,0:T(8,128)(2,1)S(1)}, bf16[4,72,1152]{2,1,0:T(8,128)(2,1)}, u32[]{:S(2)}, u32[]{:S(2)}) collective-permute-start(bf16[4,72,1152]{2,1,0:T(8,128)(2,1)S(1)} %pad_maximum_fusion.1), channel_id=1, source_target_pairs={{0,1},{1,0},{2,3},{3,2},{4,5},{5,4},{6,7},{7,6},{8,9},{9,8},{10,11... | collective-permute-start | bytes 1990664 | tf_op jit(solution)/shard_map/out_core/ppermute | solution.py:279
  27.8 16.9 %copy-start.5 = (bf16[3,72,1152]{2,1,0:T(8,128)(2,1)S(1)}, bf16[3,72,1152]{2,1,0:T(8,128)(2,1)}, u32[]{:S(2)}) copy-start(bf16[3,72,1152]{2,1,0:T(8,128)(2,1)} %copy-done.4) | copy-start | bytes 1492996
  27.8 16.9 %copy-start.7 = (bf16[1152,72]{0,1:T(8,128)(2,1)S(1)}, bf16[1152,72]{0,1:T(8,128)(2,1)}, u32[]{:S(2)}) copy-start(bf16[1152,72]{0,1:T(8,128)(2,1)} %param.20) | copy-start | bytes 497668
  27.8 16.9 %copy-start.9 = (bf16[72,1152]{1,0:T(8,128)(2,1)S(1)}, bf16[72,1152]{1,0:T(8,128)(2,1)}, u32[]{:S(2)}) copy-start(bf16[72,1152]{1,0:T(8,128)(2,1)} %copy-done.8) | copy-start | bytes 497668
  27.8 18.1 %copy-start.3 = (f32[2,64,16]{1,2,0:T(8,128)S(1)}, f32[2,64,16]{1,2,0:T(8,128)}, u32[]{:S(2)}) copy-start(f32[2,64,16]{1,2,0:T(8,128)} %param.11) | copy-start | bytes 24580
  42.1 3.8 %collective-permute-start.9 = (bf16[2,72,1152]{2,1,0:T(8,128)(2,1)S(1)}, bf16[2,72,1152]{2,1,0:T(8,128)(2,1)S(1)}, u32[]{:S(2)}, u32[]{:S(2)}) collective-permute-start(bf16[2,72,1152]{2,1,0:T(8,128)(2,1)S(1)} %get-tuple-element.25), channel_id=1, source_target_pairs={{0,1},{1,0},{2,3},{3,2},{4,5},{5,4},{6,7},{7,6},{8,9},{9,8},{10,11... | collective-permute-start | bytes 995336 | tf_op jit(solution)/shard_map/out_core/ppermute | solution.py:279
  42.2 3.7 %collective-permute-start.10 = (bf16[2,72,1152]{2,1,0:T(8,128)(2,1)S(1)}, bf16[2,72,1152]{2,1,0:T(8,128)(2,1)S(1)}, u32[]{:S(2)}, u32[]{:S(2)}) collective-permute-start(bf16[2,72,1152]{2,1,0:T(8,128)(2,1)S(1)} %get-tuple-element.24), channel_id=1, source_target_pairs={{0,1},{1,0},{2,3},{3,2},{4,5},{5,4},{6,7},{7,6},{8,9},{9,8},{10,11... | collective-permute-start | bytes 995336 | tf_op jit(solution)/shard_map/out_core/ppermute | solution.py:279
  44.9 27.7 %collective-permute-start.4 = (bf16[5,72,1152]{2,1,0:T(8,128)(2,1)S(1)}, bf16[5,72,1152]{2,1,0:T(8,128)(2,1)S(1)}, u32[]{:S(2)}, u32[]{:S(2)}) collective-permute-start(bf16[5,72,1152]{2,1,0:T(8,128)(2,1)S(1)} %broadcast_select_fusion), channel_id=1, source_target_pairs={{0,8},{1,9},{2,10},{3,11},{4,12},{5,13},{6,14},{7,15},{8,0},{9,1},... | collective-permute-start | bytes 2488328 | tf_op jit(solution)/shard_map/five_far/ppermute | solution.py:279
  48.6 18.1 %collective-permute-start.14 = (bf16[1152,128]{1,0:T(8,128)(2,1)S(1)}, bf16[1152,128]{1,0:T(8,128)(2,1)S(1)}, u32[]{:S(2)}, u32[]{:S(2)}) collective-permute-start(bf16[1152,128]{1,0:T(8,128)(2,1)S(1)} %get-tuple-element.18.refs_6_), channel_id=1, source_target_pairs={{16,2},{17,3},{18,0},{19,1},{20,6},{21,7},{22,4},{23,5},{24,10},{2... | collective-permute-start | bytes 884744 | tf_op jit(solution)/shard_map/inner/ppermute | solution.py:427
  59.3 10.0 %collective-permute-start.16 = (bf16[1152,128]{1,0:T(8,128)(2,1)S(1)}, bf16[1152,128]{1,0:T(8,128)(2,1)S(1)}, u32[]{:S(2)}, u32[]{:S(2)}) collective-permute-start(bf16[1152,128]{1,0:T(8,128)(2,1)S(1)} %get-tuple-element.18.refs_6_), channel_id=1, source_target_pairs={{0,2},{1,3},{2,0},{3,1},{4,6},{5,7},{6,4},{7,5},{8,10},{9,11},{10,... | collective-permute-start | bytes 884744 | tf_op jit(solution)/shard_map/inner/ppermute | solution.py:279
  60.6 11.3 %collective-permute-start.11 = (bf16[1152,128]{1,0:T(8,128)(2,1)S(1)}, bf16[1152,128]{1,0:T(8,128)(2,1)S(1)}, u32[]{:S(2)}, u32[]{:S(2)}) collective-permute-start(bf16[1152,128]{1,0:T(8,128)(2,1)S(1)} %get-tuple-element.18.refs_6_), channel_id=1, source_target_pairs={{16,0},{32,16},{48,32},{64,48},{80,64},{96,80},{112,96},{128,112},... | collective-permute-start | bytes 884744 | tf_op jit(solution)/shard_map/inner/ppermute | solution.py:299
  66.7 5.8 %collective-permute-start.15 = (bf16[1152,128]{1,0:T(8,128)(2,1)S(1)}, bf16[1152,128]{1,0:T(8,128)(2,1)S(1)}, u32[]{:S(2)}, u32[]{:S(2)}) collective-permute-start(bf16[1152,128]{1,0:T(8,128)(2,1)S(1)} %broadcast_select_fusion.2.refs_4_), channel_id=1, source_target_pairs={{0,1},{1,0},{2,3},{3,2},{4,5},{5,4},{6,7},{7,6},{8,9},{9,8},{10,11... | collective-permute-start | bytes 884744 | tf_op jit(solution)/shard_map/inner_core/ppermute | solution.py:279
  69.4 3.1 %collective-permute-start.17 = (bf16[1152,128]{1,0:T(8,128)(2,1)S(1)}, bf16[1152,128]{1,0:T(8,128)(2,1)S(1)}, u32[]{:S(2)}, u32[]{:S(2)}) collective-permute-start(bf16[1152,128]{1,0:T(8,128)(2,1)S(1)} %collective-permute-done.16.refs_6_), channel_id=1, source_target_pairs={{0,1},{1,0},{2,3},{3,2},{4,5},{5,4},{6,7},{7,6},{8,9},{9,8},{10,11... | collective-permute-start | bytes 884744 | tf_op jit(solution)/shard_map/inner_core/ppermute | solution.py:279
  69.4 5.7 %collective-permute-start.13 = (bf16[1152,128]{1,0:T(8,128)(2,1)S(1)}, bf16[1152,128]{1,0:T(8,128)(2,1)S(1)}, u32[]{:S(2)}, u32[]{:S(2)}) collective-permute-start(bf16[1152,128]{1,0:T(8,128)(2,1)S(1)} %get-tuple-element.18.refs_6_), channel_id=1, source_target_pairs={{0,1},{1,0},{2,3},{3,2},{4,5},{5,4},{6,7},{7,6},{8,9},{9,8},{10,11... | collective-permute-start | bytes 884744 | tf_op jit(solution)/shard_map/inner_core/ppermute | solution.py:279
  71.8 3.3 %collective-permute-start.12 = (bf16[1152,128]{1,0:T(8,128)(2,1)S(1)}, bf16[1152,128]{1,0:T(8,128)(2,1)S(1)}, u32[]{:S(2)}, u32[]{:S(2)}) collective-permute-start(bf16[1152,128]{1,0:T(8,128)(2,1)S(1)} %collective-permute-done.11.refs_4_), channel_id=1, source_target_pairs={{0,1},{1,0},{2,3},{3,2},{4,5},{5,4},{6,7},{7,6},{8,9},{9,8},{10,11... | collective-permute-start | bytes 884744 | tf_op jit(solution)/shard_map/inner_core/ppermute | solution.py:279
  73.9 7.9 %collective-permute-start.18 = (bf16[288,256]{1,0:T(8,128)(2,1)S(1)}, bf16[288,256]{1,0:T(8,128)(2,1)S(1)}, u32[]{:S(2)}, u32[]{:S(2)}) collective-permute-start(bf16[288,256]{1,0:T(8,128)(2,1)S(1)} %temporal_across.1), channel_id=1, source_target_pairs={{0,2},{1,3},{2,0},{3,1},{4,6},{5,7},{6,4},{7,5},{8,10},{9,11},{10,... | collective-permute-start | bytes 442376 | tf_op jit(solution)/shard_map/back/ppermute | solution.py:279
  76.4 18.3 %copy-start.13 = (f32[64,16]{0,1:T(8,128)S(1)}, f32[64,16]{0,1:T(8,128)}, u32[]{:S(2)}) copy-start(f32[64,16]{0,1:T(8,128)} %param.14) | copy-start | bytes 12292
  76.4 5.3 %collective-permute-start.19 = (bf16[288,256]{1,0:T(8,128)(2,1)S(1)}, bf16[288,256]{1,0:T(8,128)(2,1)S(1)}, u32[]{:S(2)}, u32[]{:S(2)}) collective-permute-start(bf16[288,256]{1,0:T(8,128)(2,1)S(1)} %temporal_near.1.near_ref), channel_id=1, source_target_pairs={{0,1},{1,0},{2,3},{3,2},{4,5},{5,4},{6,7},{7,6},{8,9},{9,8},{10,11... | collective-permute-start | bytes 442376 | tf_op jit(solution)/shard_map/back/ppermute | solution.py:279
  81.7 1.4 %collective-permute-start.20 = (bf16[288,256]{1,0:T(8,128)(2,1)S(1)}, bf16[288,256]{1,0:T(8,128)(2,1)S(1)}, u32[]{:S(2)}, u32[]{:S(2)}) collective-permute-start(bf16[288,256]{1,0:T(8,128)(2,1)S(1)} %collective-permute-done.18.across_ref), channel_id=1, source_target_pairs={{0,1},{1,0},{2,3},{3,2},{4,5},{5,4},{6,7},{7,6},{8,9},{9,8},{10,11... | collective-permute-start | bytes 442376 | tf_op jit(solution)/shard_map/back/ppermute | solution.py:279
  83.7 1.5 %collective-permute-start.21 = (bf16[576,128]{1,0:T(8,128)(2,1)S(1)}, bf16[576,128]{1,0:T(8,128)(2,1)S(1)}, u32[]{:S(2)}, u32[]{:S(2)}) collective-permute-start(bf16[576,128]{1,0:T(8,128)(2,1)S(1)} %get-tuple-element.20), channel_id=1, source_target_pairs={{0,1},{1,0},{2,3},{3,2},{4,5},{5,4},{6,7},{7,6},{8,9},{9,8},{10,11... | collective-permute-start | bytes 442376 | tf_op jit(solution)/shard_map/update/ppermute | solution.py:279
  86.9 7.8 %collective-permute-start.22 = (f32[16,64]{1,0:T(8,128)S(1)}, f32[16,64]{1,0:T(8,128)S(1)}, u32[]{:S(2)}, u32[]{:S(2)}) collective-permute-start(f32[16,64]{1,0:T(8,128)S(1)} %get-tuple-element.27), channel_id=1, source_target_pairs={{16,0},{32,16},{48,32},{64,48},{80,64},{96,80},{112,96},{128,112},... | collective-permute-start | bytes 12296 | tf_op jit(solution)/shard_map/ppermute | solution.py:299
  (6 other events, 34.9 us)
